TPU v7x, 32 devices: a whole 2x2x4 slice. The times are simulated.
32 devices in a mesh: seq: 8 (over z, y), rows: 4 (over x, core).
Axes of the slice: x: 2, y: 2, z: 4, core: 2. Of those that a mesh axis runs over, the one named last changes fastest.
Arguments:
- tokens: bfloat16 [8, 1024, 768], P('rows', 'seq'), may hold values from -6 to 6
- pair_lengths: int32 [8, 16], P('rows'), may hold values from 1 to 512, as said below
- joint_weight: bfloat16 [768, 2304], replicated, may hold values from -0.21875 to 0.21875
- query_bias: float32 [768], replicated, may hold values from -1.2 to 1.2
- value_bias: float32 [768], replicated, may hold values from -0.3 to 0.3
- out_weight: bfloat16 [768, 768], replicated, may hold values from -2 to 2
- out_bias: float32 [768], replicated, may hold values from -3 to 3
- first_gain: float32 [768], replicated, may hold values from 0.25 to 1.75
- first_shift: float32 [768], replicated, may hold values from -3 to 3
- up_weight: bfloat16 [768, 3072], replicated, may hold values from -0.21875 to 0.21875
- up_bias: float32 [3072], replicated, may hold values from -3 to 3
- down_weight: bfloat16 [3072, 768], replicated, may hold values from -0.109375 to 0.109375
- down_bias: float32 [768], replicated, may hold values from -3 to 3
- second_gain: float32 [768], replicated, may hold values from 0.25 to 1.75
- second_shift: float32 [768], replicated, may hold values from -3 to 3
- cotangent: bfloat16 [8, 1024, 768], P('rows', 'seq'), may hold values from -6 to 6
Outputs:
- outputs: bfloat16 [8, 1024, 768], P('rows', 'seq')
- token_gradient: float32 [8, 1024, 768], P('rows', 'seq')
- joint_gradient: float32 [768, 2304], P('seq')
- query_bias_gradient: float32 [768], P('seq')
- value_bias_gradient: float32 [768], P('seq')
- out_gradient: float32 [768, 768], P('seq')
- out_bias_gradient: float32 [768], P('seq')
- first_gain_gradient: float32 [768], P('seq')
- first_shift_gradient: float32 [768], P('seq')
- up_gradient: float32 [768, 3072], P('seq')
- up_bias_gradient: float32 [3072], P('seq')
- down_gradient: float32 [3072, 768], P('seq')
- down_bias_gradient: float32 [768], P('seq')
- second_gain_gradient: float32 [768], P('seq')
- second_shift_gradient: float32 [768], P('seq')
Inputs may be any that keep to these rules, and one draw needn't show every extreme that they name: `pair_lengths`: in every packed row the 16 lengths add up to 1024; no pair is longer than 512 positions (BERT's 512 at most), and in every row one pair has exactly 512.
All inputs are finite; a program needn't handle non-finite values.
Results may differ from a plain program's by a relative error of at most 0.023.
Values may be sent and summed in bfloat16 or wider, within the bound.
No kernel may reach another device: no remote copies, remote signals or barrier semaphores. Data moves between devices by JAX's collectives and lax.ppermute only.
A program may use at most 128 MiB of HBM per device.

v0:
```python
import math

import jax
import jax.numpy as jnp
from jax import lax
from jax.sharding import PartitionSpec as P

HEADS = 12
HEAD_DIM = 64


NEGATIVE = -1e30
EPSILON = 1e-12


def from_behind(value, axis, steps):
    count = lax.axis_size(axis)
    pairs = [(source, (source + steps) % count) for source in range(count)]
    return lax.ppermute(value, axis, pairs)


def layer_norm(value, gain, shift):
    mean = jnp.mean(value, axis=-1, keepdims=True)
    centred = value - mean
    spread = jnp.mean(centred * centred, axis=-1, keepdims=True)
    return centred * lax.rsqrt(spread + EPSILON) * gain + shift


def gelu_exact(value):
    return jax.nn.gelu(value, approximate=False)


def pair_index(positions, ends):
    return jnp.sum((positions[None, :, None] >= ends[:, None, :]).astype(jnp.int32), axis=2)


def split_heads(array):
    return array.reshape(array.shape[0], array.shape[1], HEADS, HEAD_DIM)


def online_block(state, query_heads, query_pairs, key_block, value_block, key_pairs):
    highest, total, summed = state
    scores = jnp.einsum(
        "rqhd,rkhd->rhqk", query_heads, split_heads(key_block), preferred_element_type=jnp.float32
    ) * HEAD_DIM ** (-0.5)
    allowed = query_pairs[:, None, :, None] == key_pairs[:, None, None, :]
    masked = jnp.where(allowed, scores, NEGATIVE)
    new_high = jnp.maximum(highest, jnp.max(masked, axis=3))
    weights = jnp.where(allowed, jnp.exp(masked - new_high[..., None]), 0.0)
    factor = jnp.exp(highest - new_high)
    total = total * factor + jnp.sum(weights, axis=3)
    summed = summed * jnp.swapaxes(factor, 1, 2)[..., None] + jnp.einsum(
        "rhqk,rkhd->rqhd",
        weights.astype(jnp.bfloat16),
        split_heads(value_block),
        preferred_element_type=jnp.float32,
    )
    return (new_high, total, summed)


def tile_terms(queries, out_grad, log_total, delta, query_pairs, keys, values, key_pairs):
    scale = HEAD_DIM ** (-0.5)
    query_heads = split_heads(queries)
    grad_heads = split_heads(out_grad)
    key_heads = split_heads(keys)
    value_heads = split_heads(values)
    scores = (
        jnp.einsum("rqhd,rkhd->rhqk", query_heads, key_heads, preferred_element_type=jnp.float32)
        * scale
    )
    allowed = query_pairs[:, None, :, None] == key_pairs[:, None, None, :]
    weights = jnp.where(
        allowed, jnp.exp(jnp.where(allowed, scores, NEGATIVE) - log_total[..., None]), 0.0
    )
    weight_grad = jnp.einsum(
        "rqhd,rkhd->rhqk", grad_heads, value_heads, preferred_element_type=jnp.float32
    )
    score_grad = (weights * (weight_grad - delta[..., None])).astype(jnp.bfloat16)
    query_term = (
        jnp.einsum("rhqk,rkhd->rqhd", score_grad, key_heads, preferred_element_type=jnp.float32)
        * scale
    )
    key_term = (
        jnp.einsum("rhqk,rqhd->rkhd", score_grad, query_heads, preferred_element_type=jnp.float32)
        * scale
    )
    value_term = jnp.einsum(
        "rhqk,rqhd->rkhd",
        weights.astype(jnp.bfloat16),
        grad_heads,
        preferred_element_type=jnp.float32,
    )
    return (
        query_term.reshape(queries.shape),
        key_term.reshape(keys.shape),
        value_term.reshape(values.shape),
    )


def body(
    tokens,
    pair_lengths,
    joint_weight,
    query_bias,
    value_bias,
    out_weight,
    out_bias,
    first_gain,
    first_shift,
    up_weight,
    up_bias,
    down_weight,
    down_bias,
    second_gain,
    second_shift,
    cotangent,
):
    rows_here, seq_here, width = tokens.shape
    count = lax.axis_size("seq")
    cycle_index = lax.axis_index("seq")
    ends = jnp.cumsum(pair_lengths, axis=1)
    offsets = jnp.arange(seq_here, dtype=jnp.int32)
    own_pairs = pair_index(cycle_index * seq_here + offsets, ends)
    block_shape = (rows_here, seq_here, width)
    flat = tokens.reshape(rows_here * seq_here, width)
    projected = jnp.dot(flat, joint_weight, preferred_element_type=jnp.float32)
    queries = (projected[:, :width] + query_bias).astype(jnp.bfloat16).reshape(block_shape)
    keys = projected[:, width : 2 * width].astype(jnp.bfloat16).reshape(block_shape)
    values = (projected[:, 2 * width :] + value_bias).astype(jnp.bfloat16).reshape(block_shape)
    query_heads = split_heads(queries)
    initial = (
        jnp.full((rows_here, HEADS, seq_here), NEGATIVE, jnp.float32),
        jnp.zeros((rows_here, HEADS, seq_here), jnp.float32),
        jnp.zeros((rows_here, seq_here, HEADS, HEAD_DIM), jnp.float32),
    )
    key_piece = lax.all_gather(keys, "seq", axis=1, tiled=True)
    value_piece = lax.all_gather(values, "seq", axis=1, tiled=True)
    length = key_piece.shape[1]
    block = math.gcd(length, seq_here)

    def one_block(index, inner_state):
        first = index * block
        key_block = lax.dynamic_slice_in_dim(key_piece, first, block, 1)
        value_block = lax.dynamic_slice_in_dim(value_piece, first, block, 1)
        key_pairs = pair_index(first + jnp.arange(block, dtype=jnp.int32), ends)
        return online_block(inner_state, query_heads, own_pairs, key_block, value_block, key_pairs)

    highest, total, summed = lax.fori_loop(0, length // block, one_block, initial)
    log_total = highest + jnp.log(total)
    attended = (
        (summed / jnp.swapaxes(total, 1, 2)[..., None]).astype(jnp.bfloat16).reshape(flat.shape)
    )
    branch = jnp.dot(attended, out_weight, preferred_element_type=jnp.float32) + out_bias
    first_sum = flat.astype(jnp.float32) + branch
    normed, first_back = jax.vjp(layer_norm, first_sum, first_gain, first_shift)
    normed_low = normed.astype(jnp.bfloat16)
    inner = jnp.dot(normed_low, up_weight, preferred_element_type=jnp.float32) + up_bias
    activated_full, gelu_back = jax.vjp(gelu_exact, inner)
    activated = activated_full.astype(jnp.bfloat16)
    feed = jnp.dot(activated, down_weight, preferred_element_type=jnp.float32) + down_bias
    second_sum = normed + feed
    result, second_back = jax.vjp(layer_norm, second_sum, second_gain, second_shift)
    outputs = result.astype(jnp.bfloat16).reshape(tokens.shape)
    second_grad, second_gain_grad, second_shift_grad = second_back(
        cotangent.astype(jnp.float32).reshape(flat.shape)
    )
    feed_grad = second_grad.astype(jnp.bfloat16)
    down_grad = jnp.einsum("ti,tj->ij", activated, feed_grad, preferred_element_type=jnp.float32)
    down_bias_grad = jnp.sum(feed_grad.astype(jnp.float32), axis=0)
    activated_grad = jnp.einsum(
        "tj,ij->ti", feed_grad, down_weight, preferred_element_type=jnp.float32
    )
    inner_grad = gelu_back(activated_grad)[0].astype(jnp.bfloat16)
    up_grad = jnp.einsum("ti,tj->ij", normed_low, inner_grad, preferred_element_type=jnp.float32)
    up_bias_grad = jnp.sum(inner_grad.astype(jnp.float32), axis=0)
    normed_grad = second_grad + jnp.einsum(
        "tj,ij->ti", inner_grad, up_weight, preferred_element_type=jnp.float32
    )
    first_grad, first_gain_grad, first_shift_grad = first_back(normed_grad)
    branch_grad = first_grad.astype(jnp.bfloat16)
    out_grad = jnp.einsum("ti,tj->ij", attended, branch_grad, preferred_element_type=jnp.float32)
    out_bias_grad = jnp.sum(branch_grad.astype(jnp.float32), axis=0)
    attended_grad = jnp.einsum(
        "tj,ij->ti", branch_grad, out_weight, preferred_element_type=jnp.float32
    ).astype(jnp.bfloat16)
    delta = jnp.sum(
        (attended_grad.astype(jnp.float32) * attended.astype(jnp.float32)).reshape(
            rows_here, seq_here, HEADS, HEAD_DIM
        ),
        axis=3,
    )
    delta = jnp.swapaxes(delta, 1, 2)
    attended_grad = attended_grad.reshape(block_shape)
    zeros_block = jnp.zeros(block_shape, jnp.float32)

    def send_key_sums(sums):
        return (
            from_behind(sums[0].astype(jnp.bfloat16), "seq", 1).astype(jnp.float32),
            from_behind(sums[1].astype(jnp.bfloat16), "seq", 1).astype(jnp.float32),
        )

    def key_work(turn, pair_block, sums, query_sum):
        anchor = (cycle_index - turn) % count
        key_pairs = pair_index(anchor * seq_here + offsets, ends)
        query_term, key_term, value_term = tile_terms(
            queries,
            attended_grad,
            log_total,
            delta,
            own_pairs,
            pair_block[0],
            pair_block[1],
            key_pairs,
        )
        return ((sums[0] + key_term, sums[1] + value_term), query_sum + query_term)

    def key_turn(turn, state):
        pair_block, sums, query_sum = state
        sums, query_sum = key_work(turn, pair_block, sums, query_sum)
        sums = send_key_sums(sums)
        pair_block = from_behind((pair_block[0], pair_block[1]), "seq", 1)
        return (pair_block, sums, query_sum)

    pair_block, sums, query_sum = lax.fori_loop(
        0, count - 1, key_turn, ((keys, values), (zeros_block, zeros_block), zeros_block)
    )
    sums, query_sum = key_work(count - 1, pair_block, sums, query_sum)
    key_sum, value_sum = send_key_sums(sums)
    query_low = query_sum.astype(jnp.bfloat16).reshape(flat.shape)
    key_low = key_sum.astype(jnp.bfloat16).reshape(flat.shape)
    value_low = value_sum.astype(jnp.bfloat16).reshape(flat.shape)
    joint_low = jnp.concatenate([query_low, key_low, value_low], axis=1)
    joint_grad = jnp.einsum("ti,tj->ij", flat, joint_low, preferred_element_type=jnp.float32)
    query_bias_grad = jnp.sum(query_low.astype(jnp.float32), axis=0)
    value_bias_grad = jnp.sum(value_low.astype(jnp.float32), axis=0)
    token_grad = first_grad + jnp.einsum(
        "tj,ij->ti", joint_low, joint_weight, preferred_element_type=jnp.float32
    )
    gradients = (
        joint_grad,
        query_bias_grad,
        value_bias_grad,
        out_grad,
        out_bias_grad,
        first_gain_grad,
        first_shift_grad,
        up_grad,
        up_bias_grad,
        down_grad,
        down_bias_grad,
        second_gain_grad,
        second_shift_grad,
    )
    shares = (
        lax.psum_scatter(
            gradients[0].astype(jnp.bfloat16), "seq", scatter_dimension=0, tiled=True
        ).astype(jnp.float32),
        lax.psum_scatter(
            gradients[1].astype(jnp.bfloat16), "seq", scatter_dimension=0, tiled=True
        ).astype(jnp.float32),
        lax.psum_scatter(
            gradients[2].astype(jnp.bfloat16), "seq", scatter_dimension=0, tiled=True
        ).astype(jnp.float32),
        lax.psum_scatter(
            gradients[3].astype(jnp.bfloat16), "seq", scatter_dimension=0, tiled=True
        ).astype(jnp.float32),
        lax.psum_scatter(
            gradients[4].astype(jnp.bfloat16), "seq", scatter_dimension=0, tiled=True
        ).astype(jnp.float32),
        lax.psum_scatter(
            gradients[5].astype(jnp.bfloat16), "seq", scatter_dimension=0, tiled=True
        ).astype(jnp.float32),
        lax.psum_scatter(
            gradients[6].astype(jnp.bfloat16), "seq", scatter_dimension=0, tiled=True
        ).astype(jnp.float32),
        lax.psum_scatter(
            gradients[7].astype(jnp.bfloat16), "seq", scatter_dimension=0, tiled=True
        ).astype(jnp.float32),
        lax.psum_scatter(
            gradients[8].astype(jnp.bfloat16), "seq", scatter_dimension=0, tiled=True
        ).astype(jnp.float32),
        lax.psum_scatter(
            gradients[9].astype(jnp.bfloat16), "seq", scatter_dimension=0, tiled=True
        ).astype(jnp.float32),
        lax.psum_scatter(
            gradients[10].astype(jnp.bfloat16), "seq", scatter_dimension=0, tiled=True
        ).astype(jnp.float32),
        lax.psum_scatter(
            gradients[11].astype(jnp.bfloat16), "seq", scatter_dimension=0, tiled=True
        ).astype(jnp.float32),
        lax.psum_scatter(
            gradients[12].astype(jnp.bfloat16), "seq", scatter_dimension=0, tiled=True
        ).astype(jnp.float32),
    )
    shares = (
        lax.psum(shares[0].astype(jnp.bfloat16), "rows").astype(jnp.float32),
        lax.psum(shares[1].astype(jnp.bfloat16), "rows").astype(jnp.float32),
        lax.psum(shares[2].astype(jnp.bfloat16), "rows").astype(jnp.float32),
        lax.psum(shares[3].astype(jnp.bfloat16), "rows").astype(jnp.float32),
        lax.psum(shares[4].astype(jnp.bfloat16), "rows").astype(jnp.float32),
        lax.psum(shares[5].astype(jnp.bfloat16), "rows").astype(jnp.float32),
        lax.psum(shares[6].astype(jnp.bfloat16), "rows").astype(jnp.float32),
        lax.psum(shares[7].astype(jnp.bfloat16), "rows").astype(jnp.float32),
        lax.psum(shares[8].astype(jnp.bfloat16), "rows").astype(jnp.float32),
        lax.psum(shares[9].astype(jnp.bfloat16), "rows").astype(jnp.float32),
        lax.psum(shares[10].astype(jnp.bfloat16), "rows").astype(jnp.float32),
        lax.psum(shares[11].astype(jnp.bfloat16), "rows").astype(jnp.float32),
        lax.psum(shares[12].astype(jnp.bfloat16), "rows").astype(jnp.float32),
    )
    return (outputs, token_grad.reshape(tokens.shape)) + tuple(shares)


def solution(mesh):
    placed = (
        P("rows", "seq", None),
        P("rows", None),
        P(),
        P(),
        P(),
        P(),
        P(),
        P(),
        P(),
        P(),
        P(),
        P(),
        P(),
        P(),
        P(),
        P("rows", "seq", None),
    )
    return jax.shard_map(
        body,
        mesh=mesh,
        in_specs=placed,
        out_specs=(
            P("rows", "seq", None),
            P("rows", "seq", None),
            P("seq", None),
            P("seq"),
            P("seq"),
            P("seq", None),
            P("seq"),
            P("seq"),
            P("seq"),
            P("seq", None),
            P("seq"),
            P("seq", None),
            P("seq"),
            P("seq"),
            P("seq"),
        ),
        check_vma=False,
    )
```

profile of v0, /device:TPU:0, one launch (start us, length us, event | category | flops | bytes accessed | tf_op | source)
XLA Modules:
  0.0 1035.3 jit_solution(10708824437440467329)
XLA Ops:
  30.6 51.1 %all-gather.5.cloned.1.call-done = bf16[2,1024,768]{1,2,0:T(8,128)(2,1)} async-done(((bf16[2,128,768]{1,2,0:T(8,128)(2,1)}), bf16[2,1024,768]{1,2,0:T(8,128)(2,1)}) %all-gather.5.cloned.1.call-update) | async-done | bytes 3145744 | tf_op jit(solution)/shard_map/all_gather | solution.py:137
  81.6 63.3 %all-gather.3.cloned.1.call-done = bf16[2,1024,768]{1,2,0:T(8,128)(2,1)} async-done(((bf16[2,128,768]{1,2,0:T(8,128)(2,1)}), bf16[2,1024,768]{1,2,0:T(8,128)(2,1)}) %all-gather.3.cloned.1.call-update) | async-done | bytes 3145744 | tf_op jit(solution)/shard_map/all_gather | solution.py:136
  144.9 90.8 %while.43 = (s32[]{:T(128)}, f32[2,12,128]{2,1,0:T(8,128)S(1)}, f32[2,12,128]{2,1,0:T(8,128)}, f32[2,128,12,64]{1,3,2,0:T(8,128)}, s32[2,128]{1,0:T(2,128)}, /*i...) while((s32[]{:T(128)}, f32[2,12,128]{2,1,0:T(8,128)S(1)}, ...), condition=%wide.region_6.7_spmd.clone, body=%wide.region_2.6_spmd.clone.sunk | while | flops 104855432 | bytes 16028107 | solution.py:148
  148.3 3.2 fusion.129
  152.4 2.7 fusion.133
  159.4 3.2 fusion.129
  163.5 3.0 fusion.133
  170.8 3.2 fusion.129
  174.9 3.0 fusion.133
  182.2 3.2 fusion.129
  186.2 3.0 fusion.133
  193.6 3.2 fusion.129
  197.6 3.0 fusion.133
  204.9 3.2 fusion.129
  209.0 3.0 fusion.133
  216.3 3.2 fusion.129
  220.3 3.0 fusion.133
  227.7 3.2 fusion.129
  231.7 3.0 fusion.133
  241.0 8.1 multiply_convert_fusion.1
  253.8 3.0 fusion.49
  265.5 2.9 convert_multiply_fusion.2
  283.2 277.9 %while.44 = (s32[]{:T(128)}, bf16[2,128,768]{1,2,0:T(8,128)(2,1)}, bf16[2,128,768]{1,2,0:T(8,128)(2,1)}, f32[2,128,768]{1,2,0:T(8,128)}, f32[2,128,768]{1,2,0:T(...) while((s32[]{:T(128)}, bf16[2,128,768]{1,2,0:T(8,128)(2,1)}, ...), condition=%wide.wide.region_18.19_spmd.clone, body=%wide.wide.region_16.18_spmd.clone.sunk | while | flops 257208208 | bytes 38286064 | solution.py:224
  296.0 3.5 collective-permute-start.3
  304.1 12.8 %collective-permute-done.2 = bf16[2,128,768]{1,2,0:T(8,128)(2,1)} collective-permute-done((bf16[2,128,768]{1,2,0:T(8,128)(2,1)}, bf16[2,128,768]{1,2,0:T(8,128)(2,1)}, u32[]{:S(2)}, u32[]{:S(2)}) %collective-permute-start.2) | collective-permute-done | bytes 393248 | tf_op jit(solution)/shard_map/while/body/eval_jaxpr/ppermute | solution.py:19
  318.9 4.9 collective-permute-done.3
  337.5 2.6 collective-permute-start.3
  345.0 14.4 %collective-permute-done.2 = bf16[2,128,768]{1,2,0:T(8,128)(2,1)} collective-permute-done((bf16[2,128,768]{1,2,0:T(8,128)(2,1)}, bf16[2,128,768]{1,2,0:T(8,128)(2,1)}, u32[]{:S(2)}, u32[]{:S(2)}) %collective-permute-start.2) | collective-permute-done | bytes 393248 | tf_op jit(solution)/shard_map/while/body/eval_jaxpr/ppermute | solution.py:19
  361.3 4.0 collective-permute-done.3
  384.7 16.2 %collective-permute-done.2 = bf16[2,128,768]{1,2,0:T(8,128)(2,1)} collective-permute-done((bf16[2,128,768]{1,2,0:T(8,128)(2,1)}, bf16[2,128,768]{1,2,0:T(8,128)(2,1)}, u32[]{:S(2)}, u32[]{:S(2)}) %collective-permute-start.2) | collective-permute-done | bytes 393248 | tf_op jit(solution)/shard_map/while/body/eval_jaxpr/ppermute | solution.py:19
  402.9 3.0 collective-permute-done.3
  424.0 17.4 %collective-permute-done.2 = bf16[2,128,768]{1,2,0:T(8,128)(2,1)} collective-permute-done((bf16[2,128,768]{1,2,0:T(8,128)(2,1)}, bf16[2,128,768]{1,2,0:T(8,128)(2,1)}, u32[]{:S(2)}, u32[]{:S(2)}) %collective-permute-start.2) | collective-permute-done | bytes 393248 | tf_op jit(solution)/shard_map/while/body/eval_jaxpr/ppermute | solution.py:19
  463.7 16.5 %collective-permute-done.2 = bf16[2,128,768]{1,2,0:T(8,128)(2,1)} collective-permute-done((bf16[2,128,768]{1,2,0:T(8,128)(2,1)}, bf16[2,128,768]{1,2,0:T(8,128)(2,1)}, u32[]{:S(2)}, u32[]{:S(2)}) %collective-permute-start.2) | collective-permute-done | bytes 393248 | tf_op jit(solution)/shard_map/while/body/eval_jaxpr/ppermute | solution.py:19
  502.4 15.6 %collective-permute-done.2 = bf16[2,128,768]{1,2,0:T(8,128)(2,1)} collective-permute-done((bf16[2,128,768]{1,2,0:T(8,128)(2,1)}, bf16[2,128,768]{1,2,0:T(8,128)(2,1)}, u32[]{:S(2)}, u32[]{:S(2)}) %collective-permute-start.2) | collective-permute-done | bytes 393248 | tf_op jit(solution)/shard_map/while/body/eval_jaxpr/ppermute | solution.py:19
  540.3 14.7 %collective-permute-done.2 = bf16[2,128,768]{1,2,0:T(8,128)(2,1)} collective-permute-done((bf16[2,128,768]{1,2,0:T(8,128)(2,1)}, bf16[2,128,768]{1,2,0:T(8,128)(2,1)}, u32[]{:S(2)}, u32[]{:S(2)}) %collective-permute-start.2) | collective-permute-done | bytes 393248 | tf_op jit(solution)/shard_map/while/body/eval_jaxpr/ppermute | solution.py:19
  582.0 2.8 convolution_multiply_fusion.3
  593.2 4.1 fusion.20
  597.3 5.8 copy.136
  603.2 2.6 convolution_convert_fusion.3
  605.9 5.4 convolution_convert_fusion.1
  611.4 5.1 convolution_convert_fusion
  616.6 66.8 %reduce-scatter.13.cloned.1.call-done = bf16[96,2304]{1,0:T(8,128)(2,1)} async-done(((bf16[768,2304]{1,0:T(8,128)(2,1)}), bf16[96,2304]{1,0:T(8,128)(2,1)}) %reduce-scatter.13.cloned.1.call-update) | async-done | bytes 442384
  685.5 65.4 %reduce-scatter.7.cloned.1.call-done = bf16[96,768]{1,0:T(8,128)(2,1)} async-done(((bf16[768,768]{1,0:T(8,128)(2,1)}), bf16[96,768]{1,0:T(8,128)(2,1)}) %reduce-scatter.7.cloned.1.call-update) | async-done | bytes 147472 | tf_op jit(solution)/shard_map/reduce_scatter | solution.py:264
  750.8 97.8 %reduce-scatter.9.cloned.1.call-done = bf16[96,3072]{1,0:T(8,128)(2,1)} async-done(((bf16[768,3072]{1,0:T(8,128)(2,1)}), bf16[96,3072]{1,0:T(8,128)(2,1)}) %reduce-scatter.9.cloned.1.call-update) | async-done | bytes 589840 | tf_op jit(solution)/shard_map/reduce_scatter | solution.py:276
  848.6 98.6 %reduce-scatter.11.cloned.1.call-done = bf16[384,768]{1,0:T(8,128)(2,1)} async-done(((bf16[3072,768]{1,0:T(8,128)(2,1)}), bf16[384,768]{1,0:T(8,128)(2,1)}) %reduce-scatter.11.cloned.1.call-update) | async-done | bytes 589840 | tf_op jit(solution)/shard_map/reduce_scatter | solution.py:282
  953.0 37.2 %all-reduce.9 = (bf16[768]{0:T(1024)(128)(2,1)}, bf16[768]{0:T(1024)(128)(2,1)}, bf16[768]{0:T(1024)(128)(2,1)}, bf16[768]{0:T(1024)(128)(2,1)}, bf16[768]{0:T(1...) all-reduce(bf16[768]{0:T(1024)(128)(2,1)S(1)} %copy-done.37, ...), channel_id=3, replica_groups=mesh['seq'=8,'rows'=4] {'seq'}, use_global_device_ids=true, to_apply=%region_23.24.clone | all-reduce | flops 9216 | bytes 36864
  1000.0 6.5 all-reduce.10
  1016.4 3.5 convolution_add_fusion.2
  (543 shorter events, 313.1 us)
Async XLA Ops:
  7.2 74.4 %all-gather.5.cloned.1.call-start = ((), (), s32[]{:S(2)}) async-start(), calls=%async_computation.5 | async-start | bytes 3538944 | tf_op jit(solution)/shard_map/all_gather | solution.py:137
  15.7 129.2 %all-gather.3.cloned.1.call-start = ((), (), s32[]{:S(2)}) async-start(), calls=%async_computation.4 | async-start | bytes 3538944 | tf_op jit(solution)/shard_map/all_gather | solution.py:136
  19.7 663.7 %reduce-scatter.13.cloned.1.call-start = ((), (), s32[]{:S(2)}) async-start(), calls=%async_computation.9 | async-start | bytes 3981312
  238.5 10.6 %slice-start = ((s8[4718592]{0:T(1024)(128)(4,1)}), s8[4194304]{0:T(1024)(128)(4,1)S(1)}, s32[]{:S(2)}) async-start(s8[4718592]{0:T(1024)(128)(4,1)} %bitcast.174), calls=%async_computation.11 | async-start | bytes 8388608
  240.7 18.5 %copy-start.8 = (f32[256,768]{1,0:T(8,128)}, f32[256,768]{1,0:T(8,128)S(1)}, u32[]{:S(2)}) copy-start(f32[256,768]{1,0:T(8,128)S(1)} %get-tuple-element.833) | copy-start | bytes 2359300
  240.7 18.5 %copy-start.29 = (f32[256]{0:T(256)}, f32[256]{0:T(256)S(1)}, u32[]{:S(2)}) copy-start(f32[256]{0:T(256)S(1)} %broadcast_multiply_fusion.1) | copy-start | bytes 3076
  241.0 18.2 %copy-start.32 = (f32[256]{0:T(256)}, f32[256]{0:T(256)S(1)}, u32[]{:S(2)}) copy-start(f32[256]{0:T(256)S(1)} %fusion.40) | copy-start | bytes 3076
  241.0 8.2 slice-start.1
  241.0 8.2 copy-start.43
  283.2 8.4 copy-start.19
  285.0 40.7 %collective-permute-start = (bf16[2,128,768]{1,2,0:T(8,128)(2,1)}, bf16[2,128,768]{1,2,0:T(8,128)(2,1)}, u32[]{:S(2)}, u32[]{:S(2)}) collective-permute-start(bf16[2,128,768]{1,2,0:T(8,128)(2,1)} %copy.192), channel_id=1, source_target_pairs={{0,4},{4,8},{8,12},{12,16},{16,20},{20,24},{24,28},{28,0},{1,5},{5... | collective-permute-start | bytes 1179656 | tf_op jit(solution)/shard_map/while/body/eval_jaxpr/ppermute | solution.py:19
  288.2 37.4 %collective-permute-start.1 = (bf16[2,128,768]{1,2,0:T(8,128)(2,1)}, bf16[2,128,768]{1,2,0:T(8,128)(2,1)}, u32[]{:S(2)}, u32[]{:S(2)}) collective-permute-start(bf16[2,128,768]{1,2,0:T(8,128)(2,1)} %copy.193), channel_id=1, source_target_pairs={{0,4},{4,8},{8,12},{12,16},{16,20},{20,24},{24,28},{28,0},{1,5},{5... | collective-permute-start | bytes 1179656 | tf_op jit(solution)/shard_map/while/body/eval_jaxpr/ppermute | solution.py:19
  294.8 22.2 %collective-permute-start.2 = (bf16[2,128,768]{1,2,0:T(8,128)(2,1)}, bf16[2,128,768]{1,2,0:T(8,128)(2,1)}, u32[]{:S(2)}, u32[]{:S(2)}) collective-permute-start(bf16[2,128,768]{1,2,0:T(8,128)(2,1)} %fusion.144), channel_id=1, source_target_pairs={{0,4},{4,8},{8,12},{12,16},{16,20},{20,24},{24,28},{28,0},{1,5},{5... | collective-permute-start | bytes 1179656 | tf_op jit(solution)/shard_map/while/body/eval_jaxpr/ppermute | solution.py:19
  296.0 27.7 %collective-permute-start.3 = (bf16[2,128,768]{1,2,0:T(8,128)(2,1)}, bf16[2,128,768]{1,2,0:T(8,128)(2,1)}, u32[]{:S(2)}, u32[]{:S(2)}) collective-permute-start(bf16[2,128,768]{1,2,0:T(8,128)(2,1)} %fusion.146), channel_id=1, source_target_pairs={{0,4},{4,8},{8,12},{12,16},{16,20},{20,24},{24,28},{28,0},{1,5},{5... | collective-permute-start | bytes 1179656 | tf_op jit(solution)/shard_map/while/body/eval_jaxpr/ppermute | solution.py:19
  327.5 39.7 %collective-permute-start = (bf16[2,128,768]{1,2,0:T(8,128)(2,1)}, bf16[2,128,768]{1,2,0:T(8,128)(2,1)}, u32[]{:S(2)}, u32[]{:S(2)}) collective-permute-start(bf16[2,128,768]{1,2,0:T(8,128)(2,1)} %copy.192), channel_id=1, source_target_pairs={{0,4},{4,8},{8,12},{12,16},{16,20},{20,24},{24,28},{28,0},{1,5},{5... | collective-permute-start | bytes 1179656 | tf_op jit(solution)/shard_map/while/body/eval_jaxpr/ppermute | solution.py:19
  329.2 38.0 %collective-permute-start.1 = (bf16[2,128,768]{1,2,0:T(8,128)(2,1)}, bf16[2,128,768]{1,2,0:T(8,128)(2,1)}, u32[]{:S(2)}, u32[]{:S(2)}) collective-permute-start(bf16[2,128,768]{1,2,0:T(8,128)(2,1)} %copy.193), channel_id=1, source_target_pairs={{0,4},{4,8},{8,12},{12,16},{16,20},{20,24},{24,28},{28,0},{1,5},{5... | collective-permute-start | bytes 1179656 | tf_op jit(solution)/shard_map/while/body/eval_jaxpr/ppermute | solution.py:19
  336.3 23.1 %collective-permute-start.2 = (bf16[2,128,768]{1,2,0:T(8,128)(2,1)}, bf16[2,128,768]{1,2,0:T(8,128)(2,1)}, u32[]{:S(2)}, u32[]{:S(2)}) collective-permute-start(bf16[2,128,768]{1,2,0:T(8,128)(2,1)} %fusion.144), channel_id=1, source_target_pairs={{0,4},{4,8},{8,12},{12,16},{16,20},{20,24},{24,28},{28,0},{1,5},{5... | collective-permute-start | bytes 1179656 | tf_op jit(solution)/shard_map/while/body/eval_jaxpr/ppermute | solution.py:19
  337.5 27.8 %collective-permute-start.3 = (bf16[2,128,768]{1,2,0:T(8,128)(2,1)}, bf16[2,128,768]{1,2,0:T(8,128)(2,1)}, u32[]{:S(2)}, u32[]{:S(2)}) collective-permute-start(bf16[2,128,768]{1,2,0:T(8,128)(2,1)} %fusion.146), channel_id=1, source_target_pairs={{0,4},{4,8},{8,12},{12,16},{16,20},{20,24},{24,28},{28,0},{1,5},{5... | collective-permute-start | bytes 1179656 | tf_op jit(solution)/shard_map/while/body/eval_jaxpr/ppermute | solution.py:19
  369.0 38.8 %collective-permute-start = (bf16[2,128,768]{1,2,0:T(8,128)(2,1)}, bf16[2,128,768]{1,2,0:T(8,128)(2,1)}, u32[]{:S(2)}, u32[]{:S(2)}) collective-permute-start(bf16[2,128,768]{1,2,0:T(8,128)(2,1)} %copy.192), channel_id=1, source_target_pairs={{0,4},{4,8},{8,12},{12,16},{16,20},{20,24},{24,28},{28,0},{1,5},{5... | collective-permute-start | bytes 1179656 | tf_op jit(solution)/shard_map/while/body/eval_jaxpr/ppermute | solution.py:19
  370.8 37.1 %collective-permute-start.1 = (bf16[2,128,768]{1,2,0:T(8,128)(2,1)}, bf16[2,128,768]{1,2,0:T(8,128)(2,1)}, u32[]{:S(2)}, u32[]{:S(2)}) collective-permute-start(bf16[2,128,768]{1,2,0:T(8,128)(2,1)} %copy.193), channel_id=1, source_target_pairs={{0,4},{4,8},{8,12},{12,16},{16,20},{20,24},{24,28},{28,0},{1,5},{5... | collective-permute-start | bytes 1179656 | tf_op jit(solution)/shard_map/while/body/eval_jaxpr/ppermute | solution.py:19
  377.3 23.6 %collective-permute-start.2 = (bf16[2,128,768]{1,2,0:T(8,128)(2,1)}, bf16[2,128,768]{1,2,0:T(8,128)(2,1)}, u32[]{:S(2)}, u32[]{:S(2)}) collective-permute-start(bf16[2,128,768]{1,2,0:T(8,128)(2,1)} %fusion.144), channel_id=1, source_target_pairs={{0,4},{4,8},{8,12},{12,16},{16,20},{20,24},{24,28},{28,0},{1,5},{5... | collective-permute-start | bytes 1179656 | tf_op jit(solution)/shard_map/while/body/eval_jaxpr/ppermute | solution.py:19
  378.5 27.4 %collective-permute-start.3 = (bf16[2,128,768]{1,2,0:T(8,128)(2,1)}, bf16[2,128,768]{1,2,0:T(8,128)(2,1)}, u32[]{:S(2)}, u32[]{:S(2)}) collective-permute-start(bf16[2,128,768]{1,2,0:T(8,128)(2,1)} %fusion.146), channel_id=1, source_target_pairs={{0,4},{4,8},{8,12},{12,16},{16,20},{20,24},{24,28},{28,0},{1,5},{5... | collective-permute-start | bytes 1179656 | tf_op jit(solution)/shard_map/while/body/eval_jaxpr/ppermute | solution.py:19
  409.6 37.9 %collective-permute-start = (bf16[2,128,768]{1,2,0:T(8,128)(2,1)}, bf16[2,128,768]{1,2,0:T(8,128)(2,1)}, u32[]{:S(2)}, u32[]{:S(2)}) collective-permute-start(bf16[2,128,768]{1,2,0:T(8,128)(2,1)} %copy.192), channel_id=1, source_target_pairs={{0,4},{4,8},{8,12},{12,16},{16,20},{20,24},{24,28},{28,0},{1,5},{5... | collective-permute-start | bytes 1179656 | tf_op jit(solution)/shard_map/while/body/eval_jaxpr/ppermute | solution.py:19
  411.4 36.1 %collective-permute-start.1 = (bf16[2,128,768]{1,2,0:T(8,128)(2,1)}, bf16[2,128,768]{1,2,0:T(8,128)(2,1)}, u32[]{:S(2)}, u32[]{:S(2)}) collective-permute-start(bf16[2,128,768]{1,2,0:T(8,128)(2,1)} %copy.193), channel_id=1, source_target_pairs={{0,4},{4,8},{8,12},{12,16},{16,20},{20,24},{24,28},{28,0},{1,5},{5... | collective-permute-start | bytes 1179656 | tf_op jit(solution)/shard_map/while/body/eval_jaxpr/ppermute | solution.py:19
  417.9 23.5 %collective-permute-start.2 = (bf16[2,128,768]{1,2,0:T(8,128)(2,1)}, bf16[2,128,768]{1,2,0:T(8,128)(2,1)}, u32[]{:S(2)}, u32[]{:S(2)}) collective-permute-start(bf16[2,128,768]{1,2,0:T(8,128)(2,1)} %fusion.144), channel_id=1, source_target_pairs={{0,4},{4,8},{8,12},{12,16},{16,20},{20,24},{24,28},{28,0},{1,5},{5... | collective-permute-start | bytes 1179656 | tf_op jit(solution)/shard_map/while/body/eval_jaxpr/ppermute | solution.py:19
  419.1 26.5 %collective-permute-start.3 = (bf16[2,128,768]{1,2,0:T(8,128)(2,1)}, bf16[2,128,768]{1,2,0:T(8,128)(2,1)}, u32[]{:S(2)}, u32[]{:S(2)}) collective-permute-start(bf16[2,128,768]{1,2,0:T(8,128)(2,1)} %fusion.146), channel_id=1, source_target_pairs={{0,4},{4,8},{8,12},{12,16},{16,20},{20,24},{24,28},{28,0},{1,5},{5... | collective-permute-start | bytes 1179656 | tf_op jit(solution)/shard_map/while/body/eval_jaxpr/ppermute | solution.py:19
  449.3 37.0 %collective-permute-start = (bf16[2,128,768]{1,2,0:T(8,128)(2,1)}, bf16[2,128,768]{1,2,0:T(8,128)(2,1)}, u32[]{:S(2)}, u32[]{:S(2)}) collective-permute-start(bf16[2,128,768]{1,2,0:T(8,128)(2,1)} %copy.192), channel_id=1, source_target_pairs={{0,4},{4,8},{8,12},{12,16},{16,20},{20,24},{24,28},{28,0},{1,5},{5... | collective-permute-start | bytes 1179656 | tf_op jit(solution)/shard_map/while/body/eval_jaxpr/ppermute | solution.py:19
  451.1 35.2 %collective-permute-start.1 = (bf16[2,128,768]{1,2,0:T(8,128)(2,1)}, bf16[2,128,768]{1,2,0:T(8,128)(2,1)}, u32[]{:S(2)}, u32[]{:S(2)}) collective-permute-start(bf16[2,128,768]{1,2,0:T(8,128)(2,1)} %copy.193), channel_id=1, source_target_pairs={{0,4},{4,8},{8,12},{12,16},{16,20},{20,24},{24,28},{28,0},{1,5},{5... | collective-permute-start | bytes 1179656 | tf_op jit(solution)/shard_map/while/body/eval_jaxpr/ppermute | solution.py:19
  457.6 22.5 %collective-permute-start.2 = (bf16[2,128,768]{1,2,0:T(8,128)(2,1)}, bf16[2,128,768]{1,2,0:T(8,128)(2,1)}, u32[]{:S(2)}, u32[]{:S(2)}) collective-permute-start(bf16[2,128,768]{1,2,0:T(8,128)(2,1)} %fusion.144), channel_id=1, source_target_pairs={{0,4},{4,8},{8,12},{12,16},{16,20},{20,24},{24,28},{28,0},{1,5},{5... | collective-permute-start | bytes 1179656 | tf_op jit(solution)/shard_map/while/body/eval_jaxpr/ppermute | solution.py:19
  458.8 25.6 %collective-permute-start.3 = (bf16[2,128,768]{1,2,0:T(8,128)(2,1)}, bf16[2,128,768]{1,2,0:T(8,128)(2,1)}, u32[]{:S(2)}, u32[]{:S(2)}) collective-permute-start(bf16[2,128,768]{1,2,0:T(8,128)(2,1)} %fusion.146), channel_id=1, source_target_pairs={{0,4},{4,8},{8,12},{12,16},{16,20},{20,24},{24,28},{28,0},{1,5},{5... | collective-permute-start | bytes 1179656 | tf_op jit(solution)/shard_map/while/body/eval_jaxpr/ppermute | solution.py:19
  488.1 36.1 %collective-permute-start = (bf16[2,128,768]{1,2,0:T(8,128)(2,1)}, bf16[2,128,768]{1,2,0:T(8,128)(2,1)}, u32[]{:S(2)}, u32[]{:S(2)}) collective-permute-start(bf16[2,128,768]{1,2,0:T(8,128)(2,1)} %copy.192), channel_id=1, source_target_pairs={{0,4},{4,8},{8,12},{12,16},{16,20},{20,24},{24,28},{28,0},{1,5},{5... | collective-permute-start | bytes 1179656 | tf_op jit(solution)/shard_map/while/body/eval_jaxpr/ppermute | solution.py:19
  489.9 34.3 %collective-permute-start.1 = (bf16[2,128,768]{1,2,0:T(8,128)(2,1)}, bf16[2,128,768]{1,2,0:T(8,128)(2,1)}, u32[]{:S(2)}, u32[]{:S(2)}) collective-permute-start(bf16[2,128,768]{1,2,0:T(8,128)(2,1)} %copy.193), channel_id=1, source_target_pairs={{0,4},{4,8},{8,12},{12,16},{16,20},{20,24},{24,28},{28,0},{1,5},{5... | collective-permute-start | bytes 1179656 | tf_op jit(solution)/shard_map/while/body/eval_jaxpr/ppermute | solution.py:19
  496.4 21.6 %collective-permute-start.2 = (bf16[2,128,768]{1,2,0:T(8,128)(2,1)}, bf16[2,128,768]{1,2,0:T(8,128)(2,1)}, u32[]{:S(2)}, u32[]{:S(2)}) collective-permute-start(bf16[2,128,768]{1,2,0:T(8,128)(2,1)} %fusion.144), channel_id=1, source_target_pairs={{0,4},{4,8},{8,12},{12,16},{16,20},{20,24},{24,28},{28,0},{1,5},{5... | collective-permute-start | bytes 1179656 | tf_op jit(solution)/shard_map/while/body/eval_jaxpr/ppermute | solution.py:19
  497.6 24.7 %collective-permute-start.3 = (bf16[2,128,768]{1,2,0:T(8,128)(2,1)}, bf16[2,128,768]{1,2,0:T(8,128)(2,1)}, u32[]{:S(2)}, u32[]{:S(2)}) collective-permute-start(bf16[2,128,768]{1,2,0:T(8,128)(2,1)} %fusion.146), channel_id=1, source_target_pairs={{0,4},{4,8},{8,12},{12,16},{16,20},{20,24},{24,28},{28,0},{1,5},{5... | collective-permute-start | bytes 1179656 | tf_op jit(solution)/shard_map/while/body/eval_jaxpr/ppermute | solution.py:19
  526.0 35.1 %collective-permute-start = (bf16[2,128,768]{1,2,0:T(8,128)(2,1)}, bf16[2,128,768]{1,2,0:T(8,128)(2,1)}, u32[]{:S(2)}, u32[]{:S(2)}) collective-permute-start(bf16[2,128,768]{1,2,0:T(8,128)(2,1)} %copy.192), channel_id=1, source_target_pairs={{0,4},{4,8},{8,12},{12,16},{16,20},{20,24},{24,28},{28,0},{1,5},{5... | collective-permute-start | bytes 1179656 | tf_op jit(solution)/shard_map/while/body/eval_jaxpr/ppermute | solution.py:19
  527.7 33.4 %collective-permute-start.1 = (bf16[2,128,768]{1,2,0:T(8,128)(2,1)}, bf16[2,128,768]{1,2,0:T(8,128)(2,1)}, u32[]{:S(2)}, u32[]{:S(2)}) collective-permute-start(bf16[2,128,768]{1,2,0:T(8,128)(2,1)} %copy.193), channel_id=1, source_target_pairs={{0,4},{4,8},{8,12},{12,16},{16,20},{20,24},{24,28},{28,0},{1,5},{5... | collective-permute-start | bytes 1179656 | tf_op jit(solution)/shard_map/while/body/eval_jaxpr/ppermute | solution.py:19
  534.2 20.7 %collective-permute-start.2 = (bf16[2,128,768]{1,2,0:T(8,128)(2,1)}, bf16[2,128,768]{1,2,0:T(8,128)(2,1)}, u32[]{:S(2)}, u32[]{:S(2)}) collective-permute-start(bf16[2,128,768]{1,2,0:T(8,128)(2,1)} %fusion.144), channel_id=1, source_target_pairs={{0,4},{4,8},{8,12},{12,16},{16,20},{20,24},{24,28},{28,0},{1,5},{5... | collective-permute-start | bytes 1179656 | tf_op jit(solution)/shard_map/while/body/eval_jaxpr/ppermute | solution.py:19
  535.4 23.7 %collective-permute-start.3 = (bf16[2,128,768]{1,2,0:T(8,128)(2,1)}, bf16[2,128,768]{1,2,0:T(8,128)(2,1)}, u32[]{:S(2)}, u32[]{:S(2)}) collective-permute-start(bf16[2,128,768]{1,2,0:T(8,128)(2,1)} %fusion.146), channel_id=1, source_target_pairs={{0,4},{4,8},{8,12},{12,16},{16,20},{20,24},{24,28},{28,0},{1,5},{5... | collective-permute-start | bytes 1179656 | tf_op jit(solution)/shard_map/while/body/eval_jaxpr/ppermute | solution.py:19
  574.9 16.5 %collective-permute-start.4 = (bf16[2,128,768]{2,1,0:T(8,128)(2,1)}, bf16[2,128,768]{2,1,0:T(8,128)(2,1)}, u32[]{:S(2)}, u32[]{:S(2)}) collective-permute-start(bf16[2,128,768]{2,1,0:T(8,128)(2,1)} %add_convert_fusion.2), channel_id=1, source_target_pairs={{0,4},{4,8},{8,12},{12,16},{16,20},{20,24},{24,28},{28,0},{1,5},{5... | collective-permute-start | bytes 1179656 | tf_op jit(solution)/shard_map/ppermute | solution.py:19
  581.7 11.5 %collective-permute-start.5 = (bf16[2,128,768]{2,1,0:T(8,128)(2,1)}, bf16[2,128,768]{2,1,0:T(8,128)(2,1)}, u32[]{:S(2)}, u32[]{:S(2)}) collective-permute-start(bf16[2,128,768]{2,1,0:T(8,128)(2,1)} %add_convert_fusion.1), channel_id=1, source_target_pairs={{0,4},{4,8},{8,12},{12,16},{16,20},{20,24},{24,28},{28,0},{1,5},{5... | collective-permute-start | bytes 1179656 | tf_op jit(solution)/shard_map/ppermute | solution.py:19
  603.2 147.7 %reduce-scatter.7.cloned.1.call-start = ((), (), s32[]{:S(2)}) async-start(), calls=%async_computation.6 | async-start | bytes 1327104 | tf_op jit(solution)/shard_map/reduce_scatter | solution.py:264
  605.8 242.8 %reduce-scatter.9.cloned.1.call-start = ((), (), s32[]{:S(2)}) async-start(), calls=%async_computation.7 | async-start | bytes 5308416 | tf_op jit(solution)/shard_map/reduce_scatter | solution.py:276
  611.3 335.8 %reduce-scatter.11.cloned.1.call-start = ((), (), s32[]{:S(2)}) async-start(), calls=%async_computation.8 | async-start | bytes 5308416 | tf_op jit(solution)/shard_map/reduce_scatter | solution.py:282
  616.5 336.6 %copy-start.34 = (bf16[768]{0:T(1024)(128)(2,1)S(1)}, bf16[768]{0:T(1024)(128)(2,1)}, u32[]{:S(2)}) copy-start(bf16[768]{0:T(1024)(128)(2,1)} %get-tuple-element.738) | copy-start | bytes 4612
  616.5 336.6 %copy-start.35 = (bf16[768]{0:T(1024)(128)(2,1)S(1)}, bf16[768]{0:T(1024)(128)(2,1)}, u32[]{:S(2)}) copy-start(bf16[768]{0:T(1024)(128)(2,1)} %get-tuple-element.811) | copy-start | bytes 4612
  616.5 336.6 %copy-start.36 = (bf16[768]{0:T(1024)(128)(2,1)S(1)}, bf16[768]{0:T(1024)(128)(2,1)}, u32[]{:S(2)}) copy-start(bf16[768]{0:T(1024)(128)(2,1)} %get-tuple-element.815) | copy-start | bytes 4612
  616.5 336.6 %copy-start.37 = (bf16[768]{0:T(1024)(128)(2,1)S(1)}, bf16[768]{0:T(1024)(128)(2,1)}, u32[]{:S(2)}) copy-start(bf16[768]{0:T(1024)(128)(2,1)} %get-tuple-element.817) | copy-start | bytes 4612
  616.5 403.3 %all-reduce.14.cloned.1.call-start = ((), (), s32[]{:S(2)}) async-start(), calls=%async_computation.10 | async-start | bytes 3833856 | tf_op jit(solution)/shard_map/psum | solution.py:296
  (100 other events, 313.6 us)
Sparse Core Ops, SparseCore 0:
  15.8 65.7 all-gather.4
  83.7 61.2 all-gather.2
  603.3 80.0 reduce-scatter.12
  687.2 63.5 reduce-scatter.6
  754.3 94.2 reduce-scatter.8
  852.1 95.0 reduce-scatter.10
  950.3 48.9 all-reduce.13
where the time goes:
time: 1040 us
  waiting for transfers between devices  573 us (55%)
  matrix products  149 us (14%)
  other arithmetic  127 us (12%)
  local copies, waits for them, and re-layouts  114 us (11%)
  blocking collectives  43.7 us (4%)
  between operations  16.4 us (2%)
    ppermute x30, waiting for transfers between devices, from_behind(): return lax.ppermute(value, axis, pairs)  131 us
    reduce_scatter x1, waiting for transfers between devices, body(): lax.psum_scatter(gradients[9].astype(jnp.bfloat16), 'seq', scatter_dimens...  98.6 us
    reduce_scatter x1, waiting for transfers between devices, body(): lax.psum_scatter(gradients[7].astype(jnp.bfloat16), 'seq', scatter_dimens...  97.8 us
    unnamed x8, waiting for transfers between devices  66.9 us
    reduce_scatter x1, waiting for transfers between devices, body(): lax.psum_scatter(gradients[3].astype(jnp.bfloat16), 'seq', scatter_dimens...  65.4 us
    all_gather x1, waiting for transfers between devices, body(): key_piece = lax.all_gather(keys, 'seq', axis=1, tiled=True)  63.3 us
    all_gather x1, waiting for transfers between devices, body(): value_piece = lax.all_gather(values, 'seq', axis=1, tiled=True)  51.1 us
    unnamed x1, blocking collectives  37.2 us
  transfers between devices with their start and end apart: 37, of which 21 were waited for; matrix products, arithmetic and copies ran while one was open for 19% of the time, Pallas kernels for 0%

commit v1 on v0

--- a/solution.py
+++ b/solution.py
@@ -1,8 +1,11 @@
+import functools
 import math
 
 import jax
 import jax.numpy as jnp
 from jax import lax
+from jax.experimental import pallas as pl
+from jax.experimental.pallas import tpu as pltpu
 from jax.sharding import PartitionSpec as P
 
 HEADS = 12
@@ -97,7 +100,7 @@
     )
 
 
-def body(
+def general_body(
     tokens,
     pair_lengths,
     joint_weight,
@@ -310,6 +313,963 @@
     return (outputs, token_grad.reshape(tokens.shape)) + tuple(shares)
 
 
+WIDTH = HEADS * HEAD_DIM
+HALF = WIDTH // 2
+FF = 4 * WIDTH
+BLOCK = 128
+OWN = 2 * BLOCK
+LANES = 128
+PAIRS_OF_HEADS = HALF // LANES
+JOINT_ROWS = 160
+UP_ROWS = 128
+DOWN_ROWS = 96
+FLOAT = jnp.float32
+LOW = jnp.bfloat16
+AXES = ("seq", "rows")
+
+
+def kernel_params(megabytes):
+    return pltpu.CompilerParams(vmem_limit_bytes=megabytes << 20)
+
+
+def shaped(shape, kind):
+    return jax.ShapeDtypeStruct(shape, kind)
+
+
+def whole(shape):
+    return pl.BlockSpec(shape, lambda *_: (0,) * len(shape))
+
+
+def cost(flops, moved, exps=0):
+    return pl.CostEstimate(flops=int(flops), bytes_accessed=int(moved), transcendentals=int(exps))
+
+
+def dot(left, right):
+    return lax.dot_general(left, right, (((1,), (0,)), ((), ())), preferred_element_type=FLOAT)
+
+
+def dot_nt(left, right):
+    return lax.dot_general(left, right, (((1,), (1,)), ((), ())), preferred_element_type=FLOAT)
+
+
+def device_at(z, y, x, c):
+    return ((z * 2 + y) * 2 + x) * 2 + c
+
+
+def permute(value, target):
+    pairs = []
+    for z in range(4):
+        for y in range(2):
+            for x in range(2):
+                for c in range(2):
+                    pairs.append((device_at(z, y, x, c), device_at(*target(z, y, x, c))))
+    return lax.ppermute(value, AXES, pairs)
+
+
+def core_swap(value):
+    return permute(value, lambda z, y, x, c: (z, y, x, 1 - c))
+
+
+def x_swap(value):
+    return permute(value, lambda z, y, x, c: (z, y, 1 - x, c))
+
+
+def y_swap(value):
+    return permute(value, lambda z, y, x, c: (z, 1 - y, x, c))
+
+
+def z_swap(value, bits):
+    return permute(value, lambda z, y, x, c: (z ^ bits, y, x, c))
+
+
+def row_swap(value, second):
+    return permute(value, lambda z, y, x, c: (2 * c + (z % 2 ^ second), y, x, z // 2))
+
+
+def first_positions(place):
+    z, y, c = place[0], place[1], place[3]
+    bases = []
+    for core, line in ((c, y), (1 - c, y), (c, 1 - y), (1 - c, 1 - y)):
+        for second in (0, 1):
+            parity = z % 2
+            parity = 1 - parity if second else parity
+            bases.append((2 * (2 * core + parity) + line) * BLOCK)
+    return bases
+
+
+def pair_ends(place, own_lengths, peer_lengths):
+    z, c = place[0], place[3]
+    here = (z // 2) == c
+    line = z % 2
+    ends, end = [], 0
+    for pair in range(own_lengths.shape[1]):
+        end = end + jnp.where(here, own_lengths[line, pair], peer_lengths[line, pair])
+        ends.append(end)
+    return ends
+
+
+def pairs_along(base, ends, axis):
+    shape = (8, BLOCK) if axis == 1 else (BLOCK, LANES)
+    position = base + lax.broadcasted_iota(jnp.int32, shape, axis)
+    ids = jnp.zeros(shape, jnp.int32)
+    for end in ends:
+        ids = ids + (position >= end).astype(jnp.int32)
+    return ids
+
+
+def head_mask(rows):
+    return lax.broadcasted_iota(jnp.int32, (rows, LANES), 1) < HEAD_DIM
+
+
+def attention_kernel(
+    place, own_lengths, peer_lengths, *refs
+):
+    blocks = refs[:8]
+    wq, wk, wv, qb, vb = refs[8:13]
+    own_out, send_out, q_out, k_out, v_out, log_out = refs[13:19]
+    bias, log_columns = refs[19:]
+    bases = first_positions(place)
+    ends = pair_ends(place, own_lengths, peer_lengths)
+    here = jnp.concatenate([block[...] for block in blocks[:4]], axis=0)
+    there = jnp.concatenate([block[...] for block in blocks[4:]], axis=0)
+    queries = dot(here, wq[...]) + qb[...]
+    q_out[...] = (queries.astype(LOW).astype(FLOAT) * HEAD_DIM**-0.5).astype(LOW)
+    for index, tokens in enumerate((here, there)):
+        rows = pl.ds(index * 512, 512)
+        k_out[rows, :] = dot(tokens, wk[...]).astype(LOW)
+        v_out[rows, :] = (dot(tokens, wv[...]) + vb[...]).astype(LOW)
+    key_ids = [pairs_along(base, ends, 1)[0:1] for base in bases]
+    for i in range(4):
+        query_ids = pairs_along(bases[i], ends, 0)
+        for j in range(8):
+            bias[pl.ds(i * BLOCK, BLOCK), pl.ds(j * BLOCK, BLOCK)] = jnp.where(
+                query_ids == key_ids[j], 0.0, NEGATIVE
+            )
+    log_columns[...] = jnp.zeros_like(log_columns)
+    for pair in range(PAIRS_OF_HEADS):
+        lanes = pl.ds(pair * LANES, LANES)
+        keys = k_out[:, lanes]
+        values = v_out[:, lanes]
+        ones = jnp.ones_like(values)
+        left_keys = head_mask(1024)
+        values_of = (jnp.where(left_keys, values, ones), jnp.where(left_keys, ones, values))
+        left = head_mask(OWN)
+        for part in range(2):
+            rows = pl.ds(part * OWN, OWN)
+            queries = q_out[rows, lanes]
+            zeros = jnp.zeros_like(queries)
+            summed = []
+            for half in range(2):
+                chosen = jnp.where(left, queries, zeros) if half == 0 else jnp.where(left, zeros, queries)
+                scores = dot_nt(chosen, keys) + bias[rows, :]
+                highest = jnp.max(scores, axis=1, keepdims=True)
+                weights = jnp.exp(scores - highest).astype(LOW)
+                total = dot(weights, values_of[half])
+                turned = pltpu.roll(total, HEAD_DIM, 1)
+                summed.append(total / turned)
+                sums = total if half == 1 else turned
+                log_total = highest + jnp.log(sums)
+                column = lax.broadcasted_iota(jnp.int32, (OWN, LANES), 1) == pair * 2 + half
+                at = log_total if pair * 2 + half < HEAD_DIM else None
+                log_columns[rows, :] = jnp.where(column, at, log_columns[rows, :])
+            attended = jnp.where(left, summed[0], summed[1]).astype(LOW)
+            target = own_out if part == 0 else send_out
+            target[:, lanes] = attended
+    log_out[...] = jnp.transpose(log_columns[...])[0:8, :]
+
+
+def attention(place, own_lengths, peer_lengths, blocks, joint_weight, query_bias, value_bias):
+    def columns(kind):
+        return pl.BlockSpec((WIDTH, HALF), lambda i, place, *_: (0, 2 * kind + place[3]))
+
+    half_row = pl.BlockSpec((1, HALF), lambda i, place, *_: (0, place[3]))
+    return pl.pallas_call(
+        attention_kernel,
+        grid_spec=pltpu.PrefetchScalarGridSpec(
+            num_scalar_prefetch=3,
+            grid=(1,),
+            in_specs=[whole((BLOCK, WIDTH))] * 8
+            + [columns(0), columns(1), columns(2), half_row, half_row],
+            out_specs=[
+                whole((OWN, HALF)),
+                whole((OWN, HALF)),
+                whole((512, HALF)),
+                whole((1024, HALF)),
+                whole((1024, HALF)),
+                whole((8, 512)),
+            ],
+            scratch_shapes=[pltpu.VMEM((512, 1024), FLOAT), pltpu.VMEM((512, LANES), FLOAT)],
+        ),
+        out_shape=[
+            shaped((OWN, HALF), LOW),
+            shaped((OWN, HALF), LOW),
+            shaped((512, HALF), LOW),
+            shaped((1024, HALF), LOW),
+            shaped((1024, HALF), LOW),
+            shaped((8, 512), FLOAT),
+        ],
+        compiler_params=kernel_params(40),
+        cost_estimate=cost(4e9, 8e6, 3e6),
+        name="attention",
+    )(
+        place, own_lengths, peer_lengths, *blocks, joint_weight, joint_weight, joint_weight,
+        query_bias.reshape(1, WIDTH), value_bias.reshape(1, WIDTH),
+    )
+
+
+def centred_norm(value):
+    mean = jnp.mean(value, axis=-1, keepdims=True)
+    centred = value - mean
+    spread = jnp.mean(centred * centred, axis=-1, keepdims=True)
+    inverse = lax.rsqrt(spread + EPSILON)
+    return centred * inverse, inverse
+
+
+def norm_back(grad, unit, inverse):
+    mean = jnp.mean(grad, axis=-1, keepdims=True)
+    along = jnp.mean(grad * unit, axis=-1, keepdims=True)
+    return (grad - mean - unit * along) * inverse
+
+
+def column_sum(value):
+    return jnp.sum(value, axis=0, keepdims=True)
+
+
+def forward_kernel(
+    place, att_own, att_other, wo_own, wo_other, out_bias, x0, x1, gain1, shift1, up, up_bias, down,
+    down_bias, gain2, shift2, cot0, cot1,
+    out0, out1, feed_grad, second_grad, act_t, slope, unit1, inverse1, normed_t, att_t, sums,
+    normed, normed_low, feed,
+):
+    step = pl.program_id(0)
+
+    @pl.when(step == 0)
+    def _():
+        tokens = jnp.concatenate([x0[...], x1[...]], axis=0).astype(FLOAT)
+        branch = dot(att_own[...], wo_own[...]) + dot(att_other[...], wo_other[...]) + out_bias[...]
+        unit, inverse = centred_norm(tokens + branch)
+        unit1[...] = unit
+        inverse1[...] = jnp.broadcast_to(inverse, (OWN, LANES))
+        value = unit * gain1[...] + shift1[...]
+        normed[...] = value
+        normed_low[...] = value.astype(LOW)
+        normed_t[...] = jnp.transpose(value).astype(LOW)
+        c = place[3]
+        att_t[pl.ds(pl.multiple_of(c * HALF, HALF), HALF), :] = jnp.transpose(
+            att_own[...].astype(FLOAT)
+        ).astype(LOW)
+        att_t[pl.ds(pl.multiple_of((1 - c) * HALF, HALF), HALF), :] = jnp.transpose(
+            att_other[...].astype(FLOAT)
+        ).astype(LOW)
+        feed[...] = jnp.zeros_like(feed)
+
+    inner = dot(normed_low[...], up[...]) + up_bias[...]
+    below = 0.5 + 0.5 * lax.erf(inner * math.sqrt(0.5))
+    density = jnp.exp(inner * inner * -0.5) * (1.0 / math.sqrt(2.0 * math.pi))
+    activated = inner * below
+    slope[...] = (below + inner * density).astype(LOW)
+    low = activated.astype(LOW)
+    act_t[...] = jnp.transpose(activated).astype(LOW)
+    feed[...] += dot(low, down[...])
+
+    @pl.when(step == pl.num_programs(0) - 1)
+    def _():
+        unit, inverse = centred_norm(normed[...] + feed[...] + down_bias[...])
+        result = (unit * gain2[...] + shift2[...]).astype(LOW)
+        out0[...] = result[0:BLOCK]
+        out1[...] = result[BLOCK:OWN]
+        cotangent = jnp.concatenate([cot0[...], cot1[...]], axis=0).astype(FLOAT)
+        grad = norm_back(cotangent * gain2[...], unit, inverse)
+        second_grad[...] = grad
+        low_grad = grad.astype(LOW)
+        feed_grad[...] = low_grad
+        sums[...] = jnp.concatenate(
+            [
+                column_sum(cotangent * unit),
+                column_sum(cotangent),
+                column_sum(low_grad.astype(FLOAT)),
+                jnp.zeros((5, WIDTH), FLOAT),
+            ],
+            axis=0,
+        )
+
+
+def row_of(vector):
+    return vector.reshape(1, vector.shape[0])
+
+
+def forward(place, att_own, att_other, tokens, cotangents, weights):
+    chunk = WIDTH
+    steps = FF // chunk
+    row = whole((1, WIDTH))
+    block = whole((BLOCK, WIDTH))
+    return pl.pallas_call(
+        forward_kernel,
+        grid_spec=pltpu.PrefetchScalarGridSpec(
+            num_scalar_prefetch=1,
+            grid=(steps,),
+            in_specs=[
+                whole((OWN, HALF)),
+                whole((OWN, HALF)),
+                pl.BlockSpec((HALF, WIDTH), lambda i, place: (place[3], 0)),
+                pl.BlockSpec((HALF, WIDTH), lambda i, place: (1 - place[3], 0)),
+                row, block, block, row, row,
+                pl.BlockSpec((WIDTH, chunk), lambda i, place: (0, i)),
+                pl.BlockSpec((1, chunk), lambda i, place: (0, i)),
+                pl.BlockSpec((chunk, WIDTH), lambda i, place: (i, 0)),
+                row, row, row, block, block,
+            ],
+            out_specs=[
+                block, block, whole((OWN, WIDTH)), whole((OWN, WIDTH)),
+                pl.BlockSpec((chunk, OWN), lambda i, place: (i, 0)),
+                pl.BlockSpec((OWN, chunk), lambda i, place: (0, i)),
+                whole((OWN, WIDTH)), whole((OWN, LANES)), whole((WIDTH, OWN)), whole((WIDTH, OWN)),
+                whole((8, WIDTH)),
+            ],
+            scratch_shapes=[
+                pltpu.VMEM((OWN, WIDTH), FLOAT),
+                pltpu.VMEM((OWN, WIDTH), LOW),
+                pltpu.VMEM((OWN, WIDTH), FLOAT),
+            ],
+        ),
+        out_shape=[
+            shaped((BLOCK, WIDTH), LOW),
+            shaped((BLOCK, WIDTH), LOW),
+            shaped((OWN, WIDTH), LOW),
+            shaped((OWN, WIDTH), FLOAT),
+            shaped((FF, OWN), LOW),
+            shaped((OWN, FF), LOW),
+            shaped((OWN, WIDTH), FLOAT),
+            shaped((OWN, LANES), FLOAT),
+            shaped((WIDTH, OWN), LOW),
+            shaped((WIDTH, OWN), LOW),
+            shaped((8, WIDTH), FLOAT),
+        ],
+        compiler_params=kernel_params(40),
+        cost_estimate=cost(2.7e9, 20e6, 2e6),
+        name="forward",
+    )(
+        place, att_own, att_other, weights["out"], weights["out"], row_of(weights["out_bias"]), *tokens,
+        row_of(weights["gain1"]), row_of(weights["shift1"]), weights["up"], row_of(weights["up_bias"]),
+        weights["down"], row_of(weights["down_bias"]), row_of(weights["gain2"]),
+        row_of(weights["shift2"]), *cotangents,
+    )
+
+
+def down_kernel(place, act_t, feed_grad, out):
+    for x in range(2):
+        out[x] = dot(act_t[0, x, 0], feed_grad[...]).astype(LOW)
+
+
+def down_units(place, act_t, feed_grad, kept):
+    return pl.pallas_call(
+        down_kernel,
+        grid_spec=pltpu.PrefetchScalarGridSpec(
+            num_scalar_prefetch=1,
+            grid=(8,),
+            in_specs=[
+                pl.BlockSpec(
+                    (1, 2, 1, DOWN_ROWS, OWN),
+                    lambda i, place: (i, 0, place[3] if kept else 1 - place[3], 0, 0),
+                ),
+                whole((OWN, WIDTH)),
+            ],
+            out_specs=pl.BlockSpec((2, DOWN_ROWS, WIDTH), lambda i, place: (i, 0, 0)),
+        ),
+        out_shape=shaped((16, DOWN_ROWS, WIDTH), LOW),
+        compiler_params=kernel_params(16),
+        cost_estimate=cost(0.6e9, 3.5e6),
+        name="down_units",
+    )(place, act_t.reshape(8, 2, 2, DOWN_ROWS, OWN), feed_grad)
+
+
+def backward_kernel(
+    place, feed_grad, slope, up, down, second_grad, unit1, inverse1, gain1, wo_own, wo_other,
+    inner_grad, first_grad, branch_grad, back_own, back_send, sums,
+    normed_grad,
+):
+    step = pl.program_id(0)
+
+    @pl.when(step == 0)
+    def _():
+        normed_grad[...] = second_grad[...]
+        sums[...] = jnp.zeros_like(sums)
+
+    grad = (dot_nt(feed_grad[...], down[...]) * slope[...].astype(FLOAT)).astype(LOW)
+    inner_grad[...] = grad
+    sums[pl.ds(4 + step, 1), :] = column_sum(grad.astype(FLOAT))
+    normed_grad[...] += dot_nt(grad, up[...])
+
+    @pl.when(step == pl.num_programs(0) - 1)
+    def _():
+        total = normed_grad[...]
+        unit = unit1[...]
+        sums[0:1, :] = column_sum(total * unit)
+        sums[1:2, :] = column_sum(total)
+        grad1 = norm_back(total * gain1[...], unit, inverse1[:, 0:1])
+        first_grad[...] = grad1
+        low = grad1.astype(LOW)
+        branch_grad[...] = low
+        sums[2:3, :] = column_sum(low.astype(FLOAT))
+        back_own[...] = dot_nt(low, wo_own[...]).astype(LOW)
+        back_send[...] = dot_nt(low, wo_other[...]).astype(LOW)
+
+
+def backward(place, feed_grad, slope, second_grad, unit1, inverse1, weights):
+    chunk = WIDTH
+    steps = FF // chunk
+    return pl.pallas_call(
+        backward_kernel,
+        grid_spec=pltpu.PrefetchScalarGridSpec(
+            num_scalar_prefetch=1,
+            grid=(steps,),
+            in_specs=[
+                whole((OWN, WIDTH)),
+                pl.BlockSpec((OWN, chunk), lambda i, place: (0, i)),
+                pl.BlockSpec((WIDTH, chunk), lambda i, place: (0, i)),
+                pl.BlockSpec((chunk, WIDTH), lambda i, place: (i, 0)),
+                whole((OWN, WIDTH)), whole((OWN, WIDTH)), whole((OWN, LANES)), whole((1, WIDTH)),
+                pl.BlockSpec((HALF, WIDTH), lambda i, place: (place[3], 0)),
+                pl.BlockSpec((HALF, WIDTH), lambda i, place: (1 - place[3], 0)),
+            ],
+            out_specs=[
+                pl.BlockSpec((OWN, chunk), lambda i, place: (0, i)),
+                whole((OWN, WIDTH)), whole((OWN, WIDTH)), whole((OWN, HALF)), whole((OWN, HALF)),
+                whole((8, WIDTH)),
+            ],
+            scratch_shapes=[pltpu.VMEM((OWN, WIDTH), FLOAT)],
+        ),
+        out_shape=[
+            shaped((OWN, FF), LOW),
+            shaped((OWN, WIDTH), FLOAT),
+            shaped((OWN, WIDTH), LOW),
+            shaped((OWN, HALF), LOW),
+            shaped((OWN, HALF), LOW),
+            shaped((8, WIDTH), FLOAT),
+        ],
+        compiler_params=kernel_params(40),
+        cost_estimate=cost(2.7e9, 16e6),
+        name="backward",
+    )(
+        place, feed_grad, slope, weights["up"], weights["down"], second_grad, unit1, inverse1,
+        row_of(weights["gain1"]), weights["out"], weights["out"],
+    )
+
+
+def up_kernel(kept, place, normed_t, inner0, inner1, att_t, branch_grad, sums0, sums1, out):
+    part = place[3] if kept else 1 - place[3]
+    outer = dot(att_t[...], branch_grad[...])
+    for x, inner, sums in ((0, inner0, sums0), (1, inner1, sums1)):
+        first = outer[x * 48 : x * 48 + 24]
+        second = outer[x * 48 + 24 : x * 48 + 48]
+        out[x] = jnp.concatenate(
+            [dot(normed_t[...], inner[...]), jnp.where(part == 0, first, second), sums[...]], axis=0
+        ).astype(LOW)
+
+
+def up_units(place, normed_t, inner_grad, att_t, branch_grad, sums0, sums1, kept):
+    def part(place):
+        return place[3] if kept else 1 - place[3]
+
+    return pl.pallas_call(
+        functools.partial(up_kernel, kept),
+        grid_spec=pltpu.PrefetchScalarGridSpec(
+            num_scalar_prefetch=1,
+            grid=(8,),
+            in_specs=[
+                pl.BlockSpec((96, OWN), lambda i, place: (i, 0)),
+                pl.BlockSpec((OWN, WIDTH), lambda i, place: (0, part(place))),
+                pl.BlockSpec((OWN, WIDTH), lambda i, place: (0, 2 + part(place))),
+                pl.BlockSpec((96, OWN), lambda i, place: (i, 0)),
+                whole((OWN, WIDTH)), whole((8, WIDTH)), whole((8, WIDTH)),
+            ],
+            out_specs=pl.BlockSpec((2, UP_ROWS, WIDTH), lambda i, place: (i, 0, 0)),
+        ),
+        out_shape=shaped((16, UP_ROWS, WIDTH), LOW),
+        compiler_params=kernel_params(16),
+        cost_estimate=cost(0.9e9, 5e6),
+        name="up_units",
+    )(place, normed_t, inner_grad, inner_grad, att_t, branch_grad, sums0, sums1)
+
+
+def attention_back_kernel(
+    place, own_lengths, peer_lengths, q, k, v, log_total, att0, att1, back0, back1,
+    dq_out, dk_out, dv_out, bias,
+):
+    bases = first_positions(place)
+    ends = pair_ends(place, own_lengths, peer_lengths)
+    query_ids = [pairs_along(base, ends, 1)[0:1] for base in bases[:4]]
+    for j in range(8):
+        key_ids = pairs_along(bases[j], ends, 0)
+        for i in range(4):
+            bias[pl.ds(j * BLOCK, BLOCK), pl.ds(i * BLOCK, BLOCK)] = jnp.where(
+                key_ids == query_ids[i], 0.0, NEGATIVE
+            )
+    for pair in range(PAIRS_OF_HEADS):
+        lanes = pl.ds(pair * LANES, LANES)
+        keys = k[:, lanes]
+        values = v[:, lanes]
+        keys_t = jnp.transpose(keys.astype(FLOAT)).astype(LOW)
+        key_grad = jnp.zeros((1024, LANES), FLOAT)
+        value_grad = jnp.zeros((1024, LANES), FLOAT)
+        left = head_mask(OWN)
+        for part, att, back in ((0, att0, back0), (1, att1, back1)):
+            rows = pl.ds(part * OWN, OWN)
+            queries = q[rows, lanes]
+            grads = back[:, lanes]
+            zeros = jnp.zeros_like(queries)
+            product = jnp.transpose(grads.astype(FLOAT) * att[:, lanes].astype(FLOAT))
+            halves = []
+            for half in range(2):
+                if half == 0:
+                    chosen, chosen_grads = jnp.where(left, queries, zeros), jnp.where(left, grads, zeros)
+                else:
+                    chosen, chosen_grads = jnp.where(left, zeros, queries), jnp.where(left, zeros, grads)
+                delta = column_sum(product[half * HEAD_DIM : (half + 1) * HEAD_DIM])
+                head = pair * 2 + half
+                scores = dot_nt(keys, chosen) + bias[:, rows]
+                weights = jnp.exp(scores - log_total[head : head + 1, rows])
+                weight_grad = dot_nt(values, chosen_grads)
+                score_grad = (weights * (weight_grad - delta)).astype(LOW)
+                value_grad = value_grad + dot(weights.astype(LOW), chosen_grads)
+                key_grad = key_grad + dot(score_grad, chosen)
+                halves.append(dot(keys_t, score_grad))
+            query_grad_t = jnp.concatenate([halves[0][0:HEAD_DIM], halves[1][HEAD_DIM:LANES]], axis=0)
+            dq_out[rows, lanes] = (jnp.transpose(query_grad_t) * HEAD_DIM**-0.5).astype(LOW)
+        dk_out[:, lanes] = key_grad.astype(LOW)
+        dv_out[:, lanes] = value_grad.astype(LOW)
+
+
+def attention_back(place, own_lengths, peer_lengths, q, k, v, log_total, att, back):
+    return pl.pallas_call(
+        attention_back_kernel,
+        grid_spec=pltpu.PrefetchScalarGridSpec(
+            num_scalar_prefetch=3,
+            grid=(1,),
+            in_specs=[whole((512, HALF)), whole((1024, HALF)), whole((1024, HALF)), whole((8, 512))]
+            + [whole((OWN, HALF))] * 4,
+            out_specs=[whole((512, HALF)), whole((1024, HALF)), whole((1024, HALF))],
+            scratch_shapes=[pltpu.VMEM((1024, 512), FLOAT)],
+        ),
+        out_shape=[shaped((512, HALF), LOW), shaped((1024, HALF), LOW), shaped((1024, HALF), LOW)],
+        compiler_params=kernel_params(40),
+        cost_estimate=cost(7e9, 6e6, 3e6),
+        name="attention_back",
+    )(place, own_lengths, peer_lengths, q, k, v, log_total, *att, *back)
+
+
+def token_kernel(place, dq, dk, dv, wq, wk, wv, send, keep):
+    for part in range(4):
+        rows = pl.ds(part * OWN, OWN)
+        total = dot_nt(dk[rows, :], wk[...]) + dot_nt(dv[rows, :], wv[...])
+        if part < 2:
+            total = total + dot_nt(dq[rows, :], wq[...])
+        target = keep if part % 2 == 0 else send
+        target[pl.ds((part // 2) * OWN, OWN), :] = total.astype(LOW)
+
+
+def token_parts(place, dq, dk, dv, joint_weight):
+    def columns(kind):
+        return pl.BlockSpec((WIDTH, HALF), lambda i, place: (0, 2 * kind + place[3]))
+
+    return pl.pallas_call(
+        token_kernel,
+        grid_spec=pltpu.PrefetchScalarGridSpec(
+            num_scalar_prefetch=1,
+            grid=(1,),
+            in_specs=[
+                whole((512, HALF)), whole((1024, HALF)), whole((1024, HALF)),
+                columns(0), columns(1), columns(2),
+            ],
+            out_specs=[whole((512, WIDTH)), whole((512, WIDTH))],
+        ),
+        out_shape=[shaped((512, WIDTH), LOW), shaped((512, WIDTH), LOW)],
+        compiler_params=kernel_params(32),
+        cost_estimate=cost(1.5e9, 5e6),
+        name="token_parts",
+    )(place, dq, dk, dv, joint_weight, joint_weight, joint_weight)
+
+
+def token_pair_kernel(keep, received, first_grad, send, own):
+    send[...] = (keep[OWN:, :].astype(FLOAT) + received[OWN:, :].astype(FLOAT)).astype(LOW)
+    own[...] = keep[:OWN, :].astype(FLOAT) + received[:OWN, :].astype(FLOAT) + first_grad[...]
+
+
+def token_pair(keep, received, first_grad):
+    return pl.pallas_call(
+        token_pair_kernel,
+        out_shape=[shaped((OWN, WIDTH), LOW), shaped((OWN, WIDTH), FLOAT)],
+        compiler_params=kernel_params(16),
+        cost_estimate=cost(1e6, 4e6),
+        name="token_pair",
+    )(keep, received, first_grad)
+
+
+def joint_kernel(
+    place, t0, t1, t2, t3, t4, t5, t6, t7, dq, dk, dv, px_send, px_keep, qy_send, qy_keep, tokens_t, rows_of
+):
+    y, x = place[1], place[2]
+    for index, block in enumerate((t0, t1, t2, t3, t4, t5, t6, t7)):
+        tokens_t[:, pl.ds(index * BLOCK, BLOCK)] = jnp.transpose(block[...].astype(FLOAT)).astype(LOW)
+    biases = jnp.concatenate(
+        [
+            column_sum(dq[...].astype(FLOAT)),
+            column_sum(dv[...].astype(FLOAT)),
+            jnp.zeros((14, HALF), FLOAT),
+        ],
+        axis=0,
+    )
+    for z in range(4):
+        for line in range(2):
+            rows = pl.ds((z * 2 + line) * 96, 96)
+            rows_of[0] = dot(tokens_t[rows, 0:512], dq[...])
+            rows_of[1] = dot(tokens_t[rows, :], dk[...])
+            rows_of[2] = dot(tokens_t[rows, :], dv[...])
+            for side in range(2):
+                target = (x + side) % 2
+                part = pl.ds(pl.multiple_of(target * 48, 16), 48)
+                unit = jnp.concatenate([rows_of[0, part], rows_of[1, part], rows_of[2, part], biases], axis=0)
+                unit = unit.astype(LOW)
+                px = px_keep if side == 0 else px_send
+                px[z, line] = unit[: JOINT_ROWS // 2]
+
+                @pl.when(y == line)
+                def _(unit=unit, target=target):
+                    qy_keep[z, target] = unit[JOINT_ROWS // 2 :]
+
+                @pl.when(y != line)
+                def _(unit=unit, target=target):
+                    qy_send[z, target] = unit[JOINT_ROWS // 2 :]
+
+
+def joint_units(place, blocks, dq, dk, dv):
+    out = (4, 2, JOINT_ROWS // 2, HALF)
+    return pl.pallas_call(
+        joint_kernel,
+        grid_spec=pltpu.PrefetchScalarGridSpec(
+            num_scalar_prefetch=1,
+            grid=(1,),
+            in_specs=[whole((BLOCK, WIDTH))] * 8
+            + [whole((512, HALF)), whole((1024, HALF)), whole((1024, HALF))],
+            out_specs=[whole(out)] * 4,
+            scratch_shapes=[pltpu.VMEM((WIDTH, 1024), LOW), pltpu.VMEM((3, 96, HALF), FLOAT)],
+        ),
+        out_shape=[shaped(out, LOW)] * 4,
+        compiler_params=kernel_params(32),
+        cost_estimate=cost(1.5e9, 6e6),
+        name="joint_units",
+    )(place, *blocks, dq, dk, dv)
+
+
+def added(left, right):
+    return (left.astype(FLOAT) + right.astype(FLOAT)).astype(LOW)
+
+
+def core_stage_kernel(place, kept, received, px_send, px_keep, qy_send, qy_keep):
+    y, x = place[1], place[2]
+    half = kept.shape[3] // 2
+    for line in range(2):
+        for target, side in ((px_keep, x), (px_send, 1 - x)):
+            target[0, line] = added(kept[0, line, side, 0:half], received[0, line, side, 0:half])
+    for side in range(2):
+        for target, line in ((qy_keep, y), (qy_send, 1 - y)):
+            target[0, side] = added(kept[0, line, side, half:], received[0, line, side, half:])
+
+
+def core_stage(place, kept, received):
+    rows = kept.shape[1]
+    block = pl.BlockSpec((1, 2, 2, rows, WIDTH), lambda i, place: (i, 0, 0, 0, 0))
+    out = (4, 2, rows // 2, WIDTH)
+    shape = (4, 2, 2, rows, WIDTH)
+    return pl.pallas_call(
+        core_stage_kernel,
+        grid_spec=pltpu.PrefetchScalarGridSpec(
+            num_scalar_prefetch=1,
+            grid=(4,),
+            in_specs=[block, block],
+            out_specs=[pl.BlockSpec((1,) + out[1:], lambda i, place: (i, 0, 0, 0))] * 4,
+        ),
+        out_shape=[shaped(out, LOW)] * 4,
+        compiler_params=kernel_params(24),
+        cost_estimate=cost(2e6, 3 * 2 * 16 * rows * WIDTH),
+        name="core_stage",
+    )(place, kept.reshape(shape), received.reshape(shape))
+
+
+def pair_stage_kernel(place, px, px_got, qy, qy_got, p_send, p_keep, q_send, q_keep):
+    y, x = place[1], place[2]
+    p_keep[0] = added(px[0, y], px_got[0, y])
+    p_send[0] = added(px[0, 1 - y], px_got[0, 1 - y])
+    q_keep[0] = added(qy[0, x], qy_got[0, x])
+    q_send[0] = added(qy[0, 1 - x], qy_got[0, 1 - x])
+
+
+def pair_stage(place, px, px_got, qy, qy_got):
+    _, _, half, width = px.shape
+    block = pl.BlockSpec((1, 2, half, width), lambda i, place: (i, 0, 0, 0))
+    return pl.pallas_call(
+        pair_stage_kernel,
+        grid_spec=pltpu.PrefetchScalarGridSpec(
+            num_scalar_prefetch=1,
+            grid=(4,),
+            in_specs=[block] * 4,
+            out_specs=[pl.BlockSpec((1, half, width), lambda i, place: (i, 0, 0))] * 4,
+        ),
+        out_shape=[shaped((4, half, width), LOW)] * 4,
+        compiler_params=kernel_params(24),
+        cost_estimate=cost(1e6, 6 * 2 * 8 * half * width),
+        name="pair_stage",
+    )(place, px, px_got, qy, qy_got)
+
+
+def line_stage_kernel(place, p, p_got, q, q_got, keep, one, two, three):
+    z = place[0]
+    half = p.shape[1]
+    low, high = z % 2, z // 2
+    flipped = 1 - low
+    other = 1 - high
+    for target, index in (
+        (keep, z),
+        (one, 2 * high + flipped),
+        (two, 2 * other + low),
+        (three, 2 * other + flipped),
+    ):
+        target[0:half] = added(p[index], p_got[index])
+        target[half:] = added(q[index], q_got[index])
+
+
+def line_stage(place, p, p_got, q, q_got):
+    _, half, width = p.shape
+    block = whole((4, half, width))
+    return pl.pallas_call(
+        line_stage_kernel,
+        grid_spec=pltpu.PrefetchScalarGridSpec(
+            num_scalar_prefetch=1,
+            grid=(1,),
+            in_specs=[block] * 4,
+            out_specs=[whole((2 * half, width))] * 4,
+        ),
+        out_shape=[shaped((2 * half, width), LOW)] * 4,
+        compiler_params=kernel_params(24),
+        cost_estimate=cost(1e6, 6 * 2 * 4 * half * width),
+        name="line_stage",
+    )(place, p, p_got, q, q_got)
+
+
+def last_sum_kernel(first, second, third, fourth, out):
+    total = first[...].astype(FLOAT) + second[...].astype(FLOAT)
+    out[...] = (total + (third[...].astype(FLOAT) + fourth[...].astype(FLOAT))).astype(LOW)
+
+
+def last_sum(parts):
+    shape = parts[0].shape
+    return pl.pallas_call(
+        last_sum_kernel,
+        out_shape=shaped(shape, LOW),
+        compiler_params=kernel_params(16),
+        cost_estimate=cost(1e6, 5 * 2 * shape[0] * shape[1]),
+        name="last_sum",
+    )(*parts)
+
+
+def reduce_units(place, px_send, px_keep, qy_send, qy_keep):
+    px_got = x_swap(px_send)
+    qy_got = y_swap(qy_send)
+    p_send, p_keep, q_send, q_keep = pair_stage(place, px_keep, px_got, qy_keep, qy_got)
+    p_got = y_swap(p_send)
+    q_got = x_swap(q_send)
+    keep, one, two, three = line_stage(place, p_keep, p_got, q_keep, q_got)
+    unit = last_sum((keep, z_swap(one, 1), z_swap(two, 2), z_swap(three, 3)))
+    return lax.all_gather(unit, "rows", axis=0)
+
+
+def pick_rows(total, rows, place):
+    seq = place[0] * 2 + place[1]
+    shift = lax.rem(WIDTH - seq * 96, WIDTH)
+    return pltpu.roll(total, shift, 1)[rows, 0:96]
+
+
+def up_out_kernel(place, units, up, out, gain2, shift2, down_bias, gain1, shift1, out_bias, up_bias, sums):
+    for q in range(4):
+        up[:, pl.ds(q * WIDTH, WIDTH)] = units[q, 0:96, :].astype(FLOAT)
+        out[pl.ds(q * 24, 24), :] = units[q, 96:120, :].astype(FLOAT)
+    seq = place[0] * 2 + place[1]
+    shift = lax.rem(WIDTH - seq * 96, WIDTH)
+    head = pltpu.roll(units[0, 112:128, :].astype(FLOAT)[8:16], shift, 1)
+    gain2[...] = head[0:1, 0:96]
+    shift2[...] = head[1:2, 0:96]
+    down_bias[...] = head[2:3, 0:96]
+    tail = units[2, 112:128, :].astype(FLOAT)[8:16]
+    sums[...] = tail
+    turned = pltpu.roll(tail, shift, 1)
+    gain1[...] = turned[0:1, 0:96]
+    shift1[...] = turned[1:2, 0:96]
+    out_bias[...] = turned[2:3, 0:96]
+    wide = sums[pl.ds(4 + seq // 2, 1), :]
+    up_bias[...] = jnp.where(seq % 2 == 0, wide[:, 0:HALF], wide[:, HALF:])
+
+
+def up_outputs(place, units):
+    small = [whole((1, 96))] * 6 + [whole((1, HALF))]
+    results = pl.pallas_call(
+        up_out_kernel,
+        grid_spec=pltpu.PrefetchScalarGridSpec(
+            num_scalar_prefetch=1,
+            grid=(1,),
+            in_specs=[whole((4, UP_ROWS, WIDTH))],
+            out_specs=[whole((96, FF)), whole((96, WIDTH))] + small,
+            scratch_shapes=[pltpu.VMEM((8, WIDTH), FLOAT)],
+        ),
+        out_shape=[shaped((96, FF), FLOAT), shaped((96, WIDTH), FLOAT)]
+        + [shaped((1, 96), FLOAT)] * 6
+        + [shaped((1, HALF), FLOAT)],
+        compiler_params=kernel_params(16),
+        cost_estimate=cost(1e6, 3e6),
+        name="up_outputs",
+    )(place, units)
+    return (*results[:2], *(vector.reshape(-1) for vector in results[2:]))
+
+
+def joint_out_kernel(place, units, joint, query_bias, value_bias, sums):
+    for x in range(2):
+        for c in range(2):
+            unit = units[2 * x + c]
+            for kind in range(3):
+                joint[pl.ds(x * 48, 48), pl.ds(kind * WIDTH + c * HALF, HALF)] = unit[
+                    kind * 48 : kind * 48 + 48
+                ].astype(FLOAT)
+            if x == 0:
+                sums[:, pl.ds(c * HALF, HALF)] = unit[144:160].astype(FLOAT)
+    seq = place[0] * 2 + place[1]
+    shift = lax.rem(WIDTH - seq * 96, WIDTH)
+    turned = pltpu.roll(sums[0:8, :], shift, 1)
+    query_bias[...] = turned[0:1, 0:96]
+    value_bias[...] = turned[1:2, 0:96]
+
+
+def joint_outputs(place, units):
+    results = pl.pallas_call(
+        joint_out_kernel,
+        grid_spec=pltpu.PrefetchScalarGridSpec(
+            num_scalar_prefetch=1,
+            grid=(1,),
+            in_specs=[whole((4, JOINT_ROWS, HALF))],
+            out_specs=[whole((96, 3 * WIDTH)), whole((1, 96)), whole((1, 96))],
+            scratch_shapes=[pltpu.VMEM((16, WIDTH), FLOAT)],
+        ),
+        out_shape=[shaped((96, 3 * WIDTH), FLOAT), shaped((1, 96), FLOAT), shaped((1, 96), FLOAT)],
+        compiler_params=kernel_params(16),
+        cost_estimate=cost(1e6, 2e6),
+        name="joint_outputs",
+    )(place, units)
+    return results[0], results[1].reshape(-1), results[2].reshape(-1)
+
+
+def row_body(
+    tokens,
+    pair_lengths,
+    joint_weight,
+    query_bias,
+    value_bias,
+    out_weight,
+    out_bias,
+    first_gain,
+    first_shift,
+    up_weight,
+    up_bias,
+    down_weight,
+    down_bias,
+    second_gain,
+    second_shift,
+    cotangent,
+):
+    seq, rows = lax.axis_index("seq"), lax.axis_index("rows")
+    z, y, x, c = seq // 2, seq % 2, rows // 2, rows % 2
+    place = jnp.stack([z, y, x, c]).astype(jnp.int32)
+    odd = z % 2
+    weights = {
+        "out": out_weight, "out_bias": out_bias, "gain1": first_gain, "shift1": first_shift,
+        "up": up_weight, "up_bias": up_bias, "down": down_weight, "down_bias": down_bias,
+        "gain2": second_gain, "shift2": second_shift,
+    }
+
+    def local_row(array, index):
+        return lax.dynamic_index_in_dim(array, index, 0, keepdims=False)
+
+    own = [row_swap(local_row(tokens, odd), 0), row_swap(local_row(tokens, 1 - odd), 1)]
+    peer_lengths = core_swap(pair_lengths)
+    across = [y_swap(block) for block in own]
+    blocks = (
+        own + [core_swap(block) for block in own] + across + [core_swap(block) for block in across]
+    )
+    cotangent, _ = lax.optimization_barrier((cotangent, across[0]))
+    cotangents = [row_swap(local_row(cotangent, odd), 0), row_swap(local_row(cotangent, 1 - odd), 1)]
+
+    att_own, att_send, q, k, v, log_total = attention(
+        place, pair_lengths, peer_lengths, blocks, joint_weight, query_bias, value_bias
+    )
+    att_other = core_swap(att_send)
+    out0, out1, feed_grad, second_grad, act_t, slope, unit1, inverse1, normed_t, att_t, sums0 = forward(
+        place, att_own, att_other, own, cotangents, weights
+    )
+    down_sent = core_swap(down_units(place, act_t, feed_grad, False))
+    down_kept = down_units(place, act_t, feed_grad, True)
+    down_gathered = reduce_units(place, *core_stage(place, down_kept, down_sent))
+    inner_grad, first_grad, branch_grad, back_own, back_send, sums1 = backward(
+        place, feed_grad, slope, second_grad, unit1, inverse1, weights
+    )
+    back_other = core_swap(back_send)
+    up_args = (place, normed_t, inner_grad, att_t, branch_grad, sums0, sums1)
+    up_sent = core_swap(up_units(*up_args, False))
+    up_kept = up_units(*up_args, True)
+    up_gathered = reduce_units(place, *core_stage(place, up_kept, up_sent))
+
+    dq, dk, dv = attention_back(
+        place, pair_lengths, peer_lengths, q, k, v, log_total, (att_own, att_send), (back_own, back_other)
+    )
+    token_send, token_keep = token_parts(place, dq, dk, dv, joint_weight)
+    token_got = core_swap(token_send)
+    joint_gathered = reduce_units(place, *joint_units(place, blocks, dq, dk, dv))
+    token_across, token_own = token_pair(token_keep, token_got, first_grad)
+    token_low = (token_own + y_swap(token_across).astype(FLOAT)).astype(LOW)
+    back0 = row_swap(token_low[:BLOCK], 0)
+    back1 = row_swap(token_low[BLOCK:], 1)
+    first, second = jnp.where(odd == 0, back0, back1), jnp.where(odd == 0, back1, back0)
+    token_grad = jnp.stack([first, second]).astype(FLOAT)
+    done0, done1 = row_swap(out0, 0), row_swap(out1, 1)
+    outputs = jnp.stack([jnp.where(odd == 0, done0, done1), jnp.where(odd == 0, done1, done0)])
+
+    down_grad = down_gathered.reshape(4 * DOWN_ROWS, WIDTH).astype(FLOAT)
+    (
+        up_grad, out_grad, second_gain_grad, second_shift_grad, down_bias_grad, first_gain_grad,
+        first_shift_grad, out_bias_grad, up_bias_grad,
+    ) = up_outputs(place, up_gathered)
+    joint_grad, query_bias_grad, value_bias_grad = joint_outputs(place, joint_gathered)
+    return (
+        outputs,
+        token_grad,
+        joint_grad,
+        query_bias_grad,
+        value_bias_grad,
+        out_grad,
+        out_bias_grad,
+        first_gain_grad,
+        first_shift_grad,
+        up_grad,
+        up_bias_grad,
+        down_grad,
+        down_bias_grad,
+        second_gain_grad,
+        second_shift_grad,
+    )
+
+
+def body(tokens, *others):
+    if (lax.axis_size("seq"), lax.axis_size("rows")) == (8, 4) and tokens.shape == (2, BLOCK, WIDTH):
+        return row_body(tokens, *others)
+    return general_body(tokens, *others)
+
+
 def solution(mesh):
     placed = (
         P("rows", "seq", None),

time: 1040 us -> 229 us (0.22)
  waiting for transfers between devices: 573 us -> 36.9 us
  matrix products: 149 us -> 0 us
  other arithmetic: 127 us -> 5.64 us
  local copies, waits for them, and re-layouts: 114 us -> 12.8 us
  Pallas kernels: 0 us -> 74.8 us
  starting transfers between devices: 10.2 us -> 66.4 us
  between operations: 16.4 us -> 1.4 us
  blocking collectives: 43.7 us -> 30.1 us
    reduce_scatter x3 -> x0, waiting for transfers between devices: 262 us -> none  [the longest x1 98.6 us: body(): lax.psum_scatter(gradients[9].astype(jnp.bfloat16), 'seq', scatter_dimens...]
    dot_general x68 -> x0, matrix products: 149 us -> none  [the longest x8 25.5 us: online_block(): jnp.einsum('rqhd,rkhd->rhqk', query_heads, split_heads(key_block), prefer...]
    all_gather x2 -> x0, waiting for transfers between devices: 114 us -> none  [the longest x1 63.3 us: body(): key_piece = lax.all_gather(keys, 'seq', axis=1, tiled=True)]
    ppermute x30 -> x42, waiting for transfers between devices: 131 us -> 36.9 us  [permute(): return lax.ppermute(value, AXES, pairs)]
    pallas_call x0 -> x24, Pallas kernels: none -> 74.8 us  [the longest x1 9.31 us: attention_back(): pl.pallas_call(attention_back_kernel, grid_spec=pltpu.PrefetchScalarGridS...]
    unnamed x8 -> x0, waiting for transfers between devices: 66.9 us -> none
    convert_element_type x44 -> x3, other arithmetic: 61.7 us -> 3.11 us  [the longest x1 1.09 us: row_body(): down_grad = down_gathered.reshape(4 * DOWN_ROWS, WIDTH).astype(FLOAT)]
    ppermute x30 -> x42, starting transfers between devices: 9.92 us -> 66.4 us  [permute(): return lax.ppermute(value, AXES, pairs)]
  transfers between devices with their start and end apart: 37 -> 42, of which waited for: 21 -> 10; matrix products, arithmetic and copies ran while one was open for 19% -> 3% of each run, Pallas kernels for 0% -> 23%
where the time goes in v1:
time: 229 us; the launch traced here: 228 us
  Pallas kernels  74.8 us (33%)
  starting transfers between devices  66.4 us (29%)
  waiting for transfers between devices  36.9 us (16%)
  blocking collectives  30.1 us (13%)
  local copies, waits for them, and re-layouts  12.8 us (6%)
  other arithmetic  5.64 us (2%)
    ppermute x42, starting transfers between devices, permute(): return lax.ppermute(value, AXES, pairs)  66.4 us
    ppermute x42, waiting for transfers between devices, permute(): return lax.ppermute(value, AXES, pairs)  36.9 us
    all_gather x3, blocking collectives, reduce_units(): return lax.all_gather(unit, 'rows', axis=0)  30.1 us
    unnamed x96, local copies, waits for them, and re-layouts  9.32 us
    pallas_call x1, Pallas kernels, attention_back(): pl.pallas_call(attention_back_kernel, grid_spec=pltpu.PrefetchScalarGridS...  9.31 us
    pallas_call x1, Pallas kernels, attention(): pl.pallas_call(attention_kernel, grid_spec=pltpu.PrefetchScalarGridSpec(n...  9.11 us
    pallas_call x1, Pallas kernels, forward(): pl.pallas_call(forward_kernel, grid_spec=pltpu.PrefetchScalarGridSpec(num...  8.67 us
    pallas_call x2, Pallas kernels, down_units(): pl.pallas_call(down_kernel, grid_spec=pltpu.PrefetchScalarGridSpec(num_sc...  7.69 us
  transfers between devices with their start and end apart: 42, of which 10 were waited for; matrix products, arithmetic and copies ran while one was open for 3% of the time, Pallas kernels for 23%

profile of v1, /device:TPU:0, one launch (start us, length us, event | category | flops | bytes accessed | tf_op | source)
XLA Modules:
  0.0 228.1 jit_solution(146199714152738880)
XLA Ops:
  2.4 3.1 %collective-permute-start.2 = (bf16[128,768]{1,0:T(8,128)(2,1)S(1)}, bf16[128,768]{1,0:T(8,128)(2,1)S(1)}, u32[]{:S(2)}, u32[]{:S(2)}) collective-permute-start(bf16[128,768]{1,0:T(8,128)(2,1)S(1)} %get-tuple-element.181), channel_id=1, source_target_pairs={{0,8},{1,24},{2,10},{3,26},{4,12},{5,28},{6,14},{7,30},{8,0},{9,16... | collective-permute-start | bytes 589832 | tf_op jit(solution)/shard_map/ppermute | solution.py:366
  5.5 1.5 collective-permute-start.5
  7.0 2.1 collective-permute-done.2.refs_1_.x1.t1
  9.2 3.3 %collective-permute-start.6 = (bf16[128,768]{1,0:T(8,128)(2,1)S(1)}, bf16[128,768]{1,0:T(8,128)(2,1)S(1)}, u32[]{:S(2)}, u32[]{:S(2)}) collective-permute-start(bf16[128,768]{1,0:T(8,128)(2,1)S(1)} %collective-permute-done.2.refs_1_.x1.t1), channel_id=1, source_target_pairs={{0,4},{1,5},{2,6},{3,7},{4,0},{5,1},{6,2},{7,3},{8,12},{9,13},{10,... | collective-permute-start | bytes 589832 | tf_op jit(solution)/shard_map/ppermute | solution.py:366
  12.5 4.4 %collective-permute-start = (s32[2,16]{1,0:T(2,128)}, s32[2,16]{1,0:T(2,128)S(1)}, u32[]{:S(2)}, u32[]{:S(2)}) collective-permute-start(s32[2,16]{1,0:T(2,128)} %own_lengths.3), channel_id=1, source_target_pairs={{0,1},{1,0},{2,3},{3,2},{4,5},{5,4},{6,7},{7,6},{8,9},{9,8},{10,11... | collective-permute-start | bytes 392 | tf_op jit(solution)/shard_map/ppermute | solution.py:366
  19.9 2.1 collective-permute-start.8
  24.8 2.1 copy-done
  27.6 9.1 %attention.1 = (bf16[256,384]{1,0:T(8,128)(2,1)S(1)}, bf16[256,384]{1,0:T(8,128)(2,1)S(1)}, bf16[512,384]{1,0:T(8,128)(2,1)S(1)}, bf16[1024,384]{1,0:T(8,128)(2,...) custom-call(s32[4]{0:T(128)S(1)} %pad_add_fusion.place, s32[2,16]{1,0:T(2,128)S(1)} %copy-done.38, ...), custom_call_target="tpu_custom_call" | custom-call | flops 4000000000 | bytes 8000000 | tf_op jit(solution)/shard_map/attention/pallas_call | solution.py:486
  36.8 5.3 %collective-permute-start.9 = (bf16[256,384]{1,0:T(8,128)(2,1)S(1)}, bf16[256,384]{1,0:T(8,128)(2,1)S(1)}, u32[]{:S(2)}, u32[]{:S(2)}) collective-permute-start(bf16[256,384]{1,0:T(8,128)(2,1)S(1)} %get-tuple-element.95.att1), channel_id=1, source_target_pairs={{0,1},{1,0},{2,3},{3,2},{4,5},{5,4},{6,7},{7,6},{8,9},{9,8},{10,11... | collective-permute-start | bytes 589832 | tf_op jit(solution)/shard_map/ppermute | solution.py:366
  43.2 8.7 %forward.1 = (bf16[128,768]{1,0:T(8,128)(2,1)S(1)}, bf16[128,768]{1,0:T(8,128)(2,1)S(1)}, bf16[256,768]{1,0:T(8,128)(2,1)S(1)}, f32[256,768]{1,0:T(8,128)S(1)}, ...) custom-call(s32[4]{0:T(128)S(1)} %pad_add_fusion.place, ...), custom_call_target="tpu_custom_call" | custom-call | flops 2700000000 | bytes 20000000 | tf_op jit(solution)/shard_map/forward/pallas_call | solution.py:606
  53.2 7.5 %backward.1 = (bf16[256,3072]{1,0:T(8,128)(2,1)S(1)}, f32[256,768]{1,0:T(8,128)S(1)}, bf16[256,768]{1,0:T(8,128)(2,1)S(1)}, bf16[256,384]{1,0:T(8,128)(2,1)S(1)}...) custom-call(s32[4]{0:T(128)S(1)} %pad_add_fusion.place, bf16[256,768]{1,0:T(8,128)(2,1)S(1)} %get-tuple-element.103.feed_grad, ...), custom_call_target="tpu_custom_call" | custom-call | flops 2700000000 | bytes 16000000 | tf_op jit(solution)/shard_map/backward/pallas_call | solution.py:721
  60.7 3.4 %up_units.3 = bf16[16,128,768]{2,1,0:T(8,128)(2,1)S(1)} custom-call(s32[4]{0:T(128)S(1)} %pad_add_fusion.place, bf16[768,256]{1,0:T(8,128)(2,1)S(1)} %get-tuple-element.133.normed_t, bf16[256,3072]{1,0:T(8,128)(2,1)S(1)} %get-tuple-element.134.inner0.inner1, bf16[256,3072]{1,0:T(8,128)(2,1)S(1)} %get-tuple-element.134.inner0.inner1, ...), custom_call_target="tpu_custom_call" | custom-call | flops 900000000 | bytes 5000000 | tf_op jit(solution)/shard_map/up_units/pallas_call | solution.py:774
  64.6 4.9 %down_units.3 = bf16[16,96,768]{2,1,0:T(8,128)(2,1)} custom-call(s32[4]{0:T(128)S(1)} %pad_add_fusion.place, bf16[8,2,2,96,256]{4,3,2,1,0:T(8,128)(2,1)S(1)} %bitcast.38, bf16[256,768]{1,0:T(8,128)(2,1)S(1)} %get-tuple-element.103.feed_grad), custom_call_target="tpu_custom_call" | custom-call | flops 600000000 | bytes 3500000 | tf_op jit(solution)/shard_map/down_units/pallas_call | solution.py:665
  70.0 4.1 %collective-permute-done.14.back1 = bf16[256,384]{1,0:T(8,128)(2,1)S(1)} collective-permute-done((bf16[256,384]{1,0:T(8,128)(2,1)S(1)}, bf16[256,384]{1,0:T(8,128)(2,1)S(1)}, u32[]{:S(2)}, u32[]{:S(2)}) %collective-permute-start.14) | collective-permute-done | bytes 196640 | tf_op jit(solution)/shard_map/ppermute | solution.py:366
  74.0 9.3 %attention_back.1 = (bf16[512,384]{1,0:T(8,128)(2,1)S(1)}, bf16[1024,384]{1,0:T(8,128)(2,1)S(1)}, bf16[1024,384]{1,0:T(8,128)(2,1)S(1)}) custom-call(s32[4]{0:T(128)S(1)} %pad_add_fusion.place, s32[2,16]{1,0:T(2,128)S(1)} %copy-done.39, s32[2,16]{1,0:T(2,128)S(1)} %collective-permute-done.peer_lengths, bf16[512,384]{1,0:T(8,128)(2,1)S(1)} %get-tuple-element.99.q, ...), custom_call_target="tpu_custom_call" | custom-call | flops 7000000000 | bytes 6000000 | tf_op jit(solution)/shard_map/attention_back/pallas_call | solution.py:844
  83.5 2.8 %token_parts.1 = (bf16[512,768]{1,0:T(8,128)(2,1)S(1)}, bf16[512,768]{1,0:T(8,128)(2,1)S(1)}) custom-call(s32[4]{0:T(128)S(1)} %pad_add_fusion.place, bf16[512,384]{1,0:T(8,128)(2,1)S(1)} %get-tuple-element.110.dq, bf16[1024,384]{1,0:T(8,128)(2,1)S(1)} %get-tuple-element.111.dk, bf16[1024,384]{1,0:T(8,128)(2,1)S(1)} %get-tuple-element.112.dv, ...), custom_call_target="tpu_custom_call" | custom-call | flops 1500000000 | bytes 5000000 | tf_op jit(solution)/shard_map/token_parts/pallas_call | solution.py:875
  86.7 5.2 %joint_units.1 = (bf16[4,2,80,384]{3,2,1,0:T(8,128)(2,1)S(1)}, bf16[4,2,80,384]{3,2,1,0:T(8,128)(2,1)S(1)}, bf16[4,2,80,384]{3,2,1,0:T(8,128)(2,1)S(1)}, bf16[4,2,80,384]{3,2,1,0:T(8,128)(2,1)S(1)}) custom-call(s32[4]{0:T(128)S(1)} %pad_add_fusion.place, bf16[128,768]{1,0:T(8,128)(2,1)S(1)} %copy-done.17, bf16[128,768]{1,0:T(8,128)(2,1)S(1)} %copy-done.19, ...), custom_call_target="tpu_custom_call" | custom-call | flops 1500000000 | bytes 6000000 | tf_op jit(solution)/shard_map/joint_units/pallas_call | solution.py:947
  92.0 1.6 collective-permute-start.19
  93.6 1.5 collective-permute-start.20
  95.1 10.2 %collective-permute-done.19.px_got = bf16[4,2,80,384]{3,2,1,0:T(8,128)(2,1)S(1)} collective-permute-done((bf16[4,2,80,384]{3,2,1,0:T(8,128)(2,1)S(1)}, bf16[4,2,80,384]{3,2,1,0:T(8,128)(2,1)S(1)}, u32[]{:S(2)}, u32[]{:S(2)}) %collective-permute-start.19) | collective-permute-done | bytes 491552 | tf_op jit(solution)/shard_map/ppermute | solution.py:366
  107.1 1.9 pair_stage.3
  109.8 1.5 collective-permute-start.21
  113.8 2.8 %down_units.2 = bf16[16,96,768]{2,1,0:T(8,128)(2,1)S(1)} custom-call(s32[4]{0:T(128)S(1)} %pad_add_fusion.place, bf16[8,2,2,96,256]{4,3,2,1,0:T(8,128)(2,1)S(1)} %bitcast.39, bf16[256,768]{1,0:T(8,128)(2,1)S(1)} %get-tuple-element.103.feed_grad), custom_call_target="tpu_custom_call" | custom-call | flops 600000000 | bytes 3500000 | tf_op jit(solution)/shard_map/down_units/pallas_call | solution.py:665
  116.6 2.3 core_stage.3
  120.7 1.5 collective-permute-start.36
  122.3 3.4 %up_units.2 = bf16[16,128,768]{2,1,0:T(8,128)(2,1)S(1)} custom-call(s32[4]{0:T(128)S(1)} %pad_add_fusion.place, bf16[768,256]{1,0:T(8,128)(2,1)S(1)} %get-tuple-element.133.normed_t, bf16[256,3072]{1,0:T(8,128)(2,1)S(1)} %get-tuple-element.134.inner0.inner1, bf16[256,3072]{1,0:T(8,128)(2,1)S(1)} %get-tuple-element.134.inner0.inner1, ...), custom_call_target="tpu_custom_call" | custom-call | flops 900000000 | bytes 5000000 | tf_op jit(solution)/shard_map/up_units/pallas_call | solution.py:774
  125.7 2.3 %core_stage.2 = (bf16[4,2,64,768]{3,2,1,0:T(8,128)(2,1)}, bf16[4,2,64,768]{3,2,1,0:T(8,128)(2,1)S(1)}, bf16[4,2,64,768]{3,2,1,0:T(8,128)(2,1)S(1)}, bf16[4,2,64,768]{3,2,1,0:T(8,128)(2,1)S(1)}) custom-call(s32[4]{0:T(128)S(1)} %pad_add_fusion.place, bf16[4,2,2,128,768]{4,3,2,1,0:T(8,128)(2,1)S(1)} %bitcast.36, bf16[4,2,2,128,768]{4,3,2,1,0:T(8,128)(2,1)S(1)} %bitcast.40), custom_call_target="tpu_custom_call" | custom-call | flops 2000000 | bytes 9437184 | tf_op jit(solution)/shard_map/core_stage/pallas_call | solution.py:984
  134.2 1.6 line_stage.3
  135.8 1.5 collective-permute-start.23
  138.4 10.2 %collective-permute-start.24 = (bf16[160,384]{1,0:T(8,128)(2,1)S(1)}, bf16[160,384]{1,0:T(8,128)(2,1)S(1)}, u32[]{:S(2)}, u32[]{:S(2)}) collective-permute-start(bf16[160,384]{1,0:T(8,128)(2,1)S(1)} %get-tuple-element.128), channel_id=1, source_target_pairs={{0,16},{1,17},{2,18},{3,19},{4,20},{5,21},{6,22},{7,23},{8,24},{9,... | collective-permute-start | bytes 368648 | tf_op jit(solution)/shard_map/ppermute | solution.py:366
  148.6 1.4 collective-permute-start.25
  150.0 2.9 %pair_stage.5 = (bf16[4,48,768]{2,1,0:T(8,128)(2,1)S(1)}, bf16[4,48,768]{2,1,0:T(8,128)(2,1)S(1)}, bf16[4,48,768]{2,1,0:T(8,128)(2,1)S(1)}, bf16[4,48,768]{2,1,0:T(8,128)(2,1)S(1)}) custom-call(s32[4]{0:T(128)S(1)} %pad_add_fusion.place, bf16[4,2,48,768]{3,2,1,0:T(8,128)(2,1)S(1)} %copy-done.7, bf16[4,2,48,768]{3,2,1,0:T(8,128)(2,1)} %collective-permute-done.35.px_got, ...), custom_call_target="tpu_custom_call" | custom-call | flops 1000000 | bytes 3538944 | tf_op jit(solution)/shard_map/pair_stage/pallas_call | solution.py:1010
  152.9 1.6 collective-permute-start.37
  154.5 1.4 collective-permute-done.24.third
  160.2 1.5 collective-permute-start.29
  161.6 1.3 collective-permute-done.37.p_got
  162.9 1.6 collective-permute-start.30
  164.5 14.8 %all-gather = bf16[640,384]{1,0:T(8,128)(2,1)S(1)} all-gather(bf16[160,384]{1,0:T(8,128)(2,1)S(1)} %last_sum.3), channel_id=2, replica_groups=mesh['seq'=8,'rows'=4] {'rows'}, dimensions={0}, use_global_device_ids=true | all-gather | bytes 614400 | tf_op jit(solution)/shard_map/all_gather | solution.py:1083
  179.3 1.5 joint_outputs.1
  182.6 2.2 collective-permute-start.40
  186.9 3.1 %collective-permute-done.39.second = bf16[96,768]{1,0:T(8,128)(2,1)S(1)} collective-permute-done((bf16[96,768]{1,0:T(8,128)(2,1)S(1)}, bf16[96,768]{1,0:T(8,128)(2,1)S(1)}, u32[]{:S(2)}, u32[]{:S(2)}) %collective-permute-start.39) | collective-permute-done | bytes 147488 | tf_op jit(solution)/shard_map/ppermute | solution.py:366
  190.1 6.5 %collective-permute-done.40.third = bf16[96,768]{1,0:T(8,128)(2,1)S(1)} collective-permute-done((bf16[96,768]{1,0:T(8,128)(2,1)S(1)}, bf16[96,768]{1,0:T(8,128)(2,1)S(1)}, u32[]{:S(2)}, u32[]{:S(2)}) %collective-permute-start.40) | collective-permute-done | bytes 147488 | tf_op jit(solution)/shard_map/ppermute | solution.py:366
  197.4 2.9 %collective-permute-start.31 = (bf16[128,768]{1,0:T(8,128)(2,1)S(1)}, bf16[128,768]{1,0:T(8,128)(2,1)S(1)}, u32[]{:S(2)}, u32[]{:S(2)}) collective-permute-start(bf16[128,768]{1,0:T(8,128)(2,1)S(1)} %get-tuple-element.148), channel_id=1, source_target_pairs={{0,8},{1,9},{2,10},{3,11},{4,12},{5,13},{6,14},{7,15},{8,0},{9,1},... | collective-permute-start | bytes 589832 | tf_op jit(solution)/shard_map/ppermute | solution.py:366
  201.0 1.8 collective-permute-start.33
  202.8 7.1 %all-gather.2 = bf16[384,768]{1,0:T(8,128)(2,1)S(1)} all-gather(bf16[96,768]{1,0:T(8,128)(2,1)S(1)} %last_sum.5), channel_id=4, replica_groups=mesh['seq'=8,'rows'=4] {'rows'}, dimensions={0}, use_global_device_ids=true | all-gather | bytes 737280 | tf_op jit(solution)/shard_map/all_gather | solution.py:1083
  211.0 6.5 %collective-permute-done.32.third = bf16[128,768]{1,0:T(8,128)(2,1)S(1)} collective-permute-done((bf16[128,768]{1,0:T(8,128)(2,1)S(1)}, bf16[128,768]{1,0:T(8,128)(2,1)S(1)}, u32[]{:S(2)}, u32[]{:S(2)}) %collective-permute-start.32) | collective-permute-done | bytes 196640 | tf_op jit(solution)/shard_map/ppermute | solution.py:366
  217.6 8.2 %all-gather.1 = bf16[512,768]{1,0:T(8,128)(2,1)S(1)} all-gather(bf16[128,768]{1,0:T(8,128)(2,1)S(1)} %last_sum.4), channel_id=3, replica_groups=mesh['seq'=8,'rows'=4] {'rows'}, dimensions={0}, use_global_device_ids=true | all-gather | bytes 983040 | tf_op jit(solution)/shard_map/all_gather | solution.py:1083
  225.8 1.7 up_outputs.1
  (178 shorter events, 37.3 us)
Async XLA Ops:
  1.7 3.8 %collective-permute-start.1 = (bf16[128,768]{1,0:T(8,128)(2,1)S(1)}, bf16[128,768]{1,0:T(8,128)(2,1)S(1)}, u32[]{:S(2)}, u32[]{:S(2)}) collective-permute-start(bf16[128,768]{1,0:T(8,128)(2,1)S(1)} %get-tuple-element.182), channel_id=1, source_target_pairs={{0,0},{1,16},{2,2},{3,18},{4,4},{5,20},{6,6},{7,22},{8,8},{9,24},{... | collective-permute-start | bytes 589832 | tf_op jit(solution)/shard_map/ppermute | solution.py:366
  2.4 6.7 %collective-permute-start.2 = (bf16[128,768]{1,0:T(8,128)(2,1)S(1)}, bf16[128,768]{1,0:T(8,128)(2,1)S(1)}, u32[]{:S(2)}, u32[]{:S(2)}) collective-permute-start(bf16[128,768]{1,0:T(8,128)(2,1)S(1)} %get-tuple-element.181), channel_id=1, source_target_pairs={{0,8},{1,24},{2,10},{3,26},{4,12},{5,28},{6,14},{7,30},{8,0},{9,16... | collective-permute-start | bytes 589832 | tf_op jit(solution)/shard_map/ppermute | solution.py:366
  5.5 37.7 %copy-start.16 = (bf16[128,768]{1,0:T(8,128)(2,1)}, bf16[128,768]{1,0:T(8,128)(2,1)S(1)}, u32[]{:S(2)}) copy-start(bf16[128,768]{1,0:T(8,128)(2,1)S(1)} %collective-permute-done.1.refs_0_.x0.t0) | copy-start | bytes 589828
  5.5 13.2 %collective-permute-start.5 = (bf16[128,768]{1,0:T(8,128)(2,1)S(1)}, bf16[128,768]{1,0:T(8,128)(2,1)S(1)}, u32[]{:S(2)}, u32[]{:S(2)}) collective-permute-start(bf16[128,768]{1,0:T(8,128)(2,1)S(1)} %collective-permute-done.1.refs_0_.x0.t0), channel_id=1, source_target_pairs={{0,4},{1,5},{2,6},{3,7},{4,0},{5,1},{6,2},{7,3},{8,12},{9,13},{10,... | collective-permute-start | bytes 589832 | tf_op jit(solution)/shard_map/ppermute | solution.py:366
  9.2 34.0 %copy-start.18 = (bf16[128,768]{1,0:T(8,128)(2,1)}, bf16[128,768]{1,0:T(8,128)(2,1)S(1)}, u32[]{:S(2)}) copy-start(bf16[128,768]{1,0:T(8,128)(2,1)S(1)} %collective-permute-done.2.refs_1_.x1.t1) | copy-start | bytes 589828
  9.2 10.7 %collective-permute-start.6 = (bf16[128,768]{1,0:T(8,128)(2,1)S(1)}, bf16[128,768]{1,0:T(8,128)(2,1)S(1)}, u32[]{:S(2)}, u32[]{:S(2)}) collective-permute-start(bf16[128,768]{1,0:T(8,128)(2,1)S(1)} %collective-permute-done.2.refs_1_.x1.t1), channel_id=1, source_target_pairs={{0,4},{1,5},{2,6},{3,7},{4,0},{5,1},{6,2},{7,3},{8,12},{9,13},{10,... | collective-permute-start | bytes 589832 | tf_op jit(solution)/shard_map/ppermute | solution.py:366
  12.5 10.7 %collective-permute-start = (s32[2,16]{1,0:T(2,128)}, s32[2,16]{1,0:T(2,128)S(1)}, u32[]{:S(2)}, u32[]{:S(2)}) collective-permute-start(s32[2,16]{1,0:T(2,128)} %own_lengths.3), channel_id=1, source_target_pairs={{0,1},{1,0},{2,3},{3,2},{4,5},{5,4},{6,7},{7,6},{8,9},{9,8},{10,11... | collective-permute-start | bytes 392 | tf_op jit(solution)/shard_map/ppermute | solution.py:366
  18.2 5.6 %collective-permute-start.3 = (bf16[128,768]{1,0:T(8,128)(2,1)S(1)}, bf16[128,768]{1,0:T(8,128)(2,1)S(1)}, u32[]{:S(2)}, u32[]{:S(2)}) collective-permute-start(bf16[128,768]{1,0:T(8,128)(2,1)S(1)} %collective-permute-done.1.refs_0_.x0.t0), channel_id=1, source_target_pairs={{0,1},{1,0},{2,3},{3,2},{4,5},{5,4},{6,7},{7,6},{8,9},{9,8},{10,11... | collective-permute-start | bytes 589832 | tf_op jit(solution)/shard_map/ppermute | solution.py:366
  18.2 6.5 %collective-permute-start.4 = (bf16[128,768]{1,0:T(8,128)(2,1)S(1)}, bf16[128,768]{1,0:T(8,128)(2,1)S(1)}, u32[]{:S(2)}, u32[]{:S(2)}) collective-permute-start(bf16[128,768]{1,0:T(8,128)(2,1)S(1)} %collective-permute-done.2.refs_1_.x1.t1), channel_id=1, source_target_pairs={{0,1},{1,0},{2,3},{3,2},{4,5},{5,4},{6,7},{7,6},{8,9},{9,8},{10,11... | collective-permute-start | bytes 589832 | tf_op jit(solution)/shard_map/ppermute | solution.py:366
  18.7 6.0 %collective-permute-start.7 = (bf16[128,768]{1,0:T(8,128)(2,1)S(1)}, bf16[128,768]{1,0:T(8,128)(2,1)S(1)}, u32[]{:S(2)}, u32[]{:S(2)}) collective-permute-start(bf16[128,768]{1,0:T(8,128)(2,1)S(1)} %collective-permute-done.5.refs_4_.t4), channel_id=1, source_target_pairs={{0,1},{1,0},{2,3},{3,2},{4,5},{5,4},{6,7},{7,6},{8,9},{9,8},{10,11... | collective-permute-start | bytes 589832 | tf_op jit(solution)/shard_map/ppermute | solution.py:366
  19.9 4.8 %collective-permute-start.8 = (bf16[128,768]{1,0:T(8,128)(2,1)S(1)}, bf16[128,768]{1,0:T(8,128)(2,1)S(1)}, u32[]{:S(2)}, u32[]{:S(2)}) collective-permute-start(bf16[128,768]{1,0:T(8,128)(2,1)S(1)} %collective-permute-done.6.refs_5_.t5), channel_id=1, source_target_pairs={{0,1},{1,0},{2,3},{3,2},{4,5},{5,4},{6,7},{7,6},{8,9},{9,8},{10,11... | collective-permute-start | bytes 589832 | tf_op jit(solution)/shard_map/ppermute | solution.py:366
  23.1 19.1 %collective-permute-start.10 = (bf16[128,768]{1,0:T(8,128)(2,1)S(1)}, bf16[128,768]{1,0:T(8,128)(2,1)S(1)}, u32[]{:S(2)}, u32[]{:S(2)}) collective-permute-start(bf16[128,768]{1,0:T(8,128)(2,1)S(1)} %get-tuple-element.180), channel_id=1, source_target_pairs={{0,0},{1,16},{2,2},{3,18},{4,4},{5,20},{6,6},{7,22},{8,8},{9,24},{... | collective-permute-start | bytes 589832 | tf_op jit(solution)/shard_map/ppermute | solution.py:366
  23.8 18.4 %collective-permute-start.11 = (bf16[128,768]{1,0:T(8,128)(2,1)S(1)}, bf16[128,768]{1,0:T(8,128)(2,1)S(1)}, u32[]{:S(2)}, u32[]{:S(2)}) collective-permute-start(bf16[128,768]{1,0:T(8,128)(2,1)S(1)} %get-tuple-element.179), channel_id=1, source_target_pairs={{0,8},{1,24},{2,10},{3,26},{4,12},{5,28},{6,14},{7,30},{8,0},{9,16... | collective-permute-start | bytes 589832 | tf_op jit(solution)/shard_map/ppermute | solution.py:366
  36.8 6.4 %collective-permute-start.9 = (bf16[256,384]{1,0:T(8,128)(2,1)S(1)}, bf16[256,384]{1,0:T(8,128)(2,1)S(1)}, u32[]{:S(2)}, u32[]{:S(2)}) collective-permute-start(bf16[256,384]{1,0:T(8,128)(2,1)S(1)} %get-tuple-element.95.att1), channel_id=1, source_target_pairs={{0,1},{1,0},{2,3},{3,2},{4,5},{5,4},{6,7},{7,6},{8,9},{9,8},{10,11... | collective-permute-start | bytes 589832 | tf_op jit(solution)/shard_map/ppermute | solution.py:366
  64.1 56.6 %collective-permute-start.26 = (bf16[16,128,768]{2,1,0:T(8,128)(2,1)S(1)}, bf16[16,128,768]{2,1,0:T(8,128)(2,1)S(1)}, u32[]{:S(2)}, u32[]{:S(2)}) collective-permute-start(bf16[16,128,768]{2,1,0:T(8,128)(2,1)S(1)} %up_units.3), channel_id=1, source_target_pairs={{0,1},{1,0},{2,3},{3,2},{4,5},{5,4},{6,7},{7,6},{8,9},{9,8},{10,11... | collective-permute-start | bytes 9437192 | tf_op jit(solution)/shard_map/ppermute | solution.py:366
  69.5 43.8 %collective-permute-start.34 = (bf16[16,96,768]{2,1,0:T(8,128)(2,1)}, bf16[16,96,768]{2,1,0:T(8,128)(2,1)S(1)}, u32[]{:S(2)}, u32[]{:S(2)}) collective-permute-start(bf16[16,96,768]{2,1,0:T(8,128)(2,1)} %down_units.3), channel_id=1, source_target_pairs={{0,1},{1,0},{2,3},{3,2},{4,5},{5,4},{6,7},{7,6},{8,9},{9,8},{10,11... | collective-permute-start | bytes 7077896 | tf_op jit(solution)/shard_map/ppermute | solution.py:366
  69.6 4.4 %collective-permute-start.14 = (bf16[256,384]{1,0:T(8,128)(2,1)S(1)}, bf16[256,384]{1,0:T(8,128)(2,1)S(1)}, u32[]{:S(2)}, u32[]{:S(2)}) collective-permute-start(bf16[256,384]{1,0:T(8,128)(2,1)S(1)} %get-tuple-element.109), channel_id=1, source_target_pairs={{0,1},{1,0},{2,3},{3,2},{4,5},{5,4},{6,7},{7,6},{8,9},{9,8},{10,11... | collective-permute-start | bytes 589832 | tf_op jit(solution)/shard_map/ppermute | solution.py:366
  86.2 19.1 %copy-start.37 = (bf16[128,768]{1,0:T(8,128)(2,1)S(1)}, bf16[128,768]{1,0:T(8,128)(2,1)}, u32[]{:S(2)}) copy-start(bf16[128,768]{1,0:T(8,128)(2,1)} %copy-done.36) | copy-start | bytes 589828
  86.2 20.3 %copy-start.31 = (bf16[128,768]{1,0:T(8,128)(2,1)S(1)}, bf16[128,768]{1,0:T(8,128)(2,1)}, u32[]{:S(2)}) copy-start(bf16[128,768]{1,0:T(8,128)(2,1)} %copy-done.30) | copy-start | bytes 589828
  86.3 25.0 %collective-permute-start.15 = (bf16[512,768]{1,0:T(8,128)(2,1)S(1)}, bf16[512,768]{1,0:T(8,128)(2,1)S(1)}, u32[]{:S(2)}, u32[]{:S(2)}) collective-permute-start(bf16[512,768]{1,0:T(8,128)(2,1)S(1)} %get-tuple-element.114), channel_id=1, source_target_pairs={{0,1},{1,0},{2,3},{3,2},{4,5},{5,4},{6,7},{7,6},{8,9},{9,8},{10,11... | collective-permute-start | bytes 2359304 | tf_op jit(solution)/shard_map/ppermute | solution.py:366
  92.0 13.3 %collective-permute-start.19 = (bf16[4,2,80,384]{3,2,1,0:T(8,128)(2,1)S(1)}, bf16[4,2,80,384]{3,2,1,0:T(8,128)(2,1)S(1)}, u32[]{:S(2)}, u32[]{:S(2)}) collective-permute-start(bf16[4,2,80,384]{3,2,1,0:T(8,128)(2,1)S(1)} %get-tuple-element.119), channel_id=1, source_target_pairs={{0,2},{1,3},{2,0},{3,1},{4,6},{5,7},{6,4},{7,5},{8,10},{9,11},{10,... | collective-permute-start | bytes 1474568 | tf_op jit(solution)/shard_map/ppermute | solution.py:366
  93.6 13.0 %collective-permute-start.20 = (bf16[4,2,80,384]{3,2,1,0:T(8,128)(2,1)S(1)}, bf16[4,2,80,384]{3,2,1,0:T(8,128)(2,1)S(1)}, u32[]{:S(2)}, u32[]{:S(2)}) collective-permute-start(bf16[4,2,80,384]{3,2,1,0:T(8,128)(2,1)S(1)} %get-tuple-element.121), channel_id=1, source_target_pairs={{0,4},{1,5},{2,6},{3,7},{4,0},{5,1},{6,2},{7,3},{8,12},{9,13},{10,... | collective-permute-start | bytes 1474568 | tf_op jit(solution)/shard_map/ppermute | solution.py:366
  105.3 4.4 %collective-permute-start.12 = (bf16[128,768]{1,0:T(8,128)(2,1)S(1)}, bf16[128,768]{1,0:T(8,128)(2,1)S(1)}, u32[]{:S(2)}, u32[]{:S(2)}) collective-permute-start(bf16[128,768]{1,0:T(8,128)(2,1)S(1)} %copy-done.37), channel_id=1, source_target_pairs={{0,0},{1,16},{2,2},{3,18},{4,4},{5,20},{6,6},{7,22},{8,8},{9,24},{... | collective-permute-start | bytes 589832 | tf_op jit(solution)/shard_map/ppermute | solution.py:366
  106.6 13.2 %collective-permute-start.13 = (bf16[128,768]{1,0:T(8,128)(2,1)S(1)}, bf16[128,768]{1,0:T(8,128)(2,1)S(1)}, u32[]{:S(2)}, u32[]{:S(2)}) collective-permute-start(bf16[128,768]{1,0:T(8,128)(2,1)S(1)} %copy-done.31), channel_id=1, source_target_pairs={{0,8},{1,24},{2,10},{3,26},{4,12},{5,28},{6,14},{7,30},{8,0},{9,16... | collective-permute-start | bytes 589832 | tf_op jit(solution)/shard_map/ppermute | solution.py:366
  109.8 19.2 %collective-permute-start.21 = (bf16[4,80,384]{2,1,0:T(8,128)(2,1)S(1)}, bf16[4,80,384]{2,1,0:T(8,128)(2,1)S(1)}, u32[]{:S(2)}, u32[]{:S(2)}) collective-permute-start(bf16[4,80,384]{2,1,0:T(8,128)(2,1)S(1)} %get-tuple-element.123), channel_id=1, source_target_pairs={{0,4},{1,5},{2,6},{3,7},{4,0},{5,1},{6,2},{7,3},{8,12},{9,13},{10,... | collective-permute-start | bytes 737288 | tf_op jit(solution)/shard_map/ppermute | solution.py:366
  111.3 19.4 %collective-permute-start.22 = (bf16[4,80,384]{2,1,0:T(8,128)(2,1)}, bf16[4,80,384]{2,1,0:T(8,128)(2,1)}, u32[]{:S(2)}, u32[]{:S(2)}) collective-permute-start(bf16[4,80,384]{2,1,0:T(8,128)(2,1)} %get-tuple-element.125), channel_id=1, source_target_pairs={{0,2},{1,3},{2,0},{3,1},{4,6},{5,7},{6,4},{7,5},{8,10},{9,11},{10,... | collective-permute-start | bytes 737288 | tf_op jit(solution)/shard_map/ppermute | solution.py:366
  113.2 22.6 %collective-permute-start.16 = (bf16[256,768]{1,0:T(8,128)(2,1)}, bf16[256,768]{1,0:T(8,128)(2,1)}, u32[]{:S(2)}, u32[]{:S(2)}) collective-permute-start(bf16[256,768]{1,0:T(8,128)(2,1)} %get-tuple-element.117), channel_id=1, source_target_pairs={{0,4},{1,5},{2,6},{3,7},{4,0},{5,1},{6,2},{7,3},{8,12},{9,13},{10,... | collective-permute-start | bytes 1179656 | tf_op jit(solution)/shard_map/ppermute | solution.py:366
  119.7 18.6 %collective-permute-start.35 = (bf16[4,2,48,768]{3,2,1,0:T(8,128)(2,1)}, bf16[4,2,48,768]{3,2,1,0:T(8,128)(2,1)}, u32[]{:S(2)}, u32[]{:S(2)}) collective-permute-start(bf16[4,2,48,768]{3,2,1,0:T(8,128)(2,1)} %get-tuple-element.159), channel_id=1, source_target_pairs={{0,2},{1,3},{2,0},{3,1},{4,6},{5,7},{6,4},{7,5},{8,10},{9,11},{10,... | collective-permute-start | bytes 1769480 | tf_op jit(solution)/shard_map/ppermute | solution.py:366
  120.7 27.9 %collective-permute-start.36 = (bf16[4,2,48,768]{3,2,1,0:T(8,128)(2,1)}, bf16[4,2,48,768]{3,2,1,0:T(8,128)(2,1)}, u32[]{:S(2)}, u32[]{:S(2)}) collective-permute-start(bf16[4,2,48,768]{3,2,1,0:T(8,128)(2,1)} %get-tuple-element.161), channel_id=1, source_target_pairs={{0,4},{1,5},{2,6},{3,7},{4,0},{5,1},{6,2},{7,3},{8,12},{9,13},{10,... | collective-permute-start | bytes 1769480 | tf_op jit(solution)/shard_map/ppermute | solution.py:366
  129.7 28.1 %collective-permute-start.27 = (bf16[4,2,64,768]{3,2,1,0:T(8,128)(2,1)}, bf16[4,2,64,768]{3,2,1,0:T(8,128)(2,1)S(1)}, u32[]{:S(2)}, u32[]{:S(2)}) collective-permute-start(bf16[4,2,64,768]{3,2,1,0:T(8,128)(2,1)} %get-tuple-element.140), channel_id=1, source_target_pairs={{0,2},{1,3},{2,0},{3,1},{4,6},{5,7},{6,4},{7,5},{8,10},{9,11},{10,... | collective-permute-start | bytes 2359304 | tf_op jit(solution)/shard_map/ppermute | solution.py:366
  130.7 19.4 %copy-start.7 = (bf16[4,2,48,768]{3,2,1,0:T(8,128)(2,1)S(1)}, bf16[4,2,48,768]{3,2,1,0:T(8,128)(2,1)}, u32[]{:S(2)}) copy-start(bf16[4,2,48,768]{3,2,1,0:T(8,128)(2,1)} %copy-done.6) | copy-start | bytes 1769476
  130.7 19.4 %copy-start.9 = (bf16[4,2,48,768]{3,2,1,0:T(8,128)(2,1)S(1)}, bf16[4,2,48,768]{3,2,1,0:T(8,128)(2,1)}, u32[]{:S(2)}) copy-start(bf16[4,2,48,768]{3,2,1,0:T(8,128)(2,1)} %copy-done.8) | copy-start | bytes 1769476
  130.7 28.5 %collective-permute-start.28 = (bf16[4,2,64,768]{3,2,1,0:T(8,128)(2,1)}, bf16[4,2,64,768]{3,2,1,0:T(8,128)(2,1)S(1)}, u32[]{:S(2)}, u32[]{:S(2)}) collective-permute-start(bf16[4,2,64,768]{3,2,1,0:T(8,128)(2,1)} %copy-done.21), channel_id=1, source_target_pairs={{0,4},{1,5},{2,6},{3,7},{4,0},{5,1},{6,2},{7,3},{8,12},{9,13},{10,... | collective-permute-start | bytes 2359304 | tf_op jit(solution)/shard_map/ppermute | solution.py:366
  135.8 17.1 %collective-permute-start.23 = (bf16[160,384]{1,0:T(8,128)(2,1)S(1)}, bf16[160,384]{1,0:T(8,128)(2,1)S(1)}, u32[]{:S(2)}, u32[]{:S(2)}) collective-permute-start(bf16[160,384]{1,0:T(8,128)(2,1)S(1)} %get-tuple-element.127), channel_id=1, source_target_pairs={{0,8},{1,9},{2,10},{3,11},{4,12},{5,13},{6,14},{7,15},{8,0},{9,1},... | collective-permute-start | bytes 368648 | tf_op jit(solution)/shard_map/ppermute | solution.py:366
  138.4 17.5 %collective-permute-start.24 = (bf16[160,384]{1,0:T(8,128)(2,1)S(1)}, bf16[160,384]{1,0:T(8,128)(2,1)S(1)}, u32[]{:S(2)}, u32[]{:S(2)}) collective-permute-start(bf16[160,384]{1,0:T(8,128)(2,1)S(1)} %get-tuple-element.128), channel_id=1, source_target_pairs={{0,16},{1,17},{2,18},{3,19},{4,20},{5,21},{6,22},{7,23},{8,24},{9,... | collective-permute-start | bytes 368648 | tf_op jit(solution)/shard_map/ppermute | solution.py:366
  148.6 8.0 %collective-permute-start.25 = (bf16[160,384]{1,0:T(8,128)(2,1)S(1)}, bf16[160,384]{1,0:T(8,128)(2,1)S(1)}, u32[]{:S(2)}, u32[]{:S(2)}) collective-permute-start(bf16[160,384]{1,0:T(8,128)(2,1)S(1)} %get-tuple-element.129), channel_id=1, source_target_pairs={{0,24},{1,25},{2,26},{3,27},{4,28},{5,29},{6,30},{7,31},{8,16},{9,... | collective-permute-start | bytes 368648 | tf_op jit(solution)/shard_map/ppermute | solution.py:366
  152.9 10.0 %collective-permute-start.37 = (bf16[4,48,768]{2,1,0:T(8,128)(2,1)S(1)}, bf16[4,48,768]{2,1,0:T(8,128)(2,1)S(1)}, u32[]{:S(2)}, u32[]{:S(2)}) collective-permute-start(bf16[4,48,768]{2,1,0:T(8,128)(2,1)S(1)} %get-tuple-element.163), channel_id=1, source_target_pairs={{0,4},{1,5},{2,6},{3,7},{4,0},{5,1},{6,2},{7,3},{8,12},{9,13},{10,... | collective-permute-start | bytes 884744 | tf_op jit(solution)/shard_map/ppermute | solution.py:366
  155.9 26.7 %collective-permute-start.17 = (bf16[128,768]{1,0:T(8,128)(2,1)S(1)}, bf16[128,768]{1,0:T(8,128)(2,1)S(1)}, u32[]{:S(2)}, u32[]{:S(2)}) collective-permute-start(bf16[128,768]{1,0:T(8,128)(2,1)S(1)} %get-tuple-element.175), channel_id=1, source_target_pairs={{0,0},{1,16},{2,2},{3,18},{4,4},{5,20},{6,6},{7,22},{8,8},{9,24},{... | collective-permute-start | bytes 589832 | tf_op jit(solution)/shard_map/ppermute | solution.py:366
  156.6 28.3 %collective-permute-start.18 = (bf16[128,768]{1,0:T(8,128)(2,1)S(1)}, bf16[128,768]{1,0:T(8,128)(2,1)S(1)}, u32[]{:S(2)}, u32[]{:S(2)}) collective-permute-start(bf16[128,768]{1,0:T(8,128)(2,1)S(1)} %get-tuple-element.176), channel_id=1, source_target_pairs={{0,8},{1,24},{2,10},{3,26},{4,12},{5,28},{6,14},{7,30},{8,0},{9,16... | collective-permute-start | bytes 589832 | tf_op jit(solution)/shard_map/ppermute | solution.py:366
  157.8 23.0 %collective-permute-start.38 = (bf16[4,48,768]{2,1,0:T(8,128)(2,1)S(1)}, bf16[4,48,768]{2,1,0:T(8,128)(2,1)S(1)}, u32[]{:S(2)}, u32[]{:S(2)}) collective-permute-start(bf16[4,48,768]{2,1,0:T(8,128)(2,1)S(1)} %get-tuple-element.165), channel_id=1, source_target_pairs={{0,2},{1,3},{2,0},{3,1},{4,6},{5,7},{6,4},{7,5},{8,10},{9,11},{10,... | collective-permute-start | bytes 884744 | tf_op jit(solution)/shard_map/ppermute | solution.py:366
  160.2 36.5 %collective-permute-start.29 = (bf16[4,64,768]{2,1,0:T(8,128)(2,1)S(1)}, bf16[4,64,768]{2,1,0:T(8,128)(2,1)S(1)}, u32[]{:S(2)}, u32[]{:S(2)}) collective-permute-start(bf16[4,64,768]{2,1,0:T(8,128)(2,1)S(1)} %get-tuple-element.144), channel_id=1, source_target_pairs={{0,4},{1,5},{2,6},{3,7},{4,0},{5,1},{6,2},{7,3},{8,12},{9,13},{10,... | collective-permute-start | bytes 1179656 | tf_op jit(solution)/shard_map/ppermute | solution.py:366
  162.9 33.8 %collective-permute-start.30 = (bf16[4,64,768]{2,1,0:T(8,128)(2,1)S(1)}, bf16[4,64,768]{2,1,0:T(8,128)(2,1)S(1)}, u32[]{:S(2)}, u32[]{:S(2)}) collective-permute-start(bf16[4,64,768]{2,1,0:T(8,128)(2,1)S(1)} %get-tuple-element.146), channel_id=1, source_target_pairs={{0,2},{1,3},{2,0},{3,1},{4,6},{5,7},{6,4},{7,5},{8,10},{9,11},{10,... | collective-permute-start | bytes 1179656 | tf_op jit(solution)/shard_map/ppermute | solution.py:366
  181.5 8.6 %collective-permute-start.39 = (bf16[96,768]{1,0:T(8,128)(2,1)S(1)}, bf16[96,768]{1,0:T(8,128)(2,1)S(1)}, u32[]{:S(2)}, u32[]{:S(2)}) collective-permute-start(bf16[96,768]{1,0:T(8,128)(2,1)S(1)} %get-tuple-element.167), channel_id=1, source_target_pairs={{0,8},{1,9},{2,10},{3,11},{4,12},{5,13},{6,14},{7,15},{8,0},{9,1},... | collective-permute-start | bytes 442376 | tf_op jit(solution)/shard_map/ppermute | solution.py:366
  182.6 14.0 %collective-permute-start.40 = (bf16[96,768]{1,0:T(8,128)(2,1)S(1)}, bf16[96,768]{1,0:T(8,128)(2,1)S(1)}, u32[]{:S(2)}, u32[]{:S(2)}) collective-permute-start(bf16[96,768]{1,0:T(8,128)(2,1)S(1)} %get-tuple-element.168), channel_id=1, source_target_pairs={{0,16},{1,17},{2,18},{3,19},{4,20},{5,21},{6,22},{7,23},{8,24},{9,... | collective-permute-start | bytes 442376 | tf_op jit(solution)/shard_map/ppermute | solution.py:366
  184.9 11.7 %collective-permute-start.41 = (bf16[96,768]{1,0:T(8,128)(2,1)S(1)}, bf16[96,768]{1,0:T(8,128)(2,1)S(1)}, u32[]{:S(2)}, u32[]{:S(2)}) collective-permute-start(bf16[96,768]{1,0:T(8,128)(2,1)S(1)} %get-tuple-element.169), channel_id=1, source_target_pairs={{0,24},{1,25},{2,26},{3,27},{4,28},{5,29},{6,30},{7,31},{8,16},{9,... | collective-permute-start | bytes 442376 | tf_op jit(solution)/shard_map/ppermute | solution.py:366
  197.4 13.6 %collective-permute-start.31 = (bf16[128,768]{1,0:T(8,128)(2,1)S(1)}, bf16[128,768]{1,0:T(8,128)(2,1)S(1)}, u32[]{:S(2)}, u32[]{:S(2)}) collective-permute-start(bf16[128,768]{1,0:T(8,128)(2,1)S(1)} %get-tuple-element.148), channel_id=1, source_target_pairs={{0,8},{1,9},{2,10},{3,11},{4,12},{5,13},{6,14},{7,15},{8,0},{9,1},... | collective-permute-start | bytes 589832 | tf_op jit(solution)/shard_map/ppermute | solution.py:366
  200.3 17.2 %collective-permute-start.32 = (bf16[128,768]{1,0:T(8,128)(2,1)S(1)}, bf16[128,768]{1,0:T(8,128)(2,1)S(1)}, u32[]{:S(2)}, u32[]{:S(2)}) collective-permute-start(bf16[128,768]{1,0:T(8,128)(2,1)S(1)} %get-tuple-element.149), channel_id=1, source_target_pairs={{0,16},{1,17},{2,18},{3,19},{4,20},{5,21},{6,22},{7,23},{8,24},{9,... | collective-permute-start | bytes 589832 | tf_op jit(solution)/shard_map/ppermute | solution.py:366
  201.0 16.5 %collective-permute-start.33 = (bf16[128,768]{1,0:T(8,128)(2,1)S(1)}, bf16[128,768]{1,0:T(8,128)(2,1)S(1)}, u32[]{:S(2)}, u32[]{:S(2)}) collective-permute-start(bf16[128,768]{1,0:T(8,128)(2,1)S(1)} %get-tuple-element.150), channel_id=1, source_target_pairs={{0,24},{1,25},{2,26},{3,27},{4,28},{5,29},{6,30},{7,31},{8,16},{9,... | collective-permute-start | bytes 589832 | tf_op jit(solution)/shard_map/ppermute | solution.py:366
  (42 other events, 316.1 us)

commit v2 on v0

--- a/solution.py
+++ b/solution.py
@@ -1,8 +1,11 @@
+import functools
 import math
 
 import jax
 import jax.numpy as jnp
 from jax import lax
+from jax.experimental import pallas as pl
+from jax.experimental.pallas import tpu as pltpu
 from jax.sharding import PartitionSpec as P
 
 HEADS = 12
@@ -97,7 +100,7 @@
     )
 
 
-def body(
+def general_body(
     tokens,
     pair_lengths,
     joint_weight,
@@ -310,6 +313,1051 @@
     return (outputs, token_grad.reshape(tokens.shape)) + tuple(shares)
 
 
+WIDTH = HEADS * HEAD_DIM
+HALF = WIDTH // 2
+FF = 4 * WIDTH
+BLOCK = 128
+OWN = 2 * BLOCK
+LANES = 128
+PAIRS_OF_HEADS = HALF // LANES
+JOINT_ROWS = 80
+JOINT_FIRST = 48
+JOINT_SECOND = JOINT_ROWS - JOINT_FIRST
+UP_ROWS = 128
+DOWN_ROWS = 96
+EXT = OWN + 16
+FLOAT = jnp.float32
+LOW = jnp.bfloat16
+AXES = ("seq", "rows")
+
+
+def kernel_params(megabytes):
+    return pltpu.CompilerParams(vmem_limit_bytes=megabytes << 20)
+
+
+def shaped(shape, kind):
+    return jax.ShapeDtypeStruct(shape, kind)
+
+
+def whole(shape):
+    return pl.BlockSpec(shape, lambda *_: (0,) * len(shape))
+
+
+def cost(flops, moved, exps=0):
+    return pl.CostEstimate(flops=1024, bytes_accessed=1024, transcendentals=0)
+
+
+def dot(left, right):
+    return lax.dot_general(left, right, (((1,), (0,)), ((), ())), preferred_element_type=FLOAT)
+
+
+def dot_nt(left, right):
+    return lax.dot_general(left, right, (((1,), (1,)), ((), ())), preferred_element_type=FLOAT)
+
+
+def call(kernel, name, place, inputs, outputs, scratch=(), grid=(1,), scalars=(), after=(), megabytes=40, work=None):
+    prefetch = 1 + len(scalars)
+    given, made = len(inputs), len(outputs)
+
+    def ordered(*refs):
+        first = prefetch + given
+        mark = refs[first + len(after) + made]
+        mark[...] = jnp.zeros_like(mark)
+        kernel(*refs[:first], *refs[first + len(after) : first + len(after) + made], *refs[first + len(after) + made + 1 :])
+
+    results = pl.pallas_call(
+        ordered,
+        grid_spec=pltpu.PrefetchScalarGridSpec(
+            num_scalar_prefetch=prefetch,
+            grid=grid,
+            in_specs=[spec for _, spec in inputs] + [pl.BlockSpec(memory_space=pl.ANY)] * len(after),
+            out_specs=[spec for _, _, spec in outputs] + [whole((8, LANES))],
+            scratch_shapes=list(scratch),
+        ),
+        out_shape=[shaped(shape, kind) for shape, kind, _ in outputs] + [shaped((8, LANES), FLOAT)],
+        compiler_params=kernel_params(megabytes),
+        cost_estimate=work,
+        name=name,
+    )(place, *scalars, *[array for array, _ in inputs], *after)
+    return results[:-1], results[-1]
+
+
+def plain(array):
+    return array, whole(array.shape)
+
+
+def made(shape, kind):
+    return shape, kind, whole(shape)
+
+
+def device_at(z, y, x, c):
+    return ((z * 2 + y) * 2 + x) * 2 + c
+
+
+def permute(value, target):
+    pairs = []
+    for z in range(4):
+        for y in range(2):
+            for x in range(2):
+                for c in range(2):
+                    pairs.append((device_at(z, y, x, c), device_at(*target(z, y, x, c))))
+    return lax.ppermute(value, AXES, pairs)
+
+
+def core_swap(value):
+    return permute(value, lambda z, y, x, c: (z, y, x, 1 - c))
+
+
+def x_swap(value):
+    return permute(value, lambda z, y, x, c: (z, y, 1 - x, c))
+
+
+def y_swap(value):
+    return permute(value, lambda z, y, x, c: (z, 1 - y, x, c))
+
+
+def z_swap(value, bits):
+    return permute(value, lambda z, y, x, c: (z ^ bits, y, x, c))
+
+
+def row_swap(value, second):
+    return permute(value, lambda z, y, x, c: (2 * c + (z % 2 ^ second), y, x, z // 2))
+
+
+def first_positions(place):
+    z, y, c = place[0], place[1], place[3]
+    bases = []
+    for core, line in ((c, y), (1 - c, y), (c, 1 - y), (1 - c, 1 - y)):
+        for second in (0, 1):
+            parity = z % 2
+            parity = 1 - parity if second else parity
+            bases.append((2 * (2 * core + parity) + line) * BLOCK)
+    return bases
+
+
+def pair_ends(place, own_lengths, peer_lengths):
+    z, c = place[0], place[3]
+    here = (z // 2) == c
+    line = z % 2
+    ends, end = [], 0
+    for pair in range(own_lengths.shape[1]):
+        end = end + jnp.where(here, own_lengths[line, pair], peer_lengths[line, pair])
+        ends.append(end)
+    return ends
+
+
+def pairs_along(base, ends, axis):
+    shape = (8, BLOCK) if axis == 1 else (BLOCK, LANES)
+    position = base + lax.broadcasted_iota(jnp.int32, shape, axis)
+    ids = jnp.zeros(shape, jnp.int32)
+    for end in ends:
+        ids = ids + (position >= end).astype(jnp.int32)
+    return ids
+
+
+def head_mask(rows):
+    return lax.broadcasted_iota(jnp.int32, (rows, LANES), 1) < HEAD_DIM
+
+
+def attention_kernel(
+    place, own_lengths, peer_lengths, *refs
+):
+    blocks = refs[:8]
+    wq, wk, wv, qb, vb = refs[8:13]
+    att_out, q_out, k_out, v_out, log_out = refs[13:18]
+    bias, log_columns = refs[18:]
+    bases = first_positions(place)
+    ends = pair_ends(place, own_lengths, peer_lengths)
+    here = jnp.concatenate([block[...] for block in blocks[:4]], axis=0)
+    there = jnp.concatenate([block[...] for block in blocks[4:]], axis=0)
+    queries = dot(here, wq[...]) + qb[...]
+    q_out[...] = (queries.astype(LOW).astype(FLOAT) * HEAD_DIM**-0.5).astype(LOW)
+    for index, tokens in enumerate((here, there)):
+        rows = pl.ds(index * 512, 512)
+        k_out[rows, :] = dot(tokens, wk[...]).astype(LOW)
+        v_out[rows, :] = (dot(tokens, wv[...]) + vb[...]).astype(LOW)
+    key_ids = [pairs_along(base, ends, 1)[0:1] for base in bases]
+    for i in range(4):
+        query_ids = pairs_along(bases[i], ends, 0)
+        for j in range(8):
+            bias[pl.ds(i * BLOCK, BLOCK), pl.ds(j * BLOCK, BLOCK)] = jnp.where(
+                query_ids == key_ids[j], 0.0, NEGATIVE
+            )
+    log_columns[...] = jnp.zeros_like(log_columns)
+    for pair in range(PAIRS_OF_HEADS):
+        lanes = pl.ds(pair * LANES, LANES)
+        keys = k_out[:, lanes]
+        values = v_out[:, lanes]
+        ones = jnp.ones_like(values)
+        left_keys = head_mask(1024)
+        values_of = (jnp.where(left_keys, values, ones), jnp.where(left_keys, ones, values))
+        left = head_mask(OWN)
+        for part in range(2):
+            rows = pl.ds(part * OWN, OWN)
+            queries = q_out[rows, lanes]
+            zeros = jnp.zeros_like(queries)
+            summed = []
+            for half in range(2):
+                chosen = jnp.where(left, queries, zeros) if half == 0 else jnp.where(left, zeros, queries)
+                scores = dot_nt(chosen, keys) + bias[rows, :]
+                highest = jnp.max(scores, axis=1, keepdims=True)
+                weights = jnp.exp(scores - highest).astype(LOW)
+                total = dot(weights, values_of[half])
+                turned = pltpu.roll(total, HEAD_DIM, 1)
+                summed.append(total / turned)
+                sums = total if half == 1 else turned
+                log_total = highest + jnp.log(sums)
+                column = lax.broadcasted_iota(jnp.int32, (OWN, LANES), 1) == pair * 2 + half
+                at = log_total if pair * 2 + half < HEAD_DIM else None
+                log_columns[rows, :] = jnp.where(column, at, log_columns[rows, :])
+            attended = jnp.where(left, summed[0], summed[1]).astype(LOW)
+            att_out[rows, lanes] = attended
+    log_out[...] = jnp.transpose(log_columns[...])[0:8, :]
+
+
+def attention(place, lengths, blocks, joint_weight, query_bias, value_bias, after=()):
+    def columns(kind):
+        return joint_weight, pl.BlockSpec((WIDTH, HALF), lambda i, place, *_: (0, 2 * kind + place[3]))
+
+    half_row = pl.BlockSpec((1, HALF), lambda i, place, *_: (0, place[3]))
+    return call(
+        attention_kernel,
+        "attention",
+        place,
+        [plain(block) for block in blocks]
+        + [columns(0), columns(1), columns(2), (row_of(query_bias), half_row), (row_of(value_bias), half_row)],
+        [
+            made((512, HALF), LOW), made((512, HALF), LOW), made((1024, HALF), LOW), made((1024, HALF), LOW),
+            made((8, 512), FLOAT),
+        ],
+        scratch=[pltpu.VMEM((512, 1024), FLOAT), pltpu.VMEM((512, LANES), FLOAT)],
+        scalars=lengths,
+        after=after,
+        work=cost(4e9, 8e6, 3e6),
+    )
+
+
+def centred_norm(value):
+    mean = jnp.mean(value, axis=-1, keepdims=True)
+    centred = value - mean
+    spread = jnp.mean(centred * centred, axis=-1, keepdims=True)
+    inverse = lax.rsqrt(spread + EPSILON)
+    return centred * inverse, inverse
+
+
+def norm_back(grad, unit, inverse):
+    mean = jnp.mean(grad, axis=-1, keepdims=True)
+    along = jnp.mean(grad * unit, axis=-1, keepdims=True)
+    return (grad - mean - unit * along) * inverse
+
+
+def column_sum(value):
+    return jnp.sum(value, axis=0, keepdims=True)
+
+
+def forward_kernel(
+    place, att, att_got, wo_own, wo_other, out_bias, x0, x1, gain1, shift1, up, up_bias, down,
+    down_bias, gain2, shift2, cot0, cot1,
+    result0, result1, feed_ext, second_grad, act_keep, act_send, slope, unit1, inverse1, normed_low, normed_t, att_t, sums,
+    normed, feed, act_t,
+):
+    step = pl.program_id(0)
+    c = place[3]
+
+    @pl.when(step == 0)
+    def _():
+        tokens = jnp.concatenate([x0[...], x1[...]], axis=0).astype(FLOAT)
+        att_own, att_other = att[0:OWN], att_got[OWN:]
+        branch = dot(att_own, wo_own[...]) + dot(att_other, wo_other[...]) + out_bias[...]
+        unit, inverse = centred_norm(tokens + branch)
+        unit1[...] = unit
+        inverse1[...] = jnp.broadcast_to(inverse, (OWN, LANES))
+        value = unit * gain1[...] + shift1[...]
+        normed[...] = value
+        normed_low[...] = value.astype(LOW)
+        normed_t[...] = jnp.transpose(value).astype(LOW)
+        mine = pl.ds(pl.multiple_of(c * HALF, HALF), HALF)
+        other = pl.ds(pl.multiple_of((1 - c) * HALF, HALF), HALF)
+        att_t[mine, :] = jnp.transpose(att[...].astype(FLOAT)).astype(LOW)
+        att_t[other, 0:OWN] = jnp.transpose(att_other.astype(FLOAT)).astype(LOW)
+        att_t[other, OWN:] = jnp.transpose(att_got[0:OWN].astype(FLOAT)).astype(LOW)
+        feed[...] = jnp.zeros_like(feed)
+
+    inner = dot(normed_low[...], up[...]) + up_bias[...]
+    below = 0.5 + 0.5 * lax.erf(inner * math.sqrt(0.5))
+    density = jnp.exp(inner * inner * -0.5) * (1.0 / math.sqrt(2.0 * math.pi))
+    activated = inner * below
+    slope[...] = (below + inner * density).astype(LOW)
+    low = activated.astype(LOW)
+    act_t[...] = jnp.transpose(activated).astype(LOW).reshape(4, 2, DOWN_ROWS, OWN)
+    act_keep[...] = act_t[:, c]
+    act_send[...] = act_t[:, 1 - c]
+    feed[...] += dot(low, down[...])
+
+    @pl.when(step == pl.num_programs(0) - 1)
+    def _():
+        unit, inverse = centred_norm(normed[...] + feed[...] + down_bias[...])
+        result = (unit * gain2[...] + shift2[...]).astype(LOW)
+        result0[...] = result[0:BLOCK]
+        result1[...] = result[BLOCK:]
+        cotangent = jnp.concatenate([cot0[...], cot1[...]], axis=0).astype(FLOAT)
+        grad = norm_back(cotangent * gain2[...], unit, inverse)
+        second_grad[...] = grad
+        low_grad = grad.astype(LOW)
+        rows = jnp.concatenate(
+            [
+                column_sum(cotangent * unit),
+                column_sum(cotangent),
+                column_sum(low_grad.astype(FLOAT)),
+                jnp.zeros((5, WIDTH), FLOAT),
+            ],
+            axis=0,
+        )
+        sums[...] = rows
+        feed_ext[0:OWN] = low_grad
+        feed_ext[OWN:] = jnp.concatenate([rows, jnp.zeros_like(rows)], axis=0).astype(LOW)
+
+
+def row_of(vector):
+    return vector.reshape(1, vector.shape[0])
+
+
+def forward(place, att, att_got, tokens, cotangents, weights, after=()):
+    chunk = WIDTH
+
+    def vector(name):
+        return plain(row_of(weights[name]))
+
+    units = ((16, DOWN_ROWS, OWN), LOW, pl.BlockSpec((4, DOWN_ROWS, OWN), lambda i, place: (i, 0, 0)))
+    return call(
+        forward_kernel,
+        "forward",
+        place,
+        [
+            plain(att),
+            plain(att_got),
+            (weights["out"], pl.BlockSpec((HALF, WIDTH), lambda i, place: (place[3], 0))),
+            (weights["out"], pl.BlockSpec((HALF, WIDTH), lambda i, place: (1 - place[3], 0))),
+            vector("out_bias"), plain(tokens[0]), plain(tokens[1]), vector("gain1"), vector("shift1"),
+            (weights["up"], pl.BlockSpec((WIDTH, chunk), lambda i, place: (0, i))),
+            (row_of(weights["up_bias"]), pl.BlockSpec((1, chunk), lambda i, place: (0, i))),
+            (weights["down"], pl.BlockSpec((chunk, WIDTH), lambda i, place: (i, 0))),
+            vector("down_bias"), vector("gain2"), vector("shift2"), plain(cotangents[0]), plain(cotangents[1]),
+        ],
+        [
+            made((BLOCK, WIDTH), LOW), made((BLOCK, WIDTH), LOW), made((EXT, WIDTH), LOW),
+            made((OWN, WIDTH), FLOAT), units, units,
+            ((OWN, FF), LOW, pl.BlockSpec((OWN, chunk), lambda i, place: (0, i))),
+            made((OWN, WIDTH), FLOAT), made((OWN, LANES), FLOAT), made((OWN, WIDTH), LOW),
+            made((WIDTH, OWN), LOW), made((WIDTH, 512), LOW), made((8, WIDTH), FLOAT),
+        ],
+        scratch=[
+            pltpu.VMEM((OWN, WIDTH), FLOAT),
+            pltpu.VMEM((OWN, WIDTH), FLOAT),
+            pltpu.VMEM((4, 2, DOWN_ROWS, OWN), LOW),
+        ],
+        grid=(FF // chunk,),
+        after=after,
+        work=cost(2.7e9, 20e6, 2e6),
+    )
+
+
+def split_units(place, units, px_send, px, qy_send, qy):
+    y, x = place[1], place[2]
+    half = units.shape[2] // 2
+    for line in range(2):
+        px[0, line] = units[line, x, 0:half]
+        px_send[0, line] = units[line, 1 - x, 0:half]
+    for side in range(2):
+        qy[0, side] = units[y, side, half:]
+        qy_send[0, side] = units[1 - y, side, half:]
+
+
+def unit_outputs(rows, width):
+    shape = (4, 2, rows // 2, width)
+    return [(shape, LOW, pl.BlockSpec((1,) + shape[1:], lambda i, place: (i, 0, 0, 0)))] * 4
+
+
+def down_kernel(place, act, act_got, feed, feed_got, px_send, px, qy_send, qy, units):
+    shape = (4 * DOWN_ROWS, OWN)
+    total = dot(act[...].reshape(shape), feed[0:OWN]) + dot(act_got[...].reshape(shape), feed_got[0:OWN])
+    units[...] = total.astype(LOW).reshape(units.shape)
+    split_units(place, units, px_send, px, qy_send, qy)
+
+
+def down_units(place, act, act_got, feed, feed_got, after=()):
+    block = pl.BlockSpec((4, DOWN_ROWS, OWN), lambda i, place: (i, 0, 0))
+    return call(
+        down_kernel,
+        "down_units",
+        place,
+        [(act, block), (act_got, block), plain(feed), plain(feed_got)],
+        unit_outputs(DOWN_ROWS, WIDTH),
+        scratch=[pltpu.VMEM((2, 2, DOWN_ROWS, WIDTH), LOW)],
+        grid=(4,),
+        after=after,
+        work=cost(0.6e9, 3.5e6),
+    )
+
+
+def backward_kernel(
+    place, feed_ext, slope, up, down, second_grad, unit1, inverse1, gain1, wo_own, wo_other,
+    inner0, inner1, send0, send1, first_grad, branch_own, back_own, misc, sums,
+    normed_grad, branch,
+):
+    step = pl.program_id(0)
+    c = place[3]
+
+    @pl.when(step == 0)
+    def _():
+        normed_grad[...] = second_grad[...]
+        sums[...] = jnp.zeros_like(sums)
+
+    grad = (dot_nt(feed_ext[0:OWN], down[...]) * slope[...].astype(FLOAT)).astype(LOW)
+    for target, index in ((inner0, c), (inner1, 2 + c), (send0, 1 - c), (send1, 3 - c)):
+
+        @pl.when(step == index)
+        def _(target=target):
+            target[...] = grad
+
+    sums[pl.ds(4 + step, 1), :] = column_sum(grad.astype(FLOAT))
+    normed_grad[...] += dot_nt(grad, up[...])
+
+    @pl.when(step == pl.num_programs(0) - 1)
+    def _():
+        total = normed_grad[...]
+        unit = unit1[...]
+        sums[0:1, :] = column_sum(total * unit)
+        sums[1:2, :] = column_sum(total)
+        grad1 = norm_back(total * gain1[...], unit, inverse1[:, 0:1])
+        first_grad[...] = grad1
+        low = grad1.astype(LOW)
+        branch[...] = low
+        sums[2:3, :] = column_sum(low.astype(FLOAT))
+        branch_own[...] = branch[:, pl.ds(pl.multiple_of(c * HALF, LANES), HALF)]
+        back_own[...] = dot_nt(low, wo_own[...]).astype(LOW)
+        misc[0:OWN, 0:HALF] = branch[:, pl.ds(pl.multiple_of((1 - c) * HALF, LANES), HALF)]
+        misc[0:OWN, HALF:] = dot_nt(low, wo_other[...]).astype(LOW)
+        rows = sums[...]
+        misc[OWN:] = jnp.concatenate([rows, jnp.zeros_like(rows)], axis=0).astype(LOW)
+
+
+def backward(place, feed_ext, slope, second_grad, unit1, inverse1, weights, after=()):
+    chunk = WIDTH
+    return call(
+        backward_kernel,
+        "backward",
+        place,
+        [
+            plain(feed_ext),
+            (slope, pl.BlockSpec((OWN, chunk), lambda i, place: (0, i))),
+            (weights["up"], pl.BlockSpec((WIDTH, chunk), lambda i, place: (0, i))),
+            (weights["down"], pl.BlockSpec((chunk, WIDTH), lambda i, place: (i, 0))),
+            plain(second_grad), plain(unit1), plain(inverse1), plain(row_of(weights["gain1"])),
+            (weights["out"], pl.BlockSpec((HALF, WIDTH), lambda i, place: (place[3], 0))),
+            (weights["out"], pl.BlockSpec((HALF, WIDTH), lambda i, place: (1 - place[3], 0))),
+        ],
+        [made((OWN, WIDTH), LOW)] * 4
+        + [
+            made((OWN, WIDTH), FLOAT), made((OWN, HALF), LOW), made((OWN, HALF), LOW), made((EXT, WIDTH), LOW),
+            made((8, WIDTH), FLOAT),
+        ],
+        scratch=[pltpu.VMEM((OWN, WIDTH), FLOAT), pltpu.VMEM((OWN, WIDTH), LOW)],
+        grid=(FF // chunk,),
+        after=after,
+        work=cost(2.7e9, 16e6),
+    )
+
+
+def up_kernel(
+    place, normed_t, normed_got, inner0, inner1, got0, got1, att_t, branch, misc, sums0, sums1, feed_got,
+    down_px, down_px_got, down_qy, down_qy_got,
+    x_send, y_send, px, qy, down_p, down_q, units, normed_got_t,
+):
+    z = pl.program_id(0)
+    y, x = place[1], place[2]
+
+    @pl.when(z == 0)
+    def _():
+        normed_got_t[...] = jnp.transpose(normed_got[...].astype(FLOAT)).astype(LOW)
+
+    theirs = normed_got_t[pl.ds(pl.multiple_of(z * 192, 32), 192), :]
+    outer = dot(att_t[:, 0:OWN], branch[...]) + dot(att_t[:, OWN:], misc[0:OWN, 0:HALF])
+    for side, inner, got, sums, pair in ((0, inner0, got0, sums0, feed_got), (1, inner1, got1, sums1, misc)):
+        grad = dot(normed_t[...], inner[...]) + dot(theirs, got[...])
+        vectors = sums[...] + pair[OWN:].astype(FLOAT)[0:8]
+        for line in range(2):
+            first = line * 96 + side * 48
+            rest = jnp.concatenate([outer[first : first + 24], outer[first + 24 : first + 48]], axis=1)
+            units[line, side] = jnp.concatenate(
+                [grad[line * 96 : line * 96 + 96], rest, vectors], axis=0
+            ).astype(LOW)
+    half = UP_ROWS // 2
+    for line in range(2):
+        px[0, line] = units[line, x, 0:half]
+        x_send[0, line * half : line * half + half] = units[line, 1 - x, 0:half]
+    for side in range(2):
+        qy[0, side] = units[y, side, half:]
+        y_send[0, side * half : side * half + half] = units[1 - y, side, half:]
+    down_p[0] = added(down_px[0, y], down_px_got[0, y])
+    y_send[0, 2 * half :] = added(down_px[0, 1 - y], down_px_got[0, 1 - y])
+    down_q[0] = added(down_qy[0, x], down_qy_got[0, x])
+    x_send[0, 2 * half :] = added(down_qy[0, 1 - x], down_qy_got[0, 1 - x])
+
+
+def up_units(
+    place, normed_t, normed_got, inner, got, att_t, branch, misc, sums0, sums1, feed_got, down_pair, after=()
+):
+    rows = pl.BlockSpec((192, OWN), lambda i, place: (i, 0))
+    down_half = DOWN_ROWS // 2
+    block = pl.BlockSpec((1, 2, down_half, WIDTH), lambda i, place: (i, 0, 0, 0))
+    sent = ((4, UP_ROWS + down_half, WIDTH), LOW, pl.BlockSpec((1, UP_ROWS + down_half, WIDTH), lambda i, place: (i, 0, 0)))
+    down = ((4, down_half, WIDTH), LOW, pl.BlockSpec((1, down_half, WIDTH), lambda i, place: (i, 0, 0)))
+    return call(
+        up_kernel,
+        "up_units",
+        place,
+        [
+            (normed_t, rows), plain(normed_got), plain(inner[0]), plain(inner[1]), plain(got[0]), plain(got[1]),
+            (att_t, pl.BlockSpec((192, 512), lambda i, place: (i, 0))),
+            plain(branch), plain(misc), plain(sums0), plain(sums1), plain(feed_got),
+        ]
+        + [(array, block) for array in down_pair],
+        [sent, sent] + unit_outputs(UP_ROWS, WIDTH)[:2] + [down, down],
+        scratch=[pltpu.VMEM((2, 2, UP_ROWS, WIDTH), LOW), pltpu.VMEM((WIDTH, OWN), LOW)],
+        grid=(4,),
+        after=after,
+        work=cost(0.9e9, 5e6),
+    )
+
+
+def attention_back_kernel(
+    place, own_lengths, peer_lengths, q, k, v, log_total, att, back0, misc,
+    dq_out, dk_out, dv_out, bias,
+):
+    bases = first_positions(place)
+    ends = pair_ends(place, own_lengths, peer_lengths)
+    query_ids = [pairs_along(base, ends, 1)[0:1] for base in bases[:4]]
+    for j in range(8):
+        key_ids = pairs_along(bases[j], ends, 0)
+        for i in range(4):
+            bias[pl.ds(j * BLOCK, BLOCK), pl.ds(i * BLOCK, BLOCK)] = jnp.where(
+                key_ids == query_ids[i], 0.0, NEGATIVE
+            )
+    for pair in range(PAIRS_OF_HEADS):
+        lanes = pl.ds(pair * LANES, LANES)
+        keys = k[:, lanes]
+        values = v[:, lanes]
+        keys_t = jnp.transpose(keys.astype(FLOAT)).astype(LOW)
+        key_grad = jnp.zeros((1024, LANES), FLOAT)
+        value_grad = jnp.zeros((1024, LANES), FLOAT)
+        left = head_mask(OWN)
+        for part in range(2):
+            rows = pl.ds(part * OWN, OWN)
+            queries = q[rows, lanes]
+            grads = back0[:, lanes] if part == 0 else misc[0:OWN, pl.ds(HALF + pair * LANES, LANES)]
+            zeros = jnp.zeros_like(queries)
+            product = jnp.transpose(grads.astype(FLOAT) * att[rows, lanes].astype(FLOAT))
+            halves = []
+            for half in range(2):
+                if half == 0:
+                    chosen, chosen_grads = jnp.where(left, queries, zeros), jnp.where(left, grads, zeros)
+                else:
+                    chosen, chosen_grads = jnp.where(left, zeros, queries), jnp.where(left, zeros, grads)
+                delta = column_sum(product[half * HEAD_DIM : (half + 1) * HEAD_DIM])
+                head = pair * 2 + half
+                scores = dot_nt(keys, chosen) + bias[:, rows]
+                weights = jnp.exp(scores - log_total[head : head + 1, rows])
+                weight_grad = dot_nt(values, chosen_grads)
+                score_grad = (weights * (weight_grad - delta)).astype(LOW)
+                value_grad = value_grad + dot(weights.astype(LOW), chosen_grads)
+                key_grad = key_grad + dot(score_grad, chosen)
+                halves.append(dot(keys_t, score_grad))
+            query_grad_t = jnp.concatenate([halves[0][0:HEAD_DIM], halves[1][HEAD_DIM:LANES]], axis=0)
+            dq_out[rows, lanes] = (jnp.transpose(query_grad_t) * HEAD_DIM**-0.5).astype(LOW)
+        dk_out[:, lanes] = key_grad.astype(LOW)
+        dv_out[:, lanes] = value_grad.astype(LOW)
+
+
+def attention_back(place, lengths, q, k, v, log_total, att, back_own, misc, after=()):
+    return call(
+        attention_back_kernel,
+        "attention_back",
+        place,
+        [plain(array) for array in (q, k, v, log_total, att, back_own, misc)],
+        [made((512, HALF), LOW), made((1024, HALF), LOW), made((1024, HALF), LOW)],
+        scratch=[pltpu.VMEM((1024, 512), FLOAT)],
+        scalars=lengths,
+        after=after,
+        work=cost(7e9, 6e6, 3e6),
+    )
+
+
+def token_kernel(place, dq, dk, dv, wq, wk, wv, own, own_send, far, far_send):
+    for part, target in enumerate((own, own_send, far, far_send)):
+        rows = pl.ds(part * OWN, OWN)
+        total = dot_nt(dk[rows, :], wk[...]) + dot_nt(dv[rows, :], wv[...])
+        if part < 2:
+            total = total + dot_nt(dq[rows, :], wq[...])
+        target[...] = total.astype(LOW)
+
+
+def token_parts(place, dq, dk, dv, joint_weight, after=()):
+    def columns(kind):
+        return joint_weight, pl.BlockSpec((WIDTH, HALF), lambda i, place: (0, 2 * kind + place[3]))
+
+    return call(
+        token_kernel,
+        "token_parts",
+        place,
+        [plain(dq), plain(dk), plain(dv), columns(0), columns(1), columns(2)],
+        [made((OWN, WIDTH), LOW)] * 4,
+        after=after,
+        work=cost(1.5e9, 5e6),
+    )
+
+
+def back_rows_kernel(place, done0, done1, back0, back1, outputs, token_grad):
+    odd = place[0] % 2
+    outputs[odd] = done0[...]
+    outputs[1 - odd] = done1[...]
+    token_grad[odd] = back0[...].astype(FLOAT)
+    token_grad[1 - odd] = back1[...].astype(FLOAT)
+
+
+def back_rows(place, done, back, after=()):
+    return call(
+        back_rows_kernel,
+        "back_rows",
+        place,
+        [plain(array) for array in (*done, *back)],
+        [made((2, BLOCK, WIDTH), LOW), made((2, BLOCK, WIDTH), FLOAT)],
+        after=after,
+        work=cost(1e6, 2e6),
+    )
+
+
+def joint_kernel(
+    place, t0, t1, t2, t3, t4, t5, t6, t7, dq, dk, dv, px_send, px, qy_send, qy, tokens_t, units
+):
+    y, x = place[1], place[2]
+    for index, block in enumerate((t0, t1, t2, t3, t4, t5, t6, t7)):
+        tokens_t[:, pl.ds(index * BLOCK, BLOCK)] = jnp.transpose(block[...].astype(FLOAT)).astype(LOW)
+    biases = jnp.concatenate([column_sum(dq[...].astype(FLOAT)), column_sum(dv[...].astype(FLOAT))], axis=1)
+    biases = jnp.concatenate([biases, jnp.zeros((7, WIDTH), FLOAT)], axis=0)
+    for z in range(4):
+        rows = pl.ds(z * 192, 192)
+        query = dot(tokens_t[rows, 0:512], dq[...])
+        key = dot(tokens_t[rows, :], dk[...])
+        value = dot(tokens_t[rows, :], dv[...])
+        for line in range(2):
+            for side in range(2):
+                at = line * 96 + side * 48
+                units[line, side, 0:JOINT_FIRST] = jnp.concatenate(
+                    [query[at : at + 48], key[at : at + 48]], axis=1
+                ).astype(LOW)
+                rest = jnp.concatenate([value[at : at + 24], value[at + 24 : at + 48]], axis=1)
+                units[line, side, JOINT_FIRST:] = jnp.concatenate([rest, biases], axis=0).astype(LOW)
+        for line in range(2):
+            px[z, line] = units[line, x, 0:JOINT_FIRST]
+            px_send[z, line] = units[line, 1 - x, 0:JOINT_FIRST]
+        for side in range(2):
+            qy[z, side] = units[y, side, JOINT_FIRST:]
+            qy_send[z, side] = units[1 - y, side, JOINT_FIRST:]
+
+
+def joint_units(place, blocks, dq, dk, dv, after=()):
+    first, second = made((4, 2, JOINT_FIRST, WIDTH), LOW), made((4, 2, JOINT_SECOND, WIDTH), LOW)
+    return call(
+        joint_kernel,
+        "joint_units",
+        place,
+        [plain(array) for array in (*blocks, dq, dk, dv)],
+        [first, first, second, second],
+        scratch=[pltpu.VMEM((WIDTH, 1024), LOW), pltpu.VMEM((2, 2, JOINT_ROWS, WIDTH), LOW)],
+        after=after,
+        work=cost(1.5e9, 6e6),
+    )
+
+
+def added(left, right):
+    return (left.astype(FLOAT) + right.astype(FLOAT)).astype(LOW)
+
+
+def second_kernel(
+    place, x_got, y_got, px, qy, down_p, down_q, far, far_got, joint_px, joint_qy,
+    x_send, y_send, p, q, down_send, down_keep,
+):
+    z_here, y, x = place[0], place[1], place[2]
+    half = UP_ROWS // 2
+    down_at = UP_ROWS
+    for z in range(4):
+        for got, have, own, keep, send in ((x_got, px, y, p, y_send), (y_got, qy, x, q, x_send)):
+            mine = pl.ds(pl.multiple_of(own * half, half), half)
+            other = pl.ds(pl.multiple_of((1 - own) * half, half), half)
+            keep[z] = added(have[z, own], got[z, mine])
+            send[pl.ds(z * half, half), :] = added(have[z, 1 - own], got[z, other])
+        for other in range(2):
+            at = z * 2 + other
+            x_send[pl.ds(OWN + at * JOINT_FIRST, JOINT_FIRST), :] = joint_px[z, other]
+            y_send[pl.ds(2 * OWN + at * JOINT_SECOND, JOINT_SECOND), :] = joint_qy[z, other]
+    y_send[pl.ds(OWN, OWN), :] = added(far[...], far_got[...])
+    low = z_here % 2
+    small = DOWN_ROWS // 2
+    for target, parity in ((down_keep, low), (down_send, 1 - low)):
+        for high in range(2):
+            index = 2 * high + parity
+            target[high, 0:small] = added(down_p[index], y_got[index, down_at:])
+            target[high, small:] = added(down_q[index], x_got[index, down_at:])
+
+
+def second_stage(place, x_got, y_got, px, qy, down_p, down_q, far, far_got, joint_px, joint_qy, after=()):
+    kept = made((4, UP_ROWS // 2, WIDTH), LOW)
+    down = made((2, DOWN_ROWS, WIDTH), LOW)
+    return call(
+        second_kernel,
+        "second_stage",
+        place,
+        [plain(array) for array in (x_got, y_got, px, qy, down_p, down_q, far, far_got, joint_px, joint_qy)],
+        [
+            made((OWN + 8 * JOINT_FIRST, WIDTH), LOW), made((2 * OWN + 8 * JOINT_SECOND, WIDTH), LOW),
+            kept, kept, down, down,
+        ],
+        after=after,
+        work=cost(1e6, 1e7),
+    )
+
+
+def third_kernel(
+    place, x_got, y_got, p, q, px, qy, own, own_got, first_grad,
+    x_send, y_send, joint_p, joint_q, up_send, up_keep, token0, token1,
+):
+    z_here, y, x = place[0], place[1], place[2]
+    half = UP_ROWS // 2
+    for z in range(4):
+
+        def from_x(line):
+            at = OWN + (z * 2 + line) * JOINT_FIRST
+            return x_got[pl.ds(pl.multiple_of(at, 16), JOINT_FIRST), :]
+
+        def from_y(side):
+            at = 2 * OWN + (z * 2 + side) * JOINT_SECOND
+            return y_got[pl.ds(pl.multiple_of(at, 16), JOINT_SECOND), :]
+
+        joint_p[z] = added(px[z, y], from_x(y))
+        y_send[z] = added(px[z, 1 - y], from_x(1 - y))
+        joint_q[z] = added(qy[z, x], from_y(x))
+        x_send[z] = added(qy[z, 1 - x], from_y(1 - x))
+    low = z_here % 2
+    for target, parity in ((up_keep, low), (up_send, 1 - low)):
+        for high in range(2):
+            index = 2 * high + parity
+            rows = pl.ds(pl.multiple_of(index * half, half), half)
+            target[high, 0:half] = added(p[index], y_got[rows, :])
+            target[high, half:] = added(q[index], x_got[rows, :])
+    across = y_got[pl.ds(OWN, OWN), :].astype(FLOAT)
+    total = own[...].astype(FLOAT) + own_got[...].astype(FLOAT) + across + first_grad[...]
+    total = total.astype(LOW)
+    token0[...] = total[0:BLOCK]
+    token1[...] = total[BLOCK:]
+
+
+def third_stage(place, arrays, after=()):
+    joint = [made((4, JOINT_SECOND, WIDTH), LOW), made((4, JOINT_FIRST, WIDTH), LOW)]
+    return call(
+        third_kernel,
+        "third_stage",
+        place,
+        [plain(array) for array in arrays],
+        joint + joint[::-1] + [made((2, UP_ROWS, WIDTH), LOW)] * 2 + [made((BLOCK, WIDTH), LOW)] * 2,
+        after=after,
+        work=cost(1e6, 1e7),
+    )
+
+
+def fourth_kernel(place, x_got, y_got, p, q, keep_two, got, send, keep, up_send, up_keep):
+    low, high_here = place[0] % 2, place[0] // 2
+    for target, parity in ((keep, low), (send, 1 - low)):
+        for high in range(2):
+            index = 2 * high + parity
+            target[high, 0:JOINT_FIRST] = added(p[index], y_got[index])
+            target[high, JOINT_FIRST:] = added(q[index], x_got[index])
+    up_keep[...] = added(keep_two[high_here], got[high_here])
+    up_send[...] = added(keep_two[1 - high_here], got[1 - high_here])
+
+
+def fourth_stage(place, arrays, after=()):
+    return call(
+        fourth_kernel,
+        "fourth_stage",
+        place,
+        [plain(array) for array in arrays],
+        [made((2, JOINT_ROWS, WIDTH), LOW)] * 2 + [made((UP_ROWS, WIDTH), LOW)] * 2,
+        after=after,
+        work=cost(1e6, 1e6),
+    )
+
+
+def end_stage_kernel(place, keep_two, got, send, keep):
+    high = place[0] // 2
+    keep[...] = added(keep_two[high], got[high])
+    send[...] = added(keep_two[1 - high], got[1 - high])
+
+
+def end_stage(place, keep_two, got, after=()):
+    return call(
+        end_stage_kernel,
+        "end_stage",
+        place,
+        [plain(keep_two), plain(got)],
+        [made(keep_two.shape[1:], LOW)] * 2,
+        after=after,
+        work=cost(1e6, 1e6),
+    )
+
+
+def last_sum_kernel(place, *refs):
+    out = refs[-1]
+    at = 0
+    for first, second in zip(refs[0:-1:2], refs[1:-1:2]):
+        out[pl.ds(at, first.shape[0]), :] = added(first[...], second[...])
+        at += first.shape[0]
+
+
+def last_sum(place, pairs, after=()):
+    arrays = [array for pair in pairs for array in pair]
+    rows = sum(pair[0].shape[0] for pair in pairs)
+    results, mark = call(
+        last_sum_kernel,
+        "last_sum",
+        place,
+        [plain(array) for array in arrays],
+        [made((rows, arrays[0].shape[1]), LOW)],
+        after=after,
+        work=cost(1e6, 1e6),
+    )
+    return results[0], mark
+
+
+def gathered(unit):
+    across = x_swap(unit)
+    return unit, core_swap(unit), across, core_swap(across)
+
+
+def quarters(place):
+    x, c = place[2], place[3]
+    return (x, c), (x, 1 - c), (1 - x, c), (1 - x, 1 - c)
+
+
+def line_shift(place):
+    seq = place[0] * 2 + place[1]
+    return lax.rem(WIDTH - seq * 96, WIDTH)
+
+
+def dense_out_kernel(
+    place, u0, u1, u2, u3, down, up, out, gain2, shift2, down_bias, gain1, shift1, out_bias, up_bias, heads, tails
+):
+    for unit, (x, c) in zip((u0, u1, u2, u3), quarters(place)):
+        quarter = 2 * x + c
+        down[pl.ds(pl.multiple_of(quarter * DOWN_ROWS, 32), DOWN_ROWS), :] = unit[0:DOWN_ROWS, :].astype(FLOAT)
+        up[:, pl.ds(pl.multiple_of(quarter * WIDTH, LANES), WIDTH)] = unit[96:192, :].astype(FLOAT)
+        rest = unit[192:224, :].astype(FLOAT)
+        lanes = pl.ds(pl.multiple_of(c * HALF, LANES), HALF)
+        out[pl.ds(pl.multiple_of(x * 48, 8), 24), lanes] = rest[0:24, 0:HALF]
+        out[pl.ds(pl.multiple_of(x * 48 + 24, 8), 24), lanes] = rest[0:24, HALF:]
+
+        @pl.when(x == 0)
+        def _(rest=rest):
+            heads[...] = rest[24:32]
+
+        @pl.when(x == 1)
+        def _(rest=rest):
+            tails[...] = rest[24:32]
+
+    seq = place[0] * 2 + place[1]
+    shift = line_shift(place)
+    head = pltpu.roll(heads[...], shift, 1)
+    gain2[...] = head[0:1, 0:96]
+    shift2[...] = head[1:2, 0:96]
+    down_bias[...] = head[2:3, 0:96]
+    tail = pltpu.roll(tails[...], shift, 1)
+    gain1[...] = tail[0:1, 0:96]
+    shift1[...] = tail[1:2, 0:96]
+    out_bias[...] = tail[2:3, 0:96]
+    wide = tails[pl.ds(4 + seq // 2, 1), :]
+    up_bias[...] = jnp.where(seq % 2 == 0, wide[:, 0:HALF], wide[:, HALF:])
+
+
+def dense_outputs(place, units, after=()):
+    results, mark = call(
+        dense_out_kernel,
+        "dense_outputs",
+        place,
+        [plain(unit) for unit in units],
+        [made((4 * DOWN_ROWS, WIDTH), FLOAT), made((96, FF), FLOAT), made((96, WIDTH), FLOAT)]
+        + [made((1, 96), FLOAT)] * 6
+        + [made((1, HALF), FLOAT)],
+        scratch=[pltpu.VMEM((8, WIDTH), FLOAT)] * 2,
+        after=after,
+        work=cost(1e6, 3e6),
+    )
+    return (*results[:3], *(vector.reshape(-1) for vector in results[3:])), mark
+
+
+def joint_out_kernel(place, u0, u1, u2, u3, joint, query_bias, value_bias, sums):
+    for unit, (x, c) in zip((u0, u1, u2, u3), quarters(place)):
+
+        def lanes(kind):
+            return pl.ds(pl.multiple_of(kind * WIDTH + c * HALF, LANES), HALF)
+
+        first = unit[0:JOINT_FIRST].astype(FLOAT)
+        rest = unit[JOINT_FIRST:].astype(FLOAT)
+        rows = pl.ds(pl.multiple_of(x * 48, 16), 48)
+        joint[rows, lanes(0)] = first[:, 0:HALF]
+        joint[rows, lanes(1)] = first[:, HALF:]
+        joint[pl.ds(pl.multiple_of(x * 48, 8), 24), lanes(2)] = rest[0:24, 0:HALF]
+        joint[pl.ds(pl.multiple_of(x * 48 + 24, 8), 24), lanes(2)] = rest[0:24, HALF:]
+
+        @pl.when(x == 0)
+        def _(rest=rest, c=c):
+            half = pl.ds(pl.multiple_of(c * HALF, LANES), HALF)
+            sums[0:1, half] = rest[24:25, 0:HALF]
+            sums[1:2, half] = rest[24:25, HALF:]
+
+    turned = pltpu.roll(sums[...], line_shift(place), 1)
+    query_bias[...] = turned[0:1, 0:96]
+    value_bias[...] = turned[1:2, 0:96]
+
+
+def joint_outputs(place, units, after=()):
+    results, mark = call(
+        joint_out_kernel,
+        "joint_outputs",
+        place,
+        [plain(unit) for unit in units],
+        [made((96, 3 * WIDTH), FLOAT), made((1, 96), FLOAT), made((1, 96), FLOAT)],
+        scratch=[pltpu.VMEM((8, WIDTH), FLOAT)],
+        after=after,
+        work=cost(1e6, 2e6),
+    )
+    return (results[0], results[1].reshape(-1), results[2].reshape(-1)), mark
+
+
+def row_body(
+    tokens,
+    pair_lengths,
+    joint_weight,
+    query_bias,
+    value_bias,
+    out_weight,
+    out_bias,
+    first_gain,
+    first_shift,
+    up_weight,
+    up_bias,
+    down_weight,
+    down_bias,
+    second_gain,
+    second_shift,
+    cotangent,
+):
+    seq, rows = lax.axis_index("seq"), lax.axis_index("rows")
+    z, y, x, c = seq // 2, seq % 2, rows // 2, rows % 2
+    place = jnp.stack([z, y, x, c]).astype(jnp.int32)
+    odd = z % 2
+    weights = {
+        "out": out_weight, "out_bias": out_bias, "gain1": first_gain, "shift1": first_shift,
+        "up": up_weight, "up_bias": up_bias, "down": down_weight, "down_bias": down_bias,
+        "gain2": second_gain, "shift2": second_shift,
+    }
+
+    def local_row(array, index):
+        return lax.dynamic_index_in_dim(array, index, 0, keepdims=False)
+
+    own = [row_swap(local_row(tokens, odd), 0), row_swap(local_row(tokens, 1 - odd), 1)]
+    lengths = (pair_lengths, core_swap(pair_lengths))
+    across = [y_swap(block) for block in own]
+    blocks = (
+        own + [core_swap(block) for block in own] + across + [core_swap(block) for block in across]
+    )
+    cotangent, _ = lax.optimization_barrier((cotangent, across[0]))
+    cotangents = [row_swap(local_row(cotangent, odd), 0), row_swap(local_row(cotangent, 1 - odd), 1)]
+
+    (att, q, k, v, log_total), mark = attention(place, lengths, blocks, joint_weight, query_bias, value_bias)
+    att_got = core_swap(att)
+    results, mark = forward(place, att, att_got, own, cotangents, weights, (mark,))
+    (
+        result0, result1, feed, second_grad, act, act_send, slope, unit1, inverse1, normed, normed_t, att_t, sums0
+    ) = results
+    act_got, feed_got, normed_got = core_swap(act_send), core_swap(feed), core_swap(normed)
+    done = (row_swap(result0, 0), row_swap(result1, 1))
+    (px_send, px, qy_send, qy), mark = down_units(place, act, act_got, feed, feed_got, (mark,))
+    down_pair = (px, x_swap(px_send), qy, y_swap(qy_send))
+    results, mark = backward(place, feed, slope, second_grad, unit1, inverse1, weights, (mark, normed_got, *done))
+    inner0, inner1, send0, send1, first_grad, branch_own, back_own, misc_send, sums1 = results
+    got, misc = (core_swap(send0), core_swap(send1)), core_swap(misc_send)
+    (x_send, y_send, px, qy, down_p, down_q), mark = up_units(
+        place, normed_t, normed_got, (inner0, inner1), got, att_t, branch_own, misc, sums0, sums1, feed_got,
+        down_pair, (mark,)
+    )
+    x_got, y_got = x_swap(x_send), y_swap(y_send)
+    (dq, dk, dv), mark = attention_back(place, lengths, q, k, v, log_total, att, back_own, misc, (mark,))
+    (token_own, own_send, token_far, far_send), mark = token_parts(place, dq, dk, dv, joint_weight, (mark,))
+    own_got, far_got = core_swap(own_send), core_swap(far_send)
+    (joint_px_send, joint_px, joint_qy_send, joint_qy), mark = joint_units(place, blocks, dq, dk, dv, (mark,))
+    (x_send, y_send, p, q_, down_send, down_keep), mark = second_stage(
+        place, x_got, y_got, px, qy, down_p, down_q, token_far, far_got, joint_px_send, joint_qy_send, (mark,)
+    )
+    x_got, y_got = x_swap(x_send), y_swap(y_send)
+    (down_send, down_keep), mark = end_stage(place, down_keep, z_swap(down_send, 1), (mark,))
+    down_got = z_swap(down_send, 2)
+    results, mark = third_stage(
+        place, (x_got, y_got, p, q_, joint_px, joint_qy, token_own, own_got, first_grad), (mark, down_got)
+    )
+    x_send, y_send, joint_p, joint_q, up_send, up_keep, token0, token1 = results
+    x_got, y_got, up_got = x_swap(x_send), y_swap(y_send), z_swap(up_send, 1)
+    (joint_send, joint_keep, up_send, up_keep), mark = fourth_stage(
+        place, (x_got, y_got, joint_p, joint_q, up_keep, up_got), (mark,)
+    )
+    joint_got, up_got = z_swap(joint_send, 1), z_swap(up_send, 2)
+    (joint_send, joint_keep), mark = end_stage(place, joint_keep, joint_got, (mark,))
+    joint_got = z_swap(joint_send, 2)
+    dense_unit, mark = last_sum(place, ((down_keep, down_got), (up_keep, up_got)), (mark,))
+    dense_all = gathered(dense_unit)
+    back = (row_swap(token0, 0), row_swap(token1, 1))
+    joint_unit, mark = last_sum(place, ((joint_keep, joint_got),), (mark,))
+    joint_all = gathered(joint_unit)
+    (outputs, token_grad), mark = back_rows(place, done, back, (mark,))
+    (
+        down_grad, up_grad, out_grad, second_gain_grad, second_shift_grad, down_bias_grad, first_gain_grad,
+        first_shift_grad, out_bias_grad, up_bias_grad,
+    ), mark = dense_outputs(place, dense_all, (mark,))
+    (joint_grad, query_bias_grad, value_bias_grad), mark = joint_outputs(place, joint_all, (mark,))
+    return (
+        outputs,
+        token_grad,
+        joint_grad,
+        query_bias_grad,
+        value_bias_grad,
+        out_grad,
+        out_bias_grad,
+        first_gain_grad,
+        first_shift_grad,
+        up_grad,
+        up_bias_grad,
+        down_grad,
+        down_bias_grad,
+        second_gain_grad,
+        second_shift_grad,
+    )
+
+
+def body(tokens, *others):
+    if (lax.axis_size("seq"), lax.axis_size("rows")) == (8, 4) and tokens.shape == (2, BLOCK, WIDTH):
+        return row_body(tokens, *others)
+    return general_body(tokens, *others)
+
+
 def solution(mesh):
     placed = (
         P("rows", "seq", None),

time: 1040 us -> 193 us (0.19)
  waiting for transfers between devices: 573 us -> 61.4 us
  matrix products: 149 us -> 0 us
  other arithmetic: 127 us -> 0.67 us
  local copies, waits for them, and re-layouts: 114 us -> 7.09 us
  Pallas kernels: 0 us -> 59.5 us
  starting transfers between devices: 10.2 us -> 62.3 us
  blocking collectives: 43.7 us -> 0 us
  between operations: 16.4 us -> 1.38 us
    reduce_scatter x3 -> x0, waiting for transfers between devices: 262 us -> none  [the longest x1 98.6 us: body(): lax.psum_scatter(gradients[9].astype(jnp.bfloat16), 'seq', scatter_dimens...]
    dot_general x68 -> x0, matrix products: 149 us -> none  [the longest x8 25.5 us: online_block(): jnp.einsum('rqhd,rkhd->rhqk', query_heads, split_heads(key_block), prefer...]
    all_gather x2 -> x0, waiting for transfers between devices: 114 us -> none  [the longest x1 63.3 us: body(): key_piece = lax.all_gather(keys, 'seq', axis=1, tiled=True)]
    ppermute x30 -> x44, waiting for transfers between devices: 131 us -> 61.4 us  [permute(): return lax.ppermute(value, AXES, pairs)]
    unnamed x8 -> x0, waiting for transfers between devices: 66.9 us -> none
    convert_element_type x44 -> x0, other arithmetic: 61.7 us -> none  [the longest x7 13.5 us: send_key_sums(): from_behind(sums[0].astype(jnp.bfloat16), 'seq', 1).astype(jnp.float32)]
    pallas_call x0 -> x18, Pallas kernels: none -> 59.5 us  [call(): pl.pallas_call(ordered, grid_spec=pltpu.PrefetchScalarGridSpec(num_scalar...]
    ppermute x30 -> x44, starting transfers between devices: 9.92 us -> 62.3 us  [permute(): return lax.ppermute(value, AXES, pairs)]
  transfers between devices with their start and end apart: 37 -> 44, of which waited for: 21 -> 17; matrix products, arithmetic and copies ran while one was open for 19% -> 1% of each run, Pallas kernels for 0% -> 17%
where the time goes in v2:
time: 193 us; the launch traced here: 192 us
  starting transfers between devices  62.3 us (32%)
  waiting for transfers between devices  61.4 us (32%)
  Pallas kernels  59.5 us (31%)
  local copies, waits for them, and re-layouts  7.09 us (4%)
    ppermute x44, starting transfers between devices, permute(): return lax.ppermute(value, AXES, pairs)  62.3 us
    ppermute x44, waiting for transfers between devices, permute(): return lax.ppermute(value, AXES, pairs)  61.4 us
    pallas_call x18, Pallas kernels, call(): pl.pallas_call(ordered, grid_spec=pltpu.PrefetchScalarGridSpec(num_scalar...  59.5 us
    unnamed x66, local copies, waits for them, and re-layouts  4.61 us
  transfers between devices with their start and end apart: 44, of which 17 were waited for; matrix products, arithmetic and copies ran while one was open for 1% of the time, Pallas kernels for 17%

profile of v2, /device:TPU:0, one launch (start us, length us, event | category | flops | bytes accessed | tf_op | source)
XLA Modules:
  0.0 192.2 jit_solution(7218104459516736187)
XLA Ops:
  0.7 1.1 dynamic-slice_bitcast_fusion.2
  1.7 3.1 %collective-permute-start.2 = (bf16[128,768]{1,0:T(8,128)(2,1)S(1)}, bf16[128,768]{1,0:T(8,128)(2,1)S(1)}, u32[]{:S(2)}, u32[]{:S(2)}) collective-permute-start(bf16[128,768]{1,0:T(8,128)(2,1)S(1)} %get-tuple-element.227), channel_id=1, source_target_pairs={{0,8},{1,24},{2,10},{3,26},{4,12},{5,28},{6,14},{7,30},{8,0},{9,16... | collective-permute-start | bytes 589832 | tf_op jit(solution)/shard_map/ppermute | solution.py:404
  5.5 3.1 %collective-permute-done.2.refs_4_.refs_7_.refs_2_ = bf16[128,768]{1,0:T(8,128)(2,1)S(1)} collective-permute-done((bf16[128,768]{1,0:T(8,128)(2,1)S(1)}, bf16[128,768]{1,0:T(8,128)(2,1)S(1)}, u32[]{:S(2)}, u32[]{:S(2)}) %collective-permute-start.2) | collective-permute-done | bytes 196640 | tf_op jit(solution)/shard_map/ppermute | solution.py:404
  8.6 2.4 %collective-permute-start.6 = (bf16[128,768]{1,0:T(8,128)(2,1)S(1)}, bf16[128,768]{1,0:T(8,128)(2,1)S(1)}, u32[]{:S(2)}, u32[]{:S(2)}) collective-permute-start(bf16[128,768]{1,0:T(8,128)(2,1)S(1)} %collective-permute-done.2.refs_4_.refs_7_.refs_2_), channel_id=1, source_target_pairs={{0,4},{1,5},{2,6},{3,7},{4,0},{5,1},{6,2},{7,3},{8,12},{9,13},{10,... | collective-permute-start | bytes 589832 | tf_op jit(solution)/shard_map/ppermute | solution.py:404
  11.0 6.2 %collective-permute-start.4 = (bf16[128,768]{1,0:T(8,128)(2,1)S(1)}, bf16[128,768]{1,0:T(8,128)(2,1)S(1)}, u32[]{:S(2)}, u32[]{:S(2)}) collective-permute-start(bf16[128,768]{1,0:T(8,128)(2,1)S(1)} %collective-permute-done.2.refs_4_.refs_7_.refs_2_), channel_id=1, source_target_pairs={{0,1},{1,0},{2,3},{3,2},{4,5},{5,4},{6,7},{7,6},{8,9},{9,8},{10,11... | collective-permute-start | bytes 589832 | tf_op jit(solution)/shard_map/ppermute | solution.py:404
  17.2 1.5 collective-permute-start.8
  19.2 1.6 collective-permute-start.7
  22.3 2.2 %copy-done = bf16[768,2304]{1,0:T(8,128)(2,1)S(1)} copy-done((bf16[768,2304]{1,0:T(8,128)(2,1)S(1)}, bf16[768,2304]{1,0:T(8,128)(2,1)}, u32[]{:S(2)}) %copy-start) | copy-done | bytes 3538968
  25.3 9.1 %attention.1 = (bf16[512,384]{1,0:T(8,128)(2,1)S(1)}, bf16[512,384]{1,0:T(8,128)(2,1)S(1)}, bf16[1024,384]{1,0:T(8,128)(2,1)S(1)}, bf16[1024,384]{1,0:T(8,128)(2...) custom-call(s32[4]{0:T(128)S(1)} %pad_add_fusion.refs_0_, s32[2,16]{1,0:T(2,128)S(1)} %copy-done.22, ...), custom_call_target="tpu_custom_call" | custom-call | flops 1024 | bytes 1024 | tf_op jit(solution)/shard_map/attention/pallas_call | solution.py:368
  36.6 1.3 collective-permute-start.11
  38.9 4.1 %collective-permute-done.11.refs_17_ = bf16[128,768]{1,0:T(8,128)(2,1)S(1)} collective-permute-done((bf16[128,768]{1,0:T(8,128)(2,1)S(1)}, bf16[128,768]{1,0:T(8,128)(2,1)S(1)}, u32[]{:S(2)}, u32[]{:S(2)}) %collective-permute-start.11) | collective-permute-done | bytes 196640 | tf_op jit(solution)/shard_map/ppermute | solution.py:404
  43.1 9.1 %forward.1 = (bf16[128,768]{1,0:T(8,128)(2,1)S(1)}, bf16[128,768]{1,0:T(8,128)(2,1)S(1)}, bf16[272,768]{1,0:T(8,128)(2,1)S(1)}, f32[256,768]{1,0:T(8,128)S(1)}, ...) custom-call(s32[4]{0:T(128)S(1)} %pad_add_fusion.refs_0_, ...), custom_call_target="tpu_custom_call" | custom-call | flops 1024 | bytes 1024 | tf_op jit(solution)/shard_map/forward/pallas_call | solution.py:368
  52.2 6.7 %collective-permute-start.15 = (bf16[16,96,256]{2,1,0:T(8,128)(2,1)S(1)}, bf16[16,96,256]{2,1,0:T(8,128)(2,1)S(1)}, u32[]{:S(2)}, u32[]{:S(2)}) collective-permute-start(bf16[16,96,256]{2,1,0:T(8,128)(2,1)S(1)} %get-tuple-element.133), channel_id=1, source_target_pairs={{0,1},{1,0},{2,3},{3,2},{4,5},{5,4},{6,7},{7,6},{8,9},{9,8},{10,11... | collective-permute-start | bytes 2359304 | tf_op jit(solution)/shard_map/ppermute | solution.py:404
  60.1 1.3 collective-permute-done.16.refs_4_.refs_12_
  61.4 2.6 %down_units.1 = (bf16[4,2,48,768]{3,2,1,0:T(8,128)(2,1)S(1)}, bf16[4,2,48,768]{3,2,1,0:T(8,128)(2,1)S(1)}, bf16[4,2,48,768]{3,2,1,0:T(8,128)(2,1)S(1)}, bf16[4,2,48,768]{3,2,1,0:T(8,128)(2,1)S(1)}, f32[8,128]{1,0:T(8,128)S(1)}) custom-call(s32[4]{0:T(128)S(1)} %pad_add_fusion.refs_0_, bf16[16,96,256]{2,1,0:T(8,128)(2,1)S(1)} %get-tuple-element.132.refs_1_, ...), custom_call_target="tpu_custom_call" | custom-call | flops 1024 | bytes 1024 | tf_op jit(solution)/shard_map/down_units/pallas_call | solution.py:368
  64.0 1.6 collective-permute-start.20
  65.6 1.5 collective-permute-start.21
  67.2 8.4 %backward.1 = (bf16[256,768]{1,0:T(8,128)(2,1)S(1)}, bf16[256,768]{1,0:T(8,128)(2,1)S(1)}, bf16[256,768]{1,0:T(8,128)(2,1)S(1)}, bf16[256,768]{1,0:T(8,128)(2,1)...) custom-call(s32[4]{0:T(128)S(1)} %pad_add_fusion.refs_0_, ...), custom_call_target="tpu_custom_call" | custom-call | flops 1024 | bytes 1024 | tf_op jit(solution)/shard_map/backward/pallas_call | solution.py:368
  75.6 4.3 %collective-permute-start.19 = (bf16[272,768]{1,0:T(8,128)(2,1)S(1)}, bf16[272,768]{1,0:T(8,128)(2,1)S(1)}, u32[]{:S(2)}, u32[]{:S(2)}) collective-permute-start(bf16[272,768]{1,0:T(8,128)(2,1)S(1)} %get-tuple-element.142), channel_id=1, source_target_pairs={{0,1},{1,0},{2,3},{3,2},{4,5},{5,4},{6,7},{7,6},{8,9},{9,8},{10,11... | collective-permute-start | bytes 1253384 | tf_op jit(solution)/shard_map/ppermute | solution.py:404
  80.4 1.4 collective-permute-done.17.refs_5_
  82.4 3.7 %up_units.1 = (bf16[4,176,768]{2,1,0:T(8,128)(2,1)S(1)}, bf16[4,176,768]{2,1,0:T(8,128)(2,1)S(1)}, bf16[4,2,64,768]{3,2,1,0:T(8,128)(2,1)S(1)}, bf16[4,2,64,768]...) custom-call(s32[4]{0:T(128)S(1)} %pad_add_fusion.refs_0_, ...), custom_call_target="tpu_custom_call" | custom-call | flops 1024 | bytes 1024 | tf_op jit(solution)/shard_map/up_units/pallas_call | solution.py:368
  86.2 1.6 collective-permute-start.22
  87.7 1.5 collective-permute-start.23
  89.3 9.3 %attention_back.1 = (bf16[512,384]{1,0:T(8,128)(2,1)S(1)}, bf16[1024,384]{1,0:T(8,128)(2,1)S(1)}, bf16[1024,384]{1,0:T(8,128)(2,1)S(1)}, f32[8,128]{1,0:T(8,128)S(1)}) custom-call(s32[4]{0:T(128)S(1)} %pad_add_fusion.refs_0_, s32[2,16]{1,0:T(2,128)S(1)} %copy-done.23, s32[2,16]{1,0:T(2,128)S(1)} %collective-permute-done.refs_2_, ...), custom_call_target="tpu_custom_call" | custom-call | flops 1024 | bytes 1024 | tf_op jit(solution)/shard_map/attention_back/pallas_call | solution.py:368
  98.7 2.8 %token_parts.1 = (bf16[256,768]{1,0:T(8,128)(2,1)S(1)}, bf16[256,768]{1,0:T(8,128)(2,1)S(1)}, bf16[256,768]{1,0:T(8,128)(2,1)S(1)}, bf16[256,768]{1,0:T(8,128)(2,1)S(1)}, f32[8,128]{1,0:T(8,128)S(1)}) custom-call(s32[4]{0:T(128)S(1)} %pad_add_fusion.refs_0_, bf16[512,384]{1,0:T(8,128)(2,1)S(1)} %get-tuple-element.162.refs_1_.refs_9_, ...), custom_call_target="tpu_custom_call" | custom-call | flops 1024 | bytes 1024 | tf_op jit(solution)/shard_map/token_parts/pallas_call | solution.py:368
  101.6 3.4 %joint_units.1 = (bf16[4,2,48,768]{3,2,1,0:T(8,128)(2,1)S(1)}, bf16[4,2,48,768]{3,2,1,0:T(8,128)(2,1)S(1)}, bf16[4,2,32,768]{3,2,1,0:T(8,128)(2,1)S(1)}, bf16[4,2,32,768]{3,2,1,0:T(8,128)(2,1)S(1)}, f32[8,128]{1,0:T(8,128)S(1)}) custom-call(s32[4]{0:T(128)S(1)} %pad_add_fusion.refs_0_, bf16[128,768]{1,0:T(8,128)(2,1)S(1)} %collective-permute-done.1.refs_3_.refs_6_.refs_1_, ...), custom_call_target="tpu_custom_call" | custom-call | flops 1024 | bytes 1024 | tf_op jit(solution)/shard_map/joint_units/pallas_call | solution.py:368
  105.0 7.4 %collective-permute-done.22.refs_1_ = bf16[4,176,768]{2,1,0:T(8,128)(2,1)S(1)} collective-permute-done((bf16[4,176,768]{2,1,0:T(8,128)(2,1)S(1)}, bf16[4,176,768]{2,1,0:T(8,128)(2,1)S(1)}, u32[]{:S(2)}, u32[]{:S(2)}) %collective-permute-start.22) | collective-permute-done | bytes 1081376 | tf_op jit(solution)/shard_map/ppermute | solution.py:404
  112.4 1.2 collective-permute-done.23.refs_2_
  113.6 1.2 second_stage.1
  114.8 1.6 collective-permute-start.26
  116.9 3.0 %collective-permute-start.28 = (bf16[2,96,768]{2,1,0:T(8,128)(2,1)S(1)}, bf16[2,96,768]{2,1,0:T(8,128)(2,1)S(1)}, u32[]{:S(2)}, u32[]{:S(2)}) collective-permute-start(bf16[2,96,768]{2,1,0:T(8,128)(2,1)S(1)} %get-tuple-element.182), channel_id=1, source_target_pairs={{0,8},{1,9},{2,10},{3,11},{4,12},{5,13},{6,14},{7,15},{8,0},{9,1},... | collective-permute-start | bytes 884744 | tf_op jit(solution)/shard_map/ppermute | solution.py:404
  119.8 5.9 %collective-permute-done.28.refs_2_ = bf16[2,96,768]{2,1,0:T(8,128)(2,1)S(1)} collective-permute-done((bf16[2,96,768]{2,1,0:T(8,128)(2,1)S(1)}, bf16[2,96,768]{2,1,0:T(8,128)(2,1)S(1)}, u32[]{:S(2)}, u32[]{:S(2)}) %collective-permute-start.28) | collective-permute-done | bytes 294944 | tf_op jit(solution)/shard_map/ppermute | solution.py:404
  126.4 1.5 collective-permute-start.29
  127.9 6.5 %collective-permute-done.29.refs_11_.refs_2_ = bf16[96,768]{1,0:T(8,128)(2,1)S(1)} collective-permute-done((bf16[96,768]{1,0:T(8,128)(2,1)S(1)}, bf16[96,768]{1,0:T(8,128)(2,1)S(1)}, u32[]{:S(2)}, u32[]{:S(2)}) %collective-permute-start.29) | collective-permute-done | bytes 147488 | tf_op jit(solution)/shard_map/ppermute | solution.py:404
  134.4 4.6 %collective-permute-done.25.refs_1_ = bf16[640,768]{1,0:T(8,128)(2,1)S(1)} collective-permute-done((bf16[640,768]{1,0:T(8,128)(2,1)S(1)}, bf16[640,768]{1,0:T(8,128)(2,1)S(1)}, u32[]{:S(2)}, u32[]{:S(2)}) %collective-permute-start.25) | collective-permute-done | bytes 983072 | tf_op jit(solution)/shard_map/ppermute | solution.py:404
  139.0 3.0 %collective-permute-done.26.refs_2_ = bf16[768,768]{1,0:T(8,128)(2,1)S(1)} collective-permute-done((bf16[768,768]{1,0:T(8,128)(2,1)S(1)}, bf16[768,768]{1,0:T(8,128)(2,1)S(1)}, u32[]{:S(2)}, u32[]{:S(2)}) %collective-permute-start.26) | collective-permute-done | bytes 1179680 | tf_op jit(solution)/shard_map/ppermute | solution.py:404
  142.0 1.2 third_stage.1
  143.1 3.0 %collective-permute-start.34 = (bf16[2,128,768]{2,1,0:T(8,128)(2,1)S(1)}, bf16[2,128,768]{2,1,0:T(8,128)(2,1)S(1)}, u32[]{:S(2)}, u32[]{:S(2)}) collective-permute-start(bf16[2,128,768]{2,1,0:T(8,128)(2,1)S(1)} %get-tuple-element.193), channel_id=1, source_target_pairs={{0,8},{1,9},{2,10},{3,11},{4,12},{5,13},{6,14},{7,15},{8,0},{9,1},... | collective-permute-start | bytes 1179656 | tf_op jit(solution)/shard_map/ppermute | solution.py:404
  146.2 1.5 collective-permute-start.33
  148.3 5.1 %collective-permute-done.32.refs_1_ = bf16[4,32,768]{2,1,0:T(8,128)(2,1)S(1)} collective-permute-done((bf16[4,32,768]{2,1,0:T(8,128)(2,1)S(1)}, bf16[4,32,768]{2,1,0:T(8,128)(2,1)S(1)}, u32[]{:S(2)}, u32[]{:S(2)}) %collective-permute-start.32) | collective-permute-done | bytes 196640 | tf_op jit(solution)/shard_map/ppermute | solution.py:404
  154.5 1.8 collective-permute-start.35
  156.3 7.2 %collective-permute-done.35.refs_2_ = bf16[2,80,768]{2,1,0:T(8,128)(2,1)S(1)} collective-permute-done((bf16[2,80,768]{2,1,0:T(8,128)(2,1)S(1)}, bf16[2,80,768]{2,1,0:T(8,128)(2,1)S(1)}, u32[]{:S(2)}, u32[]{:S(2)}) %collective-permute-start.35) | collective-permute-done | bytes 245792 | tf_op jit(solution)/shard_map/ppermute | solution.py:404
  164.1 2.7 %collective-permute-done.37.refs_4_ = bf16[128,768]{1,0:T(8,128)(2,1)S(1)} collective-permute-done((bf16[128,768]{1,0:T(8,128)(2,1)S(1)}, bf16[128,768]{1,0:T(8,128)(2,1)S(1)}, u32[]{:S(2)}, u32[]{:S(2)}) %collective-permute-start.37) | collective-permute-done | bytes 196640 | tf_op jit(solution)/shard_map/ppermute | solution.py:404
  168.2 6.5 %collective-permute-done.42.refs_3_ = bf16[224,768]{1,0:T(8,128)(2,1)S(1)} collective-permute-done((bf16[224,768]{1,0:T(8,128)(2,1)S(1)}, bf16[224,768]{1,0:T(8,128)(2,1)S(1)}, u32[]{:S(2)}, u32[]{:S(2)}) %collective-permute-start.42) | collective-permute-done | bytes 344096 | tf_op jit(solution)/shard_map/ppermute | solution.py:404
  176.2 10.0 %collective-permute-start.38 = (bf16[80,768]{1,0:T(8,128)(2,1)S(1)}, bf16[80,768]{1,0:T(8,128)(2,1)S(1)}, u32[]{:S(2)}, u32[]{:S(2)}) collective-permute-start(bf16[80,768]{1,0:T(8,128)(2,1)S(1)} %get-tuple-element.208.refs_1_), channel_id=1, source_target_pairs={{0,1},{1,0},{2,3},{3,2},{4,5},{5,4},{6,7},{7,6},{8,9},{9,8},{10,11... | collective-permute-start | bytes 368648 | tf_op jit(solution)/shard_map/ppermute | solution.py:404
  186.2 1.6 back_rows.1
  187.8 2.3 %dense_outputs.1 = (f32[384,768]{1,0:T(8,128)}, f32[96,3072]{1,0:T(8,128)}, f32[96,768]{1,0:T(8,128)}, f32[1,96]{1,0:T(1,128)}, f32[1,96]{1,0:T(1,128)}, /*index...) custom-call(s32[4]{0:T(128)S(1)} %pad_add_fusion.refs_0_, ...), custom_call_target="tpu_custom_call" | custom-call | flops 1024 | bytes 1024 | tf_op jit(solution)/shard_map/dense_outputs/pallas_call | solution.py:368
  190.7 1.5 joint_outputs.1
  (137 shorter events, 15.8 us)
Async XLA Ops:
  1.7 6.9 %collective-permute-start.2 = (bf16[128,768]{1,0:T(8,128)(2,1)S(1)}, bf16[128,768]{1,0:T(8,128)(2,1)S(1)}, u32[]{:S(2)}, u32[]{:S(2)}) collective-permute-start(bf16[128,768]{1,0:T(8,128)(2,1)S(1)} %get-tuple-element.227), channel_id=1, source_target_pairs={{0,8},{1,24},{2,10},{3,26},{4,12},{5,28},{6,14},{7,30},{8,0},{9,16... | collective-permute-start | bytes 589832 | tf_op jit(solution)/shard_map/ppermute | solution.py:404
  4.8 6.2 %collective-permute-start.1 = (bf16[128,768]{1,0:T(8,128)(2,1)S(1)}, bf16[128,768]{1,0:T(8,128)(2,1)S(1)}, u32[]{:S(2)}, u32[]{:S(2)}) collective-permute-start(bf16[128,768]{1,0:T(8,128)(2,1)S(1)} %get-tuple-element.228), channel_id=1, source_target_pairs={{0,0},{1,16},{2,2},{3,18},{4,4},{5,20},{6,6},{7,22},{8,8},{9,24},{... | collective-permute-start | bytes 589832 | tf_op jit(solution)/shard_map/ppermute | solution.py:404
  8.6 8.6 %collective-permute-start.6 = (bf16[128,768]{1,0:T(8,128)(2,1)S(1)}, bf16[128,768]{1,0:T(8,128)(2,1)S(1)}, u32[]{:S(2)}, u32[]{:S(2)}) collective-permute-start(bf16[128,768]{1,0:T(8,128)(2,1)S(1)} %collective-permute-done.2.refs_4_.refs_7_.refs_2_), channel_id=1, source_target_pairs={{0,4},{1,5},{2,6},{3,7},{4,0},{5,1},{6,2},{7,3},{8,12},{9,13},{10,... | collective-permute-start | bytes 589832 | tf_op jit(solution)/shard_map/ppermute | solution.py:404
  11.0 8.2 %collective-permute-start.5 = (bf16[128,768]{1,0:T(8,128)(2,1)S(1)}, bf16[128,768]{1,0:T(8,128)(2,1)S(1)}, u32[]{:S(2)}, u32[]{:S(2)}) collective-permute-start(bf16[128,768]{1,0:T(8,128)(2,1)S(1)} %collective-permute-done.1.refs_3_.refs_6_.refs_1_), channel_id=1, source_target_pairs={{0,4},{1,5},{2,6},{3,7},{4,0},{5,1},{6,2},{7,3},{8,12},{9,13},{10,... | collective-permute-start | bytes 589832 | tf_op jit(solution)/shard_map/ppermute | solution.py:404
  11.0 11.2 %collective-permute-start.4 = (bf16[128,768]{1,0:T(8,128)(2,1)S(1)}, bf16[128,768]{1,0:T(8,128)(2,1)S(1)}, u32[]{:S(2)}, u32[]{:S(2)}) collective-permute-start(bf16[128,768]{1,0:T(8,128)(2,1)S(1)} %collective-permute-done.2.refs_4_.refs_7_.refs_2_), channel_id=1, source_target_pairs={{0,1},{1,0},{2,3},{3,2},{4,5},{5,4},{6,7},{7,6},{8,9},{9,8},{10,11... | collective-permute-start | bytes 589832 | tf_op jit(solution)/shard_map/ppermute | solution.py:404
  17.2 5.1 %collective-permute-start.3 = (bf16[128,768]{1,0:T(8,128)(2,1)S(1)}, bf16[128,768]{1,0:T(8,128)(2,1)S(1)}, u32[]{:S(2)}, u32[]{:S(2)}) collective-permute-start(bf16[128,768]{1,0:T(8,128)(2,1)S(1)} %collective-permute-done.1.refs_3_.refs_6_.refs_1_), channel_id=1, source_target_pairs={{0,1},{1,0},{2,3},{3,2},{4,5},{5,4},{6,7},{7,6},{8,9},{9,8},{10,11... | collective-permute-start | bytes 589832 | tf_op jit(solution)/shard_map/ppermute | solution.py:404
  17.2 5.1 %collective-permute-start.8 = (bf16[128,768]{1,0:T(8,128)(2,1)S(1)}, bf16[128,768]{1,0:T(8,128)(2,1)S(1)}, u32[]{:S(2)}, u32[]{:S(2)}) collective-permute-start(bf16[128,768]{1,0:T(8,128)(2,1)S(1)} %collective-permute-done.6.refs_8_.refs_6_), channel_id=1, source_target_pairs={{0,1},{1,0},{2,3},{3,2},{4,5},{5,4},{6,7},{7,6},{8,9},{9,8},{10,11... | collective-permute-start | bytes 589832 | tf_op jit(solution)/shard_map/ppermute | solution.py:404
  19.2 3.1 %collective-permute-start.7 = (bf16[128,768]{1,0:T(8,128)(2,1)S(1)}, bf16[128,768]{1,0:T(8,128)(2,1)S(1)}, u32[]{:S(2)}, u32[]{:S(2)}) collective-permute-start(bf16[128,768]{1,0:T(8,128)(2,1)S(1)} %collective-permute-done.5.refs_7_.refs_5_), channel_id=1, source_target_pairs={{0,1},{1,0},{2,3},{3,2},{4,5},{5,4},{6,7},{7,6},{8,9},{9,8},{10,11... | collective-permute-start | bytes 589832 | tf_op jit(solution)/shard_map/ppermute | solution.py:404
  20.8 1.5 collective-permute-start
  21.5 21.5 %copy-start.21 = (f32[3072]{0:T(1024)S(1)}, f32[3072]{0:T(1024)}, u32[]{:S(2)}) copy-start(f32[3072]{0:T(1024)} %param.26) | copy-start | bytes 36868
  25.2 17.8 %copy-start.2 = (bf16[768,768]{1,0:T(8,128)(2,1)S(1)}, bf16[768,768]{1,0:T(8,128)(2,1)}, u32[]{:S(2)}) copy-start(bf16[768,768]{1,0:T(8,128)(2,1)} %refs_10_.3) | copy-start | bytes 3538948
  36.1 7.0 %collective-permute-start.9 = (bf16[512,384]{1,0:T(8,128)(2,1)S(1)}, bf16[512,384]{1,0:T(8,128)(2,1)S(1)}, u32[]{:S(2)}, u32[]{:S(2)}) collective-permute-start(bf16[512,384]{1,0:T(8,128)(2,1)S(1)} %get-tuple-element.120.refs_1_.refs_7_), channel_id=1, source_target_pairs={{0,1},{1,0},{2,3},{3,2},{4,5},{5,4},{6,7},{7,6},{8,9},{9,8},{10,11... | collective-permute-start | bytes 1179656 | tf_op jit(solution)/shard_map/ppermute | solution.py:404
  36.6 30.6 %slice-start = ((s8[4718592]{0:T(1024)(128)(4,1)}), s8[4194304]{0:T(1024)(128)(4,1)S(1)}, s32[]{:S(2)}) async-start(s8[4718592]{0:T(1024)(128)(4,1)} %bitcast.21), calls=%async_computation | async-start | bytes 8388608
  36.6 6.4 %collective-permute-start.11 = (bf16[128,768]{1,0:T(8,128)(2,1)S(1)}, bf16[128,768]{1,0:T(8,128)(2,1)S(1)}, u32[]{:S(2)}, u32[]{:S(2)}) collective-permute-start(bf16[128,768]{1,0:T(8,128)(2,1)S(1)} %get-tuple-element.225), channel_id=1, source_target_pairs={{0,8},{1,24},{2,10},{3,26},{4,12},{5,28},{6,14},{7,30},{8,0},{9,16... | collective-permute-start | bytes 589832 | tf_op jit(solution)/shard_map/ppermute | solution.py:404
  37.9 5.1 %collective-permute-start.10 = (bf16[128,768]{1,0:T(8,128)(2,1)S(1)}, bf16[128,768]{1,0:T(8,128)(2,1)S(1)}, u32[]{:S(2)}, u32[]{:S(2)}) collective-permute-start(bf16[128,768]{1,0:T(8,128)(2,1)S(1)} %get-tuple-element.226), channel_id=1, source_target_pairs={{0,0},{1,16},{2,2},{3,18},{4,4},{5,20},{6,6},{7,22},{8,8},{9,24},{... | collective-permute-start | bytes 589832 | tf_op jit(solution)/shard_map/ppermute | solution.py:404
  43.0 24.1 %slice-start.1 = ((s8[4718592]{0:T(1024)(128)(4,1)}), s8[524288]{0:T(1024)(128)(4,1)S(1)}, s32[]{:S(2)}) async-start(s8[4718592]{0:T(1024)(128)(4,1)} %bitcast.21), calls=%async_computation.1 | async-start | bytes 1048576
  52.2 9.2 %collective-permute-start.15 = (bf16[16,96,256]{2,1,0:T(8,128)(2,1)S(1)}, bf16[16,96,256]{2,1,0:T(8,128)(2,1)S(1)}, u32[]{:S(2)}, u32[]{:S(2)}) collective-permute-start(bf16[16,96,256]{2,1,0:T(8,128)(2,1)S(1)} %get-tuple-element.133), channel_id=1, source_target_pairs={{0,1},{1,0},{2,3},{3,2},{4,5},{5,4},{6,7},{7,6},{8,9},{9,8},{10,11... | collective-permute-start | bytes 2359304 | tf_op jit(solution)/shard_map/ppermute | solution.py:404
  58.9 2.5 %collective-permute-start.16 = (bf16[272,768]{1,0:T(8,128)(2,1)S(1)}, bf16[272,768]{1,0:T(8,128)(2,1)S(1)}, u32[]{:S(2)}, u32[]{:S(2)}) collective-permute-start(bf16[272,768]{1,0:T(8,128)(2,1)S(1)} %get-tuple-element.127.refs_3_.refs_1_), channel_id=1, source_target_pairs={{0,1},{1,0},{2,3},{3,2},{4,5},{5,4},{6,7},{7,6},{8,9},{9,8},{10,11... | collective-permute-start | bytes 1253384 | tf_op jit(solution)/shard_map/ppermute | solution.py:404
  59.0 8.2 %collective-permute-start.14 = (bf16[256,768]{1,0:T(8,128)(2,1)S(1)}, bf16[256,768]{1,0:T(8,128)(2,1)S(1)}, u32[]{:S(2)}, u32[]{:S(2)}) collective-permute-start(bf16[256,768]{1,0:T(8,128)(2,1)S(1)} %get-tuple-element.126), channel_id=1, source_target_pairs={{0,1},{1,0},{2,3},{3,2},{4,5},{5,4},{6,7},{7,6},{8,9},{9,8},{10,11... | collective-permute-start | bytes 1179656 | tf_op jit(solution)/shard_map/ppermute | solution.py:404
  59.4 7.7 %collective-permute-start.12 = (bf16[128,768]{1,0:T(8,128)(2,1)S(1)}, bf16[128,768]{1,0:T(8,128)(2,1)S(1)}, u32[]{:S(2)}, u32[]{:S(2)}) collective-permute-start(bf16[128,768]{1,0:T(8,128)(2,1)S(1)} %get-tuple-element.123), channel_id=1, source_target_pairs={{0,0},{1,16},{2,2},{3,18},{4,4},{5,20},{6,6},{7,22},{8,8},{9,24},{... | collective-permute-start | bytes 589832 | tf_op jit(solution)/shard_map/ppermute | solution.py:404
  60.1 7.1 %collective-permute-start.13 = (bf16[128,768]{1,0:T(8,128)(2,1)S(1)}, bf16[128,768]{1,0:T(8,128)(2,1)S(1)}, u32[]{:S(2)}, u32[]{:S(2)}) collective-permute-start(bf16[128,768]{1,0:T(8,128)(2,1)S(1)} %get-tuple-element.124), channel_id=1, source_target_pairs={{0,8},{1,24},{2,10},{3,26},{4,12},{5,28},{6,14},{7,30},{8,0},{9,16... | collective-permute-start | bytes 589832 | tf_op jit(solution)/shard_map/ppermute | solution.py:404
  64.0 18.3 %collective-permute-start.20 = (bf16[4,2,48,768]{3,2,1,0:T(8,128)(2,1)S(1)}, bf16[4,2,48,768]{3,2,1,0:T(8,128)(2,1)S(1)}, u32[]{:S(2)}, u32[]{:S(2)}) collective-permute-start(bf16[4,2,48,768]{3,2,1,0:T(8,128)(2,1)S(1)} %get-tuple-element.146), channel_id=1, source_target_pairs={{0,2},{1,3},{2,0},{3,1},{4,6},{5,7},{6,4},{7,5},{8,10},{9,11},{10,... | collective-permute-start | bytes 1769480 | tf_op jit(solution)/shard_map/ppermute | solution.py:404
  65.6 16.8 %collective-permute-start.21 = (bf16[4,2,48,768]{3,2,1,0:T(8,128)(2,1)S(1)}, bf16[4,2,48,768]{3,2,1,0:T(8,128)(2,1)S(1)}, u32[]{:S(2)}, u32[]{:S(2)}) collective-permute-start(bf16[4,2,48,768]{3,2,1,0:T(8,128)(2,1)S(1)} %get-tuple-element.148), channel_id=1, source_target_pairs={{0,4},{1,5},{2,6},{3,7},{4,0},{5,1},{6,2},{7,3},{8,12},{9,13},{10,... | collective-permute-start | bytes 1769480 | tf_op jit(solution)/shard_map/ppermute | solution.py:404
  75.6 6.8 %collective-permute-start.19 = (bf16[272,768]{1,0:T(8,128)(2,1)S(1)}, bf16[272,768]{1,0:T(8,128)(2,1)S(1)}, u32[]{:S(2)}, u32[]{:S(2)}) collective-permute-start(bf16[272,768]{1,0:T(8,128)(2,1)S(1)} %get-tuple-element.142), channel_id=1, source_target_pairs={{0,1},{1,0},{2,3},{3,2},{4,5},{5,4},{6,7},{7,6},{8,9},{9,8},{10,11... | collective-permute-start | bytes 1253384 | tf_op jit(solution)/shard_map/ppermute | solution.py:404
  79.8 1.9 %collective-permute-start.17 = (bf16[256,768]{1,0:T(8,128)(2,1)S(1)}, bf16[256,768]{1,0:T(8,128)(2,1)S(1)}, u32[]{:S(2)}, u32[]{:S(2)}) collective-permute-start(bf16[256,768]{1,0:T(8,128)(2,1)S(1)} %get-tuple-element.138), channel_id=1, source_target_pairs={{0,1},{1,0},{2,3},{3,2},{4,5},{5,4},{6,7},{7,6},{8,9},{9,8},{10,11... | collective-permute-start | bytes 1179656 | tf_op jit(solution)/shard_map/ppermute | solution.py:404
  79.9 2.4 %collective-permute-start.18 = (bf16[256,768]{1,0:T(8,128)(2,1)S(1)}, bf16[256,768]{1,0:T(8,128)(2,1)S(1)}, u32[]{:S(2)}, u32[]{:S(2)}) collective-permute-start(bf16[256,768]{1,0:T(8,128)(2,1)S(1)} %get-tuple-element.139), channel_id=1, source_target_pairs={{0,1},{1,0},{2,3},{3,2},{4,5},{5,4},{6,7},{7,6},{8,9},{9,8},{10,11... | collective-permute-start | bytes 1179656 | tf_op jit(solution)/shard_map/ppermute | solution.py:404
  86.2 26.2 %collective-permute-start.22 = (bf16[4,176,768]{2,1,0:T(8,128)(2,1)S(1)}, bf16[4,176,768]{2,1,0:T(8,128)(2,1)S(1)}, u32[]{:S(2)}, u32[]{:S(2)}) collective-permute-start(bf16[4,176,768]{2,1,0:T(8,128)(2,1)S(1)} %get-tuple-element.150), channel_id=1, source_target_pairs={{0,2},{1,3},{2,0},{3,1},{4,6},{5,7},{6,4},{7,5},{8,10},{9,11},{10,... | collective-permute-start | bytes 3244040 | tf_op jit(solution)/shard_map/ppermute | solution.py:404
  87.7 25.8 %collective-permute-start.23 = (bf16[4,176,768]{2,1,0:T(8,128)(2,1)S(1)}, bf16[4,176,768]{2,1,0:T(8,128)(2,1)S(1)}, u32[]{:S(2)}, u32[]{:S(2)}) collective-permute-start(bf16[4,176,768]{2,1,0:T(8,128)(2,1)S(1)} %get-tuple-element.151), channel_id=1, source_target_pairs={{0,4},{1,5},{2,6},{3,7},{4,0},{5,1},{6,2},{7,3},{8,12},{9,13},{10,... | collective-permute-start | bytes 3244040 | tf_op jit(solution)/shard_map/ppermute | solution.py:404
  101.5 3.5 %collective-permute-start.24 = (bf16[256,768]{1,0:T(8,128)(2,1)S(1)}, bf16[256,768]{1,0:T(8,128)(2,1)S(1)}, u32[]{:S(2)}, u32[]{:S(2)}) collective-permute-start(bf16[256,768]{1,0:T(8,128)(2,1)S(1)} %get-tuple-element.167), channel_id=1, source_target_pairs={{0,1},{1,0},{2,3},{3,2},{4,5},{5,4},{6,7},{7,6},{8,9},{9,8},{10,11... | collective-permute-start | bytes 1179656 | tf_op jit(solution)/shard_map/ppermute | solution.py:404
  114.8 27.2 %collective-permute-start.26 = (bf16[768,768]{1,0:T(8,128)(2,1)S(1)}, bf16[768,768]{1,0:T(8,128)(2,1)S(1)}, u32[]{:S(2)}, u32[]{:S(2)}) collective-permute-start(bf16[768,768]{1,0:T(8,128)(2,1)S(1)} %get-tuple-element.173), channel_id=1, source_target_pairs={{0,4},{1,5},{2,6},{3,7},{4,0},{5,1},{6,2},{7,3},{8,12},{9,13},{10,... | collective-permute-start | bytes 3538952 | tf_op jit(solution)/shard_map/ppermute | solution.py:404
  116.4 22.6 %collective-permute-start.25 = (bf16[640,768]{1,0:T(8,128)(2,1)S(1)}, bf16[640,768]{1,0:T(8,128)(2,1)S(1)}, u32[]{:S(2)}, u32[]{:S(2)}) collective-permute-start(bf16[640,768]{1,0:T(8,128)(2,1)S(1)} %get-tuple-element.172), channel_id=1, source_target_pairs={{0,2},{1,3},{2,0},{3,1},{4,6},{5,7},{6,4},{7,5},{8,10},{9,11},{10,... | collective-permute-start | bytes 2949128 | tf_op jit(solution)/shard_map/ppermute | solution.py:404
  116.9 8.9 %collective-permute-start.28 = (bf16[2,96,768]{2,1,0:T(8,128)(2,1)S(1)}, bf16[2,96,768]{2,1,0:T(8,128)(2,1)S(1)}, u32[]{:S(2)}, u32[]{:S(2)}) collective-permute-start(bf16[2,96,768]{2,1,0:T(8,128)(2,1)S(1)} %get-tuple-element.182), channel_id=1, source_target_pairs={{0,8},{1,9},{2,10},{3,11},{4,12},{5,13},{6,14},{7,15},{8,0},{9,1},... | collective-permute-start | bytes 884744 | tf_op jit(solution)/shard_map/ppermute | solution.py:404
  119.8 8.1 %collective-permute-start.27 = (bf16[256,768]{1,0:T(8,128)(2,1)S(1)}, bf16[256,768]{1,0:T(8,128)(2,1)S(1)}, u32[]{:S(2)}, u32[]{:S(2)}) collective-permute-start(bf16[256,768]{1,0:T(8,128)(2,1)S(1)} %get-tuple-element.179), channel_id=1, source_target_pairs={{0,1},{1,0},{2,3},{3,2},{4,5},{5,4},{6,7},{7,6},{8,9},{9,8},{10,11... | collective-permute-start | bytes 1179656 | tf_op jit(solution)/shard_map/ppermute | solution.py:404
  126.4 8.0 %collective-permute-start.29 = (bf16[96,768]{1,0:T(8,128)(2,1)S(1)}, bf16[96,768]{1,0:T(8,128)(2,1)S(1)}, u32[]{:S(2)}, u32[]{:S(2)}) collective-permute-start(bf16[96,768]{1,0:T(8,128)(2,1)S(1)} %get-tuple-element.185), channel_id=1, source_target_pairs={{0,16},{1,17},{2,18},{3,19},{4,20},{5,21},{6,22},{7,23},{8,24},{9,... | collective-permute-start | bytes 442376 | tf_op jit(solution)/shard_map/ppermute | solution.py:404
  143.1 10.6 %collective-permute-start.34 = (bf16[2,128,768]{2,1,0:T(8,128)(2,1)S(1)}, bf16[2,128,768]{2,1,0:T(8,128)(2,1)S(1)}, u32[]{:S(2)}, u32[]{:S(2)}) collective-permute-start(bf16[2,128,768]{2,1,0:T(8,128)(2,1)S(1)} %get-tuple-element.193), channel_id=1, source_target_pairs={{0,8},{1,9},{2,10},{3,11},{4,12},{5,13},{6,14},{7,15},{8,0},{9,1},... | collective-permute-start | bytes 1179656 | tf_op jit(solution)/shard_map/ppermute | solution.py:404
  146.2 7.2 %collective-permute-start.33 = (bf16[4,48,768]{2,1,0:T(8,128)(2,1)S(1)}, bf16[4,48,768]{2,1,0:T(8,128)(2,1)S(1)}, u32[]{:S(2)}, u32[]{:S(2)}) collective-permute-start(bf16[4,48,768]{2,1,0:T(8,128)(2,1)S(1)} %get-tuple-element.189), channel_id=1, source_target_pairs={{0,4},{1,5},{2,6},{3,7},{4,0},{5,1},{6,2},{7,3},{8,12},{9,13},{10,... | collective-permute-start | bytes 884744 | tf_op jit(solution)/shard_map/ppermute | solution.py:404
  147.7 5.7 %collective-permute-start.32 = (bf16[4,32,768]{2,1,0:T(8,128)(2,1)S(1)}, bf16[4,32,768]{2,1,0:T(8,128)(2,1)S(1)}, u32[]{:S(2)}, u32[]{:S(2)}) collective-permute-start(bf16[4,32,768]{2,1,0:T(8,128)(2,1)S(1)} %get-tuple-element.188), channel_id=1, source_target_pairs={{0,2},{1,3},{2,0},{3,1},{4,6},{5,7},{6,4},{7,5},{8,10},{9,11},{10,... | collective-permute-start | bytes 589832 | tf_op jit(solution)/shard_map/ppermute | solution.py:404
  154.5 9.0 %collective-permute-start.35 = (bf16[2,80,768]{2,1,0:T(8,128)(2,1)S(1)}, bf16[2,80,768]{2,1,0:T(8,128)(2,1)S(1)}, u32[]{:S(2)}, u32[]{:S(2)}) collective-permute-start(bf16[2,80,768]{2,1,0:T(8,128)(2,1)S(1)} %get-tuple-element.196), channel_id=1, source_target_pairs={{0,8},{1,9},{2,10},{3,11},{4,12},{5,13},{6,14},{7,15},{8,0},{9,1},... | collective-permute-start | bytes 737288 | tf_op jit(solution)/shard_map/ppermute | solution.py:404
  156.3 10.5 %collective-permute-start.37 = (bf16[128,768]{1,0:T(8,128)(2,1)S(1)}, bf16[128,768]{1,0:T(8,128)(2,1)S(1)}, u32[]{:S(2)}, u32[]{:S(2)}) collective-permute-start(bf16[128,768]{1,0:T(8,128)(2,1)S(1)} %get-tuple-element.202), channel_id=1, source_target_pairs={{0,16},{1,17},{2,18},{3,19},{4,20},{5,21},{6,22},{7,23},{8,24},{9,... | collective-permute-start | bytes 589832 | tf_op jit(solution)/shard_map/ppermute | solution.py:404
  167.4 7.3 %collective-permute-start.42 = (bf16[224,768]{1,0:T(8,128)(2,1)S(1)}, bf16[224,768]{1,0:T(8,128)(2,1)S(1)}, u32[]{:S(2)}, u32[]{:S(2)}) collective-permute-start(bf16[224,768]{1,0:T(8,128)(2,1)S(1)} %get-tuple-element.209.refs_1_), channel_id=1, source_target_pairs={{0,2},{1,3},{2,0},{3,1},{4,6},{5,7},{6,4},{7,5},{8,10},{9,11},{10,... | collective-permute-start | bytes 1032200 | tf_op jit(solution)/shard_map/ppermute | solution.py:404
  167.5 7.9 %collective-permute-start.36 = (bf16[80,768]{1,0:T(8,128)(2,1)S(1)}, bf16[80,768]{1,0:T(8,128)(2,1)S(1)}, u32[]{:S(2)}, u32[]{:S(2)}) collective-permute-start(bf16[80,768]{1,0:T(8,128)(2,1)S(1)} %get-tuple-element.199), channel_id=1, source_target_pairs={{0,16},{1,17},{2,18},{3,19},{4,20},{5,21},{6,22},{7,23},{8,24},{9,... | collective-permute-start | bytes 368648 | tf_op jit(solution)/shard_map/ppermute | solution.py:404
  168.2 19.6 %collective-permute-start.41 = (bf16[224,768]{1,0:T(8,128)(2,1)S(1)}, bf16[224,768]{1,0:T(8,128)(2,1)S(1)}, u32[]{:S(2)}, u32[]{:S(2)}) collective-permute-start(bf16[224,768]{1,0:T(8,128)(2,1)S(1)} %get-tuple-element.209.refs_1_), channel_id=1, source_target_pairs={{0,1},{1,0},{2,3},{3,2},{4,5},{5,4},{6,7},{7,6},{8,9},{9,8},{10,11... | collective-permute-start | bytes 1032200 | tf_op jit(solution)/shard_map/ppermute | solution.py:404
  174.7 13.1 %collective-permute-start.43 = (bf16[224,768]{1,0:T(8,128)(2,1)S(1)}, bf16[224,768]{1,0:T(8,128)(2,1)S(1)}, u32[]{:S(2)}, u32[]{:S(2)}) collective-permute-start(bf16[224,768]{1,0:T(8,128)(2,1)S(1)} %collective-permute-done.42.refs_3_), channel_id=1, source_target_pairs={{0,1},{1,0},{2,3},{3,2},{4,5},{5,4},{6,7},{7,6},{8,9},{9,8},{10,11... | collective-permute-start | bytes 1032200 | tf_op jit(solution)/shard_map/ppermute | solution.py:404
  174.7 1.4 collective-permute-start.30
  176.0 10.2 %collective-permute-start.39 = (bf16[80,768]{1,0:T(8,128)(2,1)S(1)}, bf16[80,768]{1,0:T(8,128)(2,1)S(1)}, u32[]{:S(2)}, u32[]{:S(2)}) collective-permute-start(bf16[80,768]{1,0:T(8,128)(2,1)S(1)} %get-tuple-element.208.refs_1_), channel_id=1, source_target_pairs={{0,2},{1,3},{2,0},{3,1},{4,6},{5,7},{6,4},{7,5},{8,10},{9,11},{10,... | collective-permute-start | bytes 368648 | tf_op jit(solution)/shard_map/ppermute | solution.py:404
  176.1 10.1 %collective-permute-start.31 = (bf16[128,768]{1,0:T(8,128)(2,1)S(1)}, bf16[128,768]{1,0:T(8,128)(2,1)S(1)}, u32[]{:S(2)}, u32[]{:S(2)}) collective-permute-start(bf16[128,768]{1,0:T(8,128)(2,1)S(1)} %get-tuple-element.187), channel_id=1, source_target_pairs={{0,8},{1,24},{2,10},{3,26},{4,12},{5,28},{6,14},{7,30},{8,0},{9,16... | collective-permute-start | bytes 589832 | tf_op jit(solution)/shard_map/ppermute | solution.py:404
  176.2 14.5 %collective-permute-start.38 = (bf16[80,768]{1,0:T(8,128)(2,1)S(1)}, bf16[80,768]{1,0:T(8,128)(2,1)S(1)}, u32[]{:S(2)}, u32[]{:S(2)}) collective-permute-start(bf16[80,768]{1,0:T(8,128)(2,1)S(1)} %get-tuple-element.208.refs_1_), channel_id=1, source_target_pairs={{0,1},{1,0},{2,3},{3,2},{4,5},{5,4},{6,7},{7,6},{8,9},{9,8},{10,11... | collective-permute-start | bytes 368648 | tf_op jit(solution)/shard_map/ppermute | solution.py:404
  186.2 4.5 %collective-permute-start.40 = (bf16[80,768]{1,0:T(8,128)(2,1)S(1)}, bf16[80,768]{1,0:T(8,128)(2,1)S(1)}, u32[]{:S(2)}, u32[]{:S(2)}) collective-permute-start(bf16[80,768]{1,0:T(8,128)(2,1)S(1)} %collective-permute-done.39.refs_3_), channel_id=1, source_target_pairs={{0,1},{1,0},{2,3},{3,2},{4,5},{5,4},{6,7},{7,6},{8,9},{9,8},{10,11... | collective-permute-start | bytes 368648 | tf_op jit(solution)/shard_map/ppermute | solution.py:404
  (29 other events, 244.0 us)

commit v3 on v2

--- a/solution.py
+++ b/solution.py
@@ -326,6 +326,7 @@
 UP_ROWS = 128
 DOWN_ROWS = 96
 EXT = OWN + 16
+DOWN_SENT = 2 * DOWN_ROWS
 FLOAT = jnp.float32
 LOW = jnp.bfloat16
 AXES = ("seq", "rows")
@@ -355,7 +356,7 @@
     return lax.dot_general(left, right, (((1,), (1,)), ((), ())), preferred_element_type=FLOAT)
 
 
-def call(kernel, name, place, inputs, outputs, scratch=(), grid=(1,), scalars=(), after=(), megabytes=40, work=None):
+def call(kernel, name, place, inputs, outputs, scratch=(), grid=(1,), scalars=(), after=(), megabytes=28, work=None, aliases=()):
     prefetch = 1 + len(scalars)
     given, made = len(inputs), len(outputs)
 
@@ -377,6 +378,7 @@
         out_shape=[shaped(shape, kind) for shape, kind, _ in outputs] + [shaped((8, LANES), FLOAT)],
         compiler_params=kernel_params(megabytes),
         cost_estimate=work,
+        input_output_aliases={prefetch + source: target for source, target in aliases},
         name=name,
     )(place, *scalars, *[array for array, _ in inputs], *after)
     return results[:-1], results[-1]
@@ -459,78 +461,120 @@
     return lax.broadcasted_iota(jnp.int32, (rows, LANES), 1) < HEAD_DIM
 
 
-def attention_kernel(
-    place, own_lengths, peer_lengths, *refs
+def first_attention_kernel(
+    place, own_lengths, peer_lengths, t0, t1, t2, t3, wq, wk, wv, qb, vb, q_out, k_out, v_out, summed, highest_out, bias
 ):
-    blocks = refs[:8]
-    wq, wk, wv, qb, vb = refs[8:13]
-    att_out, q_out, k_out, v_out, log_out = refs[13:18]
-    bias, log_columns = refs[18:]
     bases = first_positions(place)
     ends = pair_ends(place, own_lengths, peer_lengths)
-    here = jnp.concatenate([block[...] for block in blocks[:4]], axis=0)
-    there = jnp.concatenate([block[...] for block in blocks[4:]], axis=0)
-    queries = dot(here, wq[...]) + qb[...]
+    tokens = jnp.concatenate([block[...] for block in (t0, t1, t2, t3)], axis=0)
+    queries = dot(tokens, wq[...]) + qb[...]
     q_out[...] = (queries.astype(LOW).astype(FLOAT) * HEAD_DIM**-0.5).astype(LOW)
-    for index, tokens in enumerate((here, there)):
-        rows = pl.ds(index * 512, 512)
-        k_out[rows, :] = dot(tokens, wk[...]).astype(LOW)
-        v_out[rows, :] = (dot(tokens, wv[...]) + vb[...]).astype(LOW)
-    key_ids = [pairs_along(base, ends, 1)[0:1] for base in bases]
-    for i in range(4):
-        query_ids = pairs_along(bases[i], ends, 0)
-        for j in range(8):
-            bias[pl.ds(i * BLOCK, BLOCK), pl.ds(j * BLOCK, BLOCK)] = jnp.where(
-                query_ids == key_ids[j], 0.0, NEGATIVE
-            )
-    log_columns[...] = jnp.zeros_like(log_columns)
+    k_out[...] = dot(tokens, wk[...]).astype(LOW)
+    v_out[...] = (dot(tokens, wv[...]) + vb[...]).astype(LOW)
+    fill_bias(bias, bases[:4], bases[:4], ends)
     for pair in range(PAIRS_OF_HEADS):
         lanes = pl.ds(pair * LANES, LANES)
         keys = k_out[:, lanes]
-        values = v_out[:, lanes]
-        ones = jnp.ones_like(values)
-        left_keys = head_mask(1024)
-        values_of = (jnp.where(left_keys, values, ones), jnp.where(left_keys, ones, values))
-        left = head_mask(OWN)
+        values_of = with_ones(v_out[:, lanes])
         for part in range(2):
             rows = pl.ds(part * OWN, OWN)
-            queries = q_out[rows, lanes]
-            zeros = jnp.zeros_like(queries)
-            summed = []
+            chosen = halves_of(q_out[rows, lanes])
             for half in range(2):
-                chosen = jnp.where(left, queries, zeros) if half == 0 else jnp.where(left, zeros, queries)
-                scores = dot_nt(chosen, keys) + bias[rows, :]
+                scores = dot_nt(chosen[half], keys) + bias[rows, :]
                 highest = jnp.max(scores, axis=1, keepdims=True)
-                weights = jnp.exp(scores - highest).astype(LOW)
-                total = dot(weights, values_of[half])
-                turned = pltpu.roll(total, HEAD_DIM, 1)
-                summed.append(total / turned)
-                sums = total if half == 1 else turned
-                log_total = highest + jnp.log(sums)
-                column = lax.broadcasted_iota(jnp.int32, (OWN, LANES), 1) == pair * 2 + half
-                at = log_total if pair * 2 + half < HEAD_DIM else None
-                log_columns[rows, :] = jnp.where(column, at, log_columns[rows, :])
-            attended = jnp.where(left, summed[0], summed[1]).astype(LOW)
-            att_out[rows, lanes] = attended
-    log_out[...] = jnp.transpose(log_columns[...])[0:8, :]
-
-
-def attention(place, lengths, blocks, joint_weight, query_bias, value_bias, after=()):
+                summed[2 * pair + half, rows, :] = dot(jnp.exp(scores - highest).astype(LOW), values_of[half])
+                highest_out[2 * pair + half, rows, :] = jnp.broadcast_to(highest, (OWN, LANES))
+
+
+def fill_bias(bias, query_bases, key_bases, ends):
+    key_ids = [pairs_along(base, ends, 1)[0:1] for base in key_bases]
+    for i, base in enumerate(query_bases):
+        query_ids = pairs_along(base, ends, 0)
+        for j in range(len(key_bases)):
+            bias[pl.ds(i * BLOCK, BLOCK), pl.ds(j * BLOCK, BLOCK)] = jnp.where(query_ids == key_ids[j], 0.0, NEGATIVE)
+
+
+def halves_of(array):
+    left = head_mask(array.shape[0])
+    zeros = jnp.zeros_like(array)
+    return jnp.where(left, array, zeros), jnp.where(left, zeros, array)
+
+
+def with_ones(values):
+    left = head_mask(values.shape[0])
+    ones = jnp.ones_like(values)
+    return jnp.where(left, values, ones), jnp.where(left, ones, values)
+
+
+def first_attention(place, lengths, blocks, joint_weight, query_bias, value_bias, after=()):
     def columns(kind):
         return joint_weight, pl.BlockSpec((WIDTH, HALF), lambda i, place, *_: (0, 2 * kind + place[3]))
 
     half_row = pl.BlockSpec((1, HALF), lambda i, place, *_: (0, place[3]))
+    state = made((HEADS // 2, 512, LANES), FLOAT)
+    return call(
+        first_attention_kernel,
+        "first_attention",
+        place,
+        [plain(block) for block in blocks]
+        + [columns(0), columns(1), columns(2), (row_of(query_bias), half_row), (row_of(value_bias), half_row)],
+        [made((512, HALF), LOW)] * 3 + [state, state],
+        scratch=[pltpu.VMEM((512, 512), FLOAT)],
+        scalars=lengths,
+        after=after,
+        work=cost(4e9, 8e6, 3e6),
+    )
+
+
+def attention_kernel(
+    place, own_lengths, peer_lengths, t0, t1, t2, t3, wk, wv, vb, q, summed_in, highest_in,
+    att_out, k_out, v_out, log_out, bias, log_columns,
+):
+    bases = first_positions(place)
+    ends = pair_ends(place, own_lengths, peer_lengths)
+    tokens = jnp.concatenate([block[...] for block in (t0, t1, t2, t3)], axis=0)
+    k_out[...] = dot(tokens, wk[...]).astype(LOW)
+    v_out[...] = (dot(tokens, wv[...]) + vb[...]).astype(LOW)
+    fill_bias(bias, bases[:4], bases[4:], ends)
+    log_columns[...] = jnp.zeros_like(log_columns)
+    column = lax.broadcasted_iota(jnp.int32, (OWN, LANES), 1)
+    left = head_mask(OWN)
+    for pair in range(PAIRS_OF_HEADS):
+        lanes = pl.ds(pair * LANES, LANES)
+        keys = k_out[:, lanes]
+        values_of = with_ones(v_out[:, lanes])
+        for part in range(2):
+            rows = pl.ds(part * OWN, OWN)
+            chosen = halves_of(q[rows, lanes])
+            results = []
+            for half in range(2):
+                head = 2 * pair + half
+                scores = dot_nt(chosen[half], keys) + bias[rows, :]
+                before = highest_in[head, rows, :]
+                highest = jnp.maximum(before, jnp.max(scores, axis=1, keepdims=True))
+                weights = jnp.exp(scores - highest[:, 0:1]).astype(LOW)
+                total = dot(weights, values_of[half]) + jnp.exp(before - highest) * summed_in[head, rows, :]
+                turned = pltpu.roll(total, HEAD_DIM, 1)
+                results.append(total / turned)
+                log_total = highest + jnp.log(total if half == 1 else turned)
+                log_columns[rows, :] = jnp.where(column == head, log_total, log_columns[rows, :])
+            att_out[rows, lanes] = jnp.where(left, results[0], results[1]).astype(LOW)
+    log_out[...] = jnp.transpose(log_columns[...])[0:8, :]
+
+
+def attention(place, lengths, blocks, joint_weight, value_bias, q, summed, highest, after=()):
+    def columns(kind):
+        return joint_weight, pl.BlockSpec((WIDTH, HALF), lambda i, place, *_: (0, 2 * kind + place[3]))
+
+    half_row = pl.BlockSpec((1, HALF), lambda i, place, *_: (0, place[3]))
     return call(
         attention_kernel,
         "attention",
         place,
         [plain(block) for block in blocks]
-        + [columns(0), columns(1), columns(2), (row_of(query_bias), half_row), (row_of(value_bias), half_row)],
-        [
-            made((512, HALF), LOW), made((512, HALF), LOW), made((1024, HALF), LOW), made((1024, HALF), LOW),
-            made((8, 512), FLOAT),
-        ],
-        scratch=[pltpu.VMEM((512, 1024), FLOAT), pltpu.VMEM((512, LANES), FLOAT)],
+        + [columns(1), columns(2), (row_of(value_bias), half_row), plain(q), plain(summed), plain(highest)],
+        [made((512, HALF), LOW)] * 3 + [made((8, 512), FLOAT)],
+        scratch=[pltpu.VMEM((512, 512), FLOAT), pltpu.VMEM((512, LANES), FLOAT)],
         scalars=lengths,
         after=after,
         work=cost(4e9, 8e6, 3e6),
@@ -771,8 +815,7 @@
 
 def up_kernel(
     place, normed_t, normed_got, inner0, inner1, got0, got1, att_t, branch, misc, sums0, sums1, feed_got,
-    down_px, down_px_got, down_qy, down_qy_got,
-    x_send, y_send, px, qy, down_p, down_q, units, normed_got_t,
+    x_send, y_send, px, qy, units, normed_got_t,
 ):
     z = pl.program_id(0)
     y, x = place[1], place[2]
@@ -793,26 +836,16 @@
                 [grad[line * 96 : line * 96 + 96], rest, vectors], axis=0
             ).astype(LOW)
     half = UP_ROWS // 2
-    for line in range(2):
-        px[0, line] = units[line, x, 0:half]
-        x_send[0, line * half : line * half + half] = units[line, 1 - x, 0:half]
-    for side in range(2):
-        qy[0, side] = units[y, side, half:]
-        y_send[0, side * half : side * half + half] = units[1 - y, side, half:]
-    down_p[0] = added(down_px[0, y], down_px_got[0, y])
-    y_send[0, 2 * half :] = added(down_px[0, 1 - y], down_px_got[0, 1 - y])
-    down_q[0] = added(down_qy[0, x], down_qy_got[0, x])
-    x_send[0, 2 * half :] = added(down_qy[0, 1 - x], down_qy_got[0, 1 - x])
-
-
-def up_units(
-    place, normed_t, normed_got, inner, got, att_t, branch, misc, sums0, sums1, feed_got, down_pair, after=()
-):
+    for index in range(2):
+        rows = pl.ds(pl.multiple_of(DOWN_SENT + (z * 2 + index) * half, half), half)
+        px[0, index] = units[index, x, 0:half]
+        x_send[rows, :] = units[index, 1 - x, 0:half]
+        qy[0, index] = units[y, index, half:]
+        y_send[rows, :] = units[1 - y, index, half:]
+
+
+def up_units(place, normed_t, normed_got, inner, got, att_t, branch, misc, sums0, sums1, feed_got, after=()):
     rows = pl.BlockSpec((192, OWN), lambda i, place: (i, 0))
-    down_half = DOWN_ROWS // 2
-    block = pl.BlockSpec((1, 2, down_half, WIDTH), lambda i, place: (i, 0, 0, 0))
-    sent = ((4, UP_ROWS + down_half, WIDTH), LOW, pl.BlockSpec((1, UP_ROWS + down_half, WIDTH), lambda i, place: (i, 0, 0)))
-    down = ((4, down_half, WIDTH), LOW, pl.BlockSpec((1, down_half, WIDTH), lambda i, place: (i, 0, 0)))
     return call(
         up_kernel,
         "up_units",
@@ -821,9 +854,8 @@
             (normed_t, rows), plain(normed_got), plain(inner[0]), plain(inner[1]), plain(got[0]), plain(got[1]),
             (att_t, pl.BlockSpec((192, 512), lambda i, place: (i, 0))),
             plain(branch), plain(misc), plain(sums0), plain(sums1), plain(feed_got),
-        ]
-        + [(array, block) for array in down_pair],
-        [sent, sent] + unit_outputs(UP_ROWS, WIDTH)[:2] + [down, down],
+        ],
+        [made((DOWN_SENT + 4 * UP_ROWS, WIDTH), LOW)] * 2 + unit_outputs(UP_ROWS, WIDTH)[:2],
         scratch=[pltpu.VMEM((2, 2, UP_ROWS, WIDTH), LOW), pltpu.VMEM((WIDTH, OWN), LOW)],
         grid=(4,),
         after=after,
@@ -832,7 +864,7 @@
 
 
 def attention_back_kernel(
-    place, own_lengths, peer_lengths, q, k, v, log_total, att, back0, misc,
+    place, own_lengths, peer_lengths, q, k0, k1, v0, v1, log_total, att, back0, misc,
     dq_out, dk_out, dv_out, bias,
 ):
     bases = first_positions(place)
@@ -846,8 +878,8 @@
             )
     for pair in range(PAIRS_OF_HEADS):
         lanes = pl.ds(pair * LANES, LANES)
-        keys = k[:, lanes]
-        values = v[:, lanes]
+        keys = jnp.concatenate([k0[:, lanes], k1[:, lanes]], axis=0)
+        values = jnp.concatenate([v0[:, lanes], v1[:, lanes]], axis=0)
         keys_t = jnp.transpose(keys.astype(FLOAT)).astype(LOW)
         key_grad = jnp.zeros((1024, LANES), FLOAT)
         value_grad = jnp.zeros((1024, LANES), FLOAT)
@@ -879,12 +911,12 @@
         dv_out[:, lanes] = value_grad.astype(LOW)
 
 
-def attention_back(place, lengths, q, k, v, log_total, att, back_own, misc, after=()):
+def attention_back(place, lengths, q, keys, values, log_total, att, back_own, misc, after=()):
     return call(
         attention_back_kernel,
         "attention_back",
         place,
-        [plain(array) for array in (q, k, v, log_total, att, back_own, misc)],
+        [plain(array) for array in (q, *keys, *values, log_total, att, back_own, misc)],
         [made((512, HALF), LOW), made((1024, HALF), LOW), made((1024, HALF), LOW)],
         scratch=[pltpu.VMEM((1024, 512), FLOAT)],
         scalars=lengths,
@@ -917,6 +949,25 @@
     )
 
 
+def token_last_kernel(place, own, own_got, across, first_grad, token0, token1):
+    total = own[...].astype(FLOAT) + own_got[...].astype(FLOAT) + across[8 * JOINT_SECOND :].astype(FLOAT) + first_grad[...]
+    total = total.astype(LOW)
+    token0[...] = total[0:BLOCK]
+    token1[...] = total[BLOCK:]
+
+
+def token_last(place, arrays, after=()):
+    return call(
+        token_last_kernel,
+        "token_last",
+        place,
+        [plain(array) for array in arrays],
+        [made((BLOCK, WIDTH), LOW)] * 2,
+        after=after,
+        work=cost(1e6, 2e6),
+    )
+
+
 def back_rows_kernel(place, done0, done1, back0, back1, outputs, token_grad):
     odd = place[0] % 2
     outputs[odd] = done0[...]
@@ -938,9 +989,10 @@
 
 
 def joint_kernel(
-    place, t0, t1, t2, t3, t4, t5, t6, t7, dq, dk, dv, px_send, px, qy_send, qy, tokens_t, units
+    place, t0, t1, t2, t3, t4, t5, t6, t7, dq, dk, dv, far, far_got, px_send, px, qy_send, qy, tokens_t, units
 ):
     y, x = place[1], place[2]
+    qy_send[pl.ds(8 * JOINT_SECOND, OWN), :] = added(far[...], far_got[...])
     for index, block in enumerate((t0, t1, t2, t3, t4, t5, t6, t7)):
         tokens_t[:, pl.ds(index * BLOCK, BLOCK)] = jnp.transpose(block[...].astype(FLOAT)).astype(LOW)
     biases = jnp.concatenate([column_sum(dq[...].astype(FLOAT)), column_sum(dv[...].astype(FLOAT))], axis=1)
@@ -963,17 +1015,17 @@
             px_send[z, line] = units[line, 1 - x, 0:JOINT_FIRST]
         for side in range(2):
             qy[z, side] = units[y, side, JOINT_FIRST:]
-            qy_send[z, side] = units[1 - y, side, JOINT_FIRST:]
-
-
-def joint_units(place, blocks, dq, dk, dv, after=()):
+            qy_send[pl.ds((z * 2 + side) * JOINT_SECOND, JOINT_SECOND), :] = units[1 - y, side, JOINT_FIRST:]
+
+
+def joint_units(place, blocks, dq, dk, dv, far, far_got, after=()):
     first, second = made((4, 2, JOINT_FIRST, WIDTH), LOW), made((4, 2, JOINT_SECOND, WIDTH), LOW)
     return call(
         joint_kernel,
         "joint_units",
         place,
-        [plain(array) for array in (*blocks, dq, dk, dv)],
-        [first, first, second, second],
+        [plain(array) for array in (*blocks, dq, dk, dv, far, far_got)],
+        [first, first, made((8 * JOINT_SECOND + OWN, WIDTH), LOW), second],
         scratch=[pltpu.VMEM((WIDTH, 1024), LOW), pltpu.VMEM((2, 2, JOINT_ROWS, WIDTH), LOW)],
         after=after,
         work=cost(1.5e9, 6e6),
@@ -984,115 +1036,137 @@
     return (left.astype(FLOAT) + right.astype(FLOAT)).astype(LOW)
 
 
+def down_pair_kernel(place, px, px_got, qy, qy_got, x_in, y_in, x_send, y_send, p, q):
+    y, x = place[1], place[2]
+    p[0] = added(px[0, y], px_got[0, y])
+    y_send[...] = added(px[0, 1 - y], px_got[0, 1 - y])
+    q[0] = added(qy[0, x], qy_got[0, x])
+    x_send[...] = added(qy[0, 1 - x], qy_got[0, 1 - x])
+
+
+def down_pair_stage(place, arrays, x_send, y_send, after=()):
+    half = DOWN_ROWS // 2
+    block = pl.BlockSpec((1, 2, half, WIDTH), lambda i, place: (i, 0, 0, 0))
+    sent = (x_send.shape, LOW, pl.BlockSpec((half, WIDTH), lambda i, place: (i, 0)))
+    kept = ((4, half, WIDTH), LOW, pl.BlockSpec((1, half, WIDTH), lambda i, place: (i, 0, 0)))
+    anywhere = pl.BlockSpec(memory_space=pl.ANY)
+    return call(
+        down_pair_kernel,
+        "down_pair_stage",
+        place,
+        [(array, block) for array in arrays] + [(x_send, anywhere), (y_send, anywhere)],
+        [sent, sent, kept, kept],
+        grid=(4,),
+        after=after,
+        work=cost(1e6, 1e7),
+        aliases=((4, 0), (5, 1)),
+    )
+
+
 def second_kernel(
-    place, x_got, y_got, px, qy, down_p, down_q, far, far_got, joint_px, joint_qy,
-    x_send, y_send, p, q, down_send, down_keep,
+    place, x_got, y_got, px, qy, down_p, down_q, x_send, y_send, p, q, down_send, down_keep
 ):
     z_here, y, x = place[0], place[1], place[2]
     half = UP_ROWS // 2
-    down_at = UP_ROWS
     for z in range(4):
         for got, have, own, keep, send in ((x_got, px, y, p, y_send), (y_got, qy, x, q, x_send)):
-            mine = pl.ds(pl.multiple_of(own * half, half), half)
-            other = pl.ds(pl.multiple_of((1 - own) * half, half), half)
-            keep[z] = added(have[z, own], got[z, mine])
-            send[pl.ds(z * half, half), :] = added(have[z, 1 - own], got[z, other])
-        for other in range(2):
-            at = z * 2 + other
-            x_send[pl.ds(OWN + at * JOINT_FIRST, JOINT_FIRST), :] = joint_px[z, other]
-            y_send[pl.ds(2 * OWN + at * JOINT_SECOND, JOINT_SECOND), :] = joint_qy[z, other]
-    y_send[pl.ds(OWN, OWN), :] = added(far[...], far_got[...])
+            at = DOWN_SENT + z * UP_ROWS
+            mine = pl.ds(pl.multiple_of(at + own * half, half), half)
+            other = pl.ds(pl.multiple_of(at + (1 - own) * half, half), half)
+            keep[z] = added(have[z, own], got[mine, :])
+            send[pl.ds(z * half, half), :] = added(have[z, 1 - own], got[other, :])
     low = z_here % 2
     small = DOWN_ROWS // 2
     for target, parity in ((down_keep, low), (down_send, 1 - low)):
         for high in range(2):
             index = 2 * high + parity
-            target[high, 0:small] = added(down_p[index], y_got[index, down_at:])
-            target[high, small:] = added(down_q[index], x_got[index, down_at:])
-
-
-def second_stage(place, x_got, y_got, px, qy, down_p, down_q, far, far_got, joint_px, joint_qy, after=()):
+            rows = pl.ds(pl.multiple_of(index * small, small), small)
+            target[high, 0:small] = added(down_p[index], y_got[rows, :])
+            target[high, small:] = added(down_q[index], x_got[rows, :])
+
+
+def second_stage(place, arrays, after=()):
     kept = made((4, UP_ROWS // 2, WIDTH), LOW)
     down = made((2, DOWN_ROWS, WIDTH), LOW)
     return call(
         second_kernel,
         "second_stage",
         place,
-        [plain(array) for array in (x_got, y_got, px, qy, down_p, down_q, far, far_got, joint_px, joint_qy)],
-        [
-            made((OWN + 8 * JOINT_FIRST, WIDTH), LOW), made((2 * OWN + 8 * JOINT_SECOND, WIDTH), LOW),
-            kept, kept, down, down,
-        ],
+        [plain(array) for array in arrays],
+        [made((OWN, WIDTH), LOW), made((OWN, WIDTH), LOW), kept, kept, down, down],
         after=after,
         work=cost(1e6, 1e7),
     )
 
 
-def third_kernel(
-    place, x_got, y_got, p, q, px, qy, own, own_got, first_grad,
-    x_send, y_send, joint_p, joint_q, up_send, up_keep, token0, token1,
-):
-    z_here, y, x = place[0], place[1], place[2]
+def joint_pair_kernel(place, px, px_got, qy, qy_got, x_send, y_send, p, q):
+    y, x = place[1], place[2]
+    for z in range(4):
+        p[z] = added(px[z, y], px_got[z, y])
+        y_send[z] = added(px[z, 1 - y], px_got[z, 1 - y])
+
+
+        def from_y(side):
+            return qy_got[pl.ds(pl.multiple_of((z * 2 + side) * JOINT_SECOND, 32), JOINT_SECOND), :]
+
+        q[z] = added(qy[z, x], from_y(x))
+        x_send[z] = added(qy[z, 1 - x], from_y(1 - x))
+
+
+def joint_pair_stage(place, arrays, after=()):
+    first, second = made((4, JOINT_FIRST, WIDTH), LOW), made((4, JOINT_SECOND, WIDTH), LOW)
+    return call(
+        joint_pair_kernel,
+        "joint_pair_stage",
+        place,
+        [plain(array) for array in arrays],
+        [second, first, first, second],
+        after=after,
+        work=cost(1e6, 1e7),
+    )
+
+
+def up_line_kernel(place, x_got, y_got, p, q, down_two, down_got, send, keep, down_send, down_keep):
+    low, high_here = place[0] % 2, place[0] // 2
     half = UP_ROWS // 2
-    for z in range(4):
-
-        def from_x(line):
-            at = OWN + (z * 2 + line) * JOINT_FIRST
-            return x_got[pl.ds(pl.multiple_of(at, 16), JOINT_FIRST), :]
-
-        def from_y(side):
-            at = 2 * OWN + (z * 2 + side) * JOINT_SECOND
-            return y_got[pl.ds(pl.multiple_of(at, 16), JOINT_SECOND), :]
-
-        joint_p[z] = added(px[z, y], from_x(y))
-        y_send[z] = added(px[z, 1 - y], from_x(1 - y))
-        joint_q[z] = added(qy[z, x], from_y(x))
-        x_send[z] = added(qy[z, 1 - x], from_y(1 - x))
-    low = z_here % 2
-    for target, parity in ((up_keep, low), (up_send, 1 - low)):
+    for target, parity in ((keep, low), (send, 1 - low)):
         for high in range(2):
             index = 2 * high + parity
             rows = pl.ds(pl.multiple_of(index * half, half), half)
             target[high, 0:half] = added(p[index], y_got[rows, :])
             target[high, half:] = added(q[index], x_got[rows, :])
-    across = y_got[pl.ds(OWN, OWN), :].astype(FLOAT)
-    total = own[...].astype(FLOAT) + own_got[...].astype(FLOAT) + across + first_grad[...]
-    total = total.astype(LOW)
-    token0[...] = total[0:BLOCK]
-    token1[...] = total[BLOCK:]
-
-
-def third_stage(place, arrays, after=()):
-    joint = [made((4, JOINT_SECOND, WIDTH), LOW), made((4, JOINT_FIRST, WIDTH), LOW)]
-    return call(
-        third_kernel,
-        "third_stage",
+    down_keep[...] = added(down_two[high_here], down_got[high_here])
+    down_send[...] = added(down_two[1 - high_here], down_got[1 - high_here])
+
+
+def up_line_stage(place, arrays, after=()):
+    return call(
+        up_line_kernel,
+        "up_line_stage",
         place,
         [plain(array) for array in arrays],
-        joint + joint[::-1] + [made((2, UP_ROWS, WIDTH), LOW)] * 2 + [made((BLOCK, WIDTH), LOW)] * 2,
+        [made((2, UP_ROWS, WIDTH), LOW)] * 2 + [made((DOWN_ROWS, WIDTH), LOW)] * 2,
         after=after,
         work=cost(1e6, 1e7),
     )
 
 
-def fourth_kernel(place, x_got, y_got, p, q, keep_two, got, send, keep, up_send, up_keep):
-    low, high_here = place[0] % 2, place[0] // 2
+def joint_line_kernel(place, x_got, y_got, p, q, send, keep):
+    low = place[0] % 2
     for target, parity in ((keep, low), (send, 1 - low)):
         for high in range(2):
             index = 2 * high + parity
             target[high, 0:JOINT_FIRST] = added(p[index], y_got[index])
             target[high, JOINT_FIRST:] = added(q[index], x_got[index])
-    up_keep[...] = added(keep_two[high_here], got[high_here])
-    up_send[...] = added(keep_two[1 - high_here], got[1 - high_here])
-
-
-def fourth_stage(place, arrays, after=()):
-    return call(
-        fourth_kernel,
-        "fourth_stage",
+
+
+def joint_line_stage(place, arrays, after=()):
+    return call(
+        joint_line_kernel,
+        "joint_line_stage",
         place,
         [plain(array) for array in arrays],
-        [made((2, JOINT_ROWS, WIDTH), LOW)] * 2 + [made((UP_ROWS, WIDTH), LOW)] * 2,
+        [made((2, JOINT_ROWS, WIDTH), LOW)] * 2,
         after=after,
         work=cost(1e6, 1e6),
     )
@@ -1277,13 +1351,17 @@
     own = [row_swap(local_row(tokens, odd), 0), row_swap(local_row(tokens, 1 - odd), 1)]
     lengths = (pair_lengths, core_swap(pair_lengths))
     across = [y_swap(block) for block in own]
-    blocks = (
-        own + [core_swap(block) for block in own] + across + [core_swap(block) for block in across]
-    )
-    cotangent, _ = lax.optimization_barrier((cotangent, across[0]))
+    here = own + [core_swap(block) for block in own]
+    (q, k_here, v_here, summed, highest), mark = first_attention(
+        place, lengths, here, joint_weight, query_bias, value_bias
+    )
+    across[0], across[1], mark = lax.optimization_barrier((across[0], across[1], mark))
+    there = across + [core_swap(block) for block in across]
+    blocks = here + there
     cotangents = [row_swap(local_row(cotangent, odd), 0), row_swap(local_row(cotangent, 1 - odd), 1)]
-
-    (att, q, k, v, log_total), mark = attention(place, lengths, blocks, joint_weight, query_bias, value_bias)
+    (att, k_there, v_there, log_total), mark = attention(
+        place, lengths, there, joint_weight, value_bias, q, summed, highest, (mark, *cotangents)
+    )
     att_got = core_swap(att)
     results, mark = forward(place, att, att_got, own, cotangents, weights, (mark,))
     (
@@ -1293,41 +1371,48 @@
     done = (row_swap(result0, 0), row_swap(result1, 1))
     (px_send, px, qy_send, qy), mark = down_units(place, act, act_got, feed, feed_got, (mark,))
     down_pair = (px, x_swap(px_send), qy, y_swap(qy_send))
-    results, mark = backward(place, feed, slope, second_grad, unit1, inverse1, weights, (mark, normed_got, *done))
+    results, mark = backward(place, feed, slope, second_grad, unit1, inverse1, weights, (mark, normed_got))
     inner0, inner1, send0, send1, first_grad, branch_own, back_own, misc_send, sums1 = results
     got, misc = (core_swap(send0), core_swap(send1)), core_swap(misc_send)
-    (x_send, y_send, px, qy, down_p, down_q), mark = up_units(
-        place, normed_t, normed_got, (inner0, inner1), got, att_t, branch_own, misc, sums0, sums1, feed_got,
-        down_pair, (mark,)
-    )
+    (x_send, y_send, px, qy), mark = up_units(
+        place, normed_t, normed_got, (inner0, inner1), got, att_t, branch_own, misc, sums0, sums1, feed_got, (mark,)
+    )
+    (x_send, y_send, down_p, down_q), mark = down_pair_stage(place, down_pair, x_send, y_send, (mark,))
     x_got, y_got = x_swap(x_send), y_swap(y_send)
-    (dq, dk, dv), mark = attention_back(place, lengths, q, k, v, log_total, att, back_own, misc, (mark,))
-    (token_own, own_send, token_far, far_send), mark = token_parts(place, dq, dk, dv, joint_weight, (mark,))
+    (dq, dk, dv), mark = attention_back(
+        place, lengths, q, (k_here, k_there), (v_here, v_there), log_total, att, back_own, misc, (mark,)
+    )
+    (token_own, own_send, token_far, far_send), mark = token_parts(place, dq, dk, dv, joint_weight, (mark, *done))
     own_got, far_got = core_swap(own_send), core_swap(far_send)
-    (joint_px_send, joint_px, joint_qy_send, joint_qy), mark = joint_units(place, blocks, dq, dk, dv, (mark,))
-    (x_send, y_send, p, q_, down_send, down_keep), mark = second_stage(
-        place, x_got, y_got, px, qy, down_p, down_q, token_far, far_got, joint_px_send, joint_qy_send, (mark,)
-    )
-    x_got, y_got = x_swap(x_send), y_swap(y_send)
-    (down_send, down_keep), mark = end_stage(place, down_keep, z_swap(down_send, 1), (mark,))
-    down_got = z_swap(down_send, 2)
-    results, mark = third_stage(
-        place, (x_got, y_got, p, q_, joint_px, joint_qy, token_own, own_got, first_grad), (mark, down_got)
-    )
-    x_send, y_send, joint_p, joint_q, up_send, up_keep, token0, token1 = results
-    x_got, y_got, up_got = x_swap(x_send), y_swap(y_send), z_swap(up_send, 1)
-    (joint_send, joint_keep, up_send, up_keep), mark = fourth_stage(
-        place, (x_got, y_got, joint_p, joint_q, up_keep, up_got), (mark,)
-    )
-    joint_got, up_got = z_swap(joint_send, 1), z_swap(up_send, 2)
-    (joint_send, joint_keep), mark = end_stage(place, joint_keep, joint_got, (mark,))
-    joint_got = z_swap(joint_send, 2)
+    (px_send, joint_px, qy_send, joint_qy), mark = joint_units(
+        place, blocks, dq, dk, dv, token_far, far_got, (mark,)
+    )
+    (x_send, y_send, p, q_, down_send, down_two), mark = second_stage(
+        place, (x_got, y_got, px, qy, down_p, down_q), (mark,)
+    )
+    x_got, y_got, down_got = x_swap(x_send), y_swap(y_send), z_swap(down_send, 1)
+    px_send, qy_send, mark = lax.optimization_barrier((px_send, qy_send, mark))
+    across = y_swap(qy_send)
+    joint_pair = (joint_px, x_swap(px_send), joint_qy, across)
+    (up_send, up_two, down_send, down_keep), mark = up_line_stage(
+        place, (x_got, y_got, p, q_, down_two, down_got), (mark,)
+    )
+    up_got, down_got = z_swap(up_send, 1), z_swap(down_send, 2)
+    (up_send, up_keep), mark = end_stage(place, up_two, up_got, (mark, down_got))
+    up_got = z_swap(up_send, 2)
+    (x_send, y_send, joint_p, joint_q), mark = joint_pair_stage(place, joint_pair, (mark,))
+    joint_x_got, joint_y_got = x_swap(x_send), y_swap(y_send)
+    (token0, token1), mark = token_last(place, (token_own, own_got, across, first_grad), (mark,))
+    back = (row_swap(token0, 0), row_swap(token1, 1))
     dense_unit, mark = last_sum(place, ((down_keep, down_got), (up_keep, up_got)), (mark,))
     dense_all = gathered(dense_unit)
-    back = (row_swap(token0, 0), row_swap(token1, 1))
+    (joint_send, joint_two), mark = joint_line_stage(place, (joint_x_got, joint_y_got, joint_p, joint_q), (mark,))
+    joint_got = z_swap(joint_send, 1)
+    (joint_send, joint_keep), mark = end_stage(place, joint_two, joint_got, (mark,))
+    joint_got = z_swap(joint_send, 2)
+    (outputs, token_grad), mark = back_rows(place, done, back, (mark,))
     joint_unit, mark = last_sum(place, ((joint_keep, joint_got),), (mark,))
     joint_all = gathered(joint_unit)
-    (outputs, token_grad), mark = back_rows(place, done, back, (mark,))
     (
         down_grad, up_grad, out_grad, second_gain_grad, second_shift_grad, down_bias_grad, first_gain_grad,
         first_shift_grad, out_bias_grad, up_bias_grad,

time: 193 us -> 172 us (0.89)
  waiting for transfers between devices: 61.4 us -> 46 us
  starting transfers between devices: 62.3 us -> 56.9 us
  Pallas kernels: 59.5 us -> 62.7 us
  local copies, waits for them, and re-layouts: 7.09 us -> 3.91 us
    ppermute x44 -> x46, waiting for transfers between devices: 61.4 us -> 46 us  [permute(): return lax.ppermute(value, AXES, pairs)]
    ppermute x44 -> x46, starting transfers between devices: 62.3 us -> 56.9 us  [permute(): return lax.ppermute(value, AXES, pairs)]
    pallas_call x18 -> x22, Pallas kernels: 59.5 us -> 62.7 us  [call(): pl.pallas_call(ordered, grid_spec=pltpu.PrefetchScalarGridSpec(num_scalar...]
    unnamed x66 -> x32, local copies, waits for them, and re-layouts: 4.61 us -> 2.07 us
  transfers between devices with their start and end apart: 44 -> 46, of which waited for: 17 -> 20; matrix products, arithmetic and copies ran while one was open for 1% -> 1% of each run, Pallas kernels for 17% -> 26%
where the time goes in v3:
time: 172 us; the launch traced here: 171 us
  Pallas kernels  62.7 us (36%)
  starting transfers between devices  56.9 us (33%)
  waiting for transfers between devices  46 us (27%)
  local copies, waits for them, and re-layouts  3.91 us (2%)
    pallas_call x22, Pallas kernels, call(): pl.pallas_call(ordered, grid_spec=pltpu.PrefetchScalarGridSpec(num_scalar...  62.7 us
    ppermute x46, starting transfers between devices, permute(): return lax.ppermute(value, AXES, pairs)  56.9 us
    ppermute x46, waiting for transfers between devices, permute(): return lax.ppermute(value, AXES, pairs)  46 us
  transfers between devices with their start and end apart: 46, of which 20 were waited for; matrix products, arithmetic and copies ran while one was open for 1% of the time, Pallas kernels for 26%

profile of v3, /device:TPU:0, one launch (start us, length us, event | category | flops | bytes accessed | tf_op | source)
XLA Modules:
  0.0 171.3 jit_solution(11690303923452169768)
XLA Ops:
  1.8 3.1 %collective-permute-start.3 = (bf16[128,768]{1,0:T(8,128)(2,1)S(1)}, bf16[128,768]{1,0:T(8,128)(2,1)S(1)}, u32[]{:S(2)}, u32[]{:S(2)}) collective-permute-start(bf16[128,768]{1,0:T(8,128)(2,1)S(1)} %get-tuple-element.257), channel_id=1, source_target_pairs={{0,8},{1,24},{2,10},{3,26},{4,12},{5,28},{6,14},{7,30},{8,0},{9,16... | collective-permute-start | bytes 589832 | tf_op jit(solution)/shard_map/ppermute | solution.py:406
  5.6 3.5 %collective-permute-start = (s32[2,16]{1,0:T(2,128)}, s32[2,16]{1,0:T(2,128)S(1)}, u32[]{:S(2)}, u32[]{:S(2)}) collective-permute-start(s32[2,16]{1,0:T(2,128)} %refs_1_.5), channel_id=1, source_target_pairs={{0,1},{1,0},{2,3},{3,2},{4,5},{5,4},{6,7},{7,6},{8,9},{9,8},{10,11... | collective-permute-start | bytes 392 | tf_op jit(solution)/shard_map/ppermute | solution.py:406
  9.7 2.1 %collective-permute-start.6 = (bf16[128,768]{1,0:T(8,128)(2,1)S(1)}, bf16[128,768]{1,0:T(8,128)(2,1)S(1)}, u32[]{:S(2)}, u32[]{:S(2)}) collective-permute-start(bf16[128,768]{1,0:T(8,128)(2,1)S(1)} %collective-permute-done.3.refs_4_.refs_7_.refs_2_), channel_id=1, source_target_pairs={{0,1},{1,0},{2,3},{3,2},{4,5},{5,4},{6,7},{7,6},{8,9},{9,8},{10,11... | collective-permute-start | bytes 589832 | tf_op jit(solution)/shard_map/ppermute | solution.py:406
  11.8 1.5 collective-permute-start.4
  13.3 2.7 %collective-permute-start.5 = (bf16[128,768]{1,0:T(8,128)(2,1)S(1)}, bf16[128,768]{1,0:T(8,128)(2,1)S(1)}, u32[]{:S(2)}, u32[]{:S(2)}) collective-permute-start(bf16[128,768]{1,0:T(8,128)(2,1)S(1)} %collective-permute-done.1.refs_3_.refs_6_.refs_1_), channel_id=1, source_target_pairs={{0,1},{1,0},{2,3},{3,2},{4,5},{5,4},{6,7},{7,6},{8,9},{9,8},{10,11... | collective-permute-start | bytes 589832 | tf_op jit(solution)/shard_map/ppermute | solution.py:406
  16.0 1.5 collective-permute-start.2
  18.5 2.0 %copy-done = bf16[768,2304]{1,0:T(8,128)(2,1)S(1)} copy-done((bf16[768,2304]{1,0:T(8,128)(2,1)S(1)}, bf16[768,2304]{1,0:T(8,128)(2,1)}, u32[]{:S(2)}) %copy-start) | copy-done | bytes 3538968
  20.5 6.1 %first_attention.1 = (bf16[512,384]{1,0:T(8,128)(2,1)S(1)}, bf16[512,384]{1,0:T(8,128)(2,1)S(1)}, bf16[512,384]{1,0:T(8,128)(2,1)S(1)}, f32[6,512,128]{2,1,0:T(8...) custom-call(s32[4]{0:T(128)S(1)} %pad_add_fusion.refs_0_, s32[2,16]{1,0:T(2,128)S(1)} %copy-done.5, ...), custom_call_target="tpu_custom_call" | custom-call | flops 1024 | bytes 1024 | tf_op jit(solution)/shard_map/first_attention/pallas_call | solution.py:369
  26.6 3.9 %collective-permute-start.7 = (bf16[128,768]{1,0:T(8,128)(2,1)S(1)}, bf16[128,768]{1,0:T(8,128)(2,1)S(1)}, u32[]{:S(2)}, u32[]{:S(2)}) collective-permute-start(bf16[128,768]{1,0:T(8,128)(2,1)S(1)} %collective-permute-done.2.refs_3_.refs_5_), channel_id=1, source_target_pairs={{0,1},{1,0},{2,3},{3,2},{4,5},{5,4},{6,7},{7,6},{8,9},{9,8},{10,11... | collective-permute-start | bytes 589832 | tf_op jit(solution)/shard_map/ppermute | solution.py:406
  32.1 7.3 %attention.1 = (bf16[512,384]{1,0:T(8,128)(2,1)S(1)}, bf16[512,384]{1,0:T(8,128)(2,1)S(1)}, bf16[512,384]{1,0:T(8,128)(2,1)S(1)}, f32[8,512]{1,0:T(8,128)S(1)}, f32[8,128]{1,0:T(8,128)S(1)}) custom-call(s32[4]{0:T(128)S(1)} %pad_add_fusion.refs_0_, s32[2,16]{1,0:T(2,128)S(1)} %copy-done.5, s32[2,16]{1,0:T(2,128)S(1)} %collective-permute-done.refs_2_, ...), custom_call_target="tpu_custom_call" | custom-call | flops 1024 | bytes 1024 | tf_op jit(solution)/shard_map/attention/pallas_call | solution.py:369
  39.8 1.3 collective-permute-done.11.refs_2_
  41.2 7.4 %forward.1 = (bf16[128,768]{1,0:T(8,128)(2,1)S(1)}, bf16[128,768]{1,0:T(8,128)(2,1)S(1)}, bf16[272,768]{1,0:T(8,128)(2,1)S(1)}, f32[256,768]{1,0:T(8,128)S(1)}, ...) custom-call(s32[4]{0:T(128)S(1)} %pad_add_fusion.refs_0_, ...), custom_call_target="tpu_custom_call" | custom-call | flops 1024 | bytes 1024 | tf_op jit(solution)/shard_map/forward/pallas_call | solution.py:369
  49.5 2.1 %collective-permute-done.15.refs_4_.refs_12_ = bf16[272,768]{1,0:T(8,128)(2,1)S(1)} collective-permute-done((bf16[272,768]{1,0:T(8,128)(2,1)S(1)}, bf16[272,768]{1,0:T(8,128)(2,1)S(1)}, u32[]{:S(2)}, u32[]{:S(2)}) %collective-permute-start.15) | collective-permute-done | bytes 417824 | tf_op jit(solution)/shard_map/ppermute | solution.py:406
  51.6 2.6 %down_units.1 = (bf16[4,2,48,768]{3,2,1,0:T(8,128)(2,1)S(1)}, bf16[4,2,48,768]{3,2,1,0:T(8,128)(2,1)S(1)}, bf16[4,2,48,768]{3,2,1,0:T(8,128)(2,1)S(1)}, bf16[4,2,48,768]{3,2,1,0:T(8,128)(2,1)S(1)}, f32[8,128]{1,0:T(8,128)S(1)}) custom-call(s32[4]{0:T(128)S(1)} %pad_add_fusion.refs_0_, bf16[16,96,256]{2,1,0:T(8,128)(2,1)S(1)} %get-tuple-element.156.refs_1_, ...), custom_call_target="tpu_custom_call" | custom-call | flops 1024 | bytes 1024 | tf_op jit(solution)/shard_map/down_units/pallas_call | solution.py:369
  54.2 1.6 collective-permute-start.18
  56.3 7.2 %backward.1 = (bf16[256,768]{1,0:T(8,128)(2,1)S(1)}, bf16[256,768]{1,0:T(8,128)(2,1)S(1)}, bf16[256,768]{1,0:T(8,128)(2,1)S(1)}, bf16[256,768]{1,0:T(8,128)(2,1)...) custom-call(s32[4]{0:T(128)S(1)} %pad_add_fusion.refs_0_, ...), custom_call_target="tpu_custom_call" | custom-call | flops 1024 | bytes 1024 | tf_op jit(solution)/shard_map/backward/pallas_call | solution.py:369
  64.1 1.7 %collective-permute-done.20.refs_5_ = bf16[256,768]{1,0:T(8,128)(2,1)S(1)} collective-permute-done((bf16[256,768]{1,0:T(8,128)(2,1)S(1)}, bf16[256,768]{1,0:T(8,128)(2,1)S(1)}, u32[]{:S(2)}, u32[]{:S(2)}) %collective-permute-start.20) | collective-permute-done | bytes 393248 | tf_op jit(solution)/shard_map/ppermute | solution.py:406
  66.4 3.3 %up_units.1 = (bf16[704,768]{1,0:T(8,128)(2,1)S(1)}, bf16[704,768]{1,0:T(8,128)(2,1)S(1)}, bf16[4,2,64,768]{3,2,1,0:T(8,128)(2,1)S(1)}, bf16[4,2,64,768]{3,2,1,0:T(8,128)(2,1)S(1)}, f32[8,128]{1,0:T(8,128)S(1)}) custom-call(s32[4]{0:T(128)S(1)} %pad_add_fusion.refs_0_, bf16[768,256]{1,0:T(8,128)(2,1)S(1)} %get-tuple-element.167.refs_1_, ...), custom_call_target="tpu_custom_call" | custom-call | flops 1024 | bytes 1024 | tf_op jit(solution)/shard_map/up_units/pallas_call | solution.py:369
  69.8 1.2 collective-permute-done.19.refs_4_
  74.1 1.2 collective-permute-start.13
  75.3 9.4 %attention_back.1 = (bf16[512,384]{1,0:T(8,128)(2,1)S(1)}, bf16[1024,384]{1,0:T(8,128)(2,1)S(1)}, bf16[1024,384]{1,0:T(8,128)(2,1)S(1)}, f32[8,128]{1,0:T(8,128)S(1)}) custom-call(s32[4]{0:T(128)S(1)} %pad_add_fusion.refs_0_, s32[2,16]{1,0:T(2,128)S(1)} %copy-done.5, s32[2,16]{1,0:T(2,128)S(1)} %collective-permute-done.refs_2_, ...), custom_call_target="tpu_custom_call" | custom-call | flops 1024 | bytes 1024 | tf_op jit(solution)/shard_map/attention_back/pallas_call | solution.py:369
  84.7 2.8 %token_parts.1 = (bf16[256,768]{1,0:T(8,128)(2,1)S(1)}, bf16[256,768]{1,0:T(8,128)(2,1)S(1)}, bf16[256,768]{1,0:T(8,128)(2,1)S(1)}, bf16[256,768]{1,0:T(8,128)(2,1)S(1)}, f32[8,128]{1,0:T(8,128)S(1)}) custom-call(s32[4]{0:T(128)S(1)} %pad_add_fusion.refs_0_, bf16[512,384]{1,0:T(8,128)(2,1)S(1)} %get-tuple-element.181.refs_1_.refs_9_, ...), custom_call_target="tpu_custom_call" | custom-call | flops 1024 | bytes 1024 | tf_op jit(solution)/shard_map/token_parts/pallas_call | solution.py:369
  87.5 3.0 %collective-permute-start.23 = (bf16[256,768]{1,0:T(8,128)(2,1)S(1)}, bf16[256,768]{1,0:T(8,128)(2,1)S(1)}, u32[]{:S(2)}, u32[]{:S(2)}) collective-permute-start(bf16[256,768]{1,0:T(8,128)(2,1)S(1)} %get-tuple-element.188), channel_id=1, source_target_pairs={{0,1},{1,0},{2,3},{3,2},{4,5},{5,4},{6,7},{7,6},{8,9},{9,8},{10,11... | collective-permute-start | bytes 1179656 | tf_op jit(solution)/shard_map/ppermute | solution.py:406
  90.6 1.3 collective-permute-done.23.refs_13_
  91.9 3.5 %joint_units.1 = (bf16[4,2,48,768]{3,2,1,0:T(8,128)(2,1)S(1)}, bf16[4,2,48,768]{3,2,1,0:T(8,128)(2,1)S(1)}, bf16[512,768]{1,0:T(8,128)(2,1)S(1)}, bf16[4,2,32,768]{3,2,1,0:T(8,128)(2,1)S(1)}, f32[8,128]{1,0:T(8,128)S(1)}) custom-call(s32[4]{0:T(128)S(1)} %pad_add_fusion.refs_0_, bf16[128,768]{1,0:T(8,128)(2,1)S(1)} %collective-permute-done.1.refs_3_.refs_6_.refs_1_, ...), custom_call_target="tpu_custom_call" | custom-call | flops 1024 | bytes 1024 | tf_op jit(solution)/shard_map/joint_units/pallas_call | solution.py:369
  95.4 1.7 collective-permute-done.24.refs_1_
  98.5 1.5 collective-permute-start.28
  100.0 1.3 collective-permute-start.29
  102.0 1.2 collective-permute-start.30
  103.8 4.9 %collective-permute-done.30.refs_6_ = bf16[2,96,768]{2,1,0:T(8,128)(2,1)S(1)} collective-permute-done((bf16[2,96,768]{2,1,0:T(8,128)(2,1)S(1)}, bf16[2,96,768]{2,1,0:T(8,128)(2,1)S(1)}, u32[]{:S(2)}, u32[]{:S(2)}) %collective-permute-start.30) | collective-permute-done | bytes 294944 | tf_op jit(solution)/shard_map/ppermute | solution.py:406
  108.7 1.9 %collective-permute-done.28.refs_1_ = bf16[256,768]{1,0:T(8,128)(2,1)S(1)} collective-permute-done((bf16[256,768]{1,0:T(8,128)(2,1)S(1)}, bf16[256,768]{1,0:T(8,128)(2,1)S(1)}, u32[]{:S(2)}, u32[]{:S(2)}) %collective-permute-start.28) | collective-permute-done | bytes 393248 | tf_op jit(solution)/shard_map/ppermute | solution.py:406
  110.6 1.4 collective-permute-done.29.refs_2_
  112.9 1.3 collective-permute-start.31
  114.1 1.7 collective-permute-start.32
  115.8 7.1 %collective-permute-done.32.refs_4_.refs_2_ = bf16[96,768]{1,0:T(8,128)(2,1)S(1)} collective-permute-done((bf16[96,768]{1,0:T(8,128)(2,1)S(1)}, bf16[96,768]{1,0:T(8,128)(2,1)S(1)}, u32[]{:S(2)}, u32[]{:S(2)}) %collective-permute-start.32) | collective-permute-done | bytes 147488 | tf_op jit(solution)/shard_map/ppermute | solution.py:406
  124.5 1.5 collective-permute-done.26.refs_4_.refs_3_
  126.8 1.6 collective-permute-start.36
  128.4 2.9 %collective-permute-start.37 = (bf16[128,768]{1,0:T(8,128)(2,1)S(1)}, bf16[128,768]{1,0:T(8,128)(2,1)S(1)}, u32[]{:S(2)}, u32[]{:S(2)}) collective-permute-start(bf16[128,768]{1,0:T(8,128)(2,1)S(1)} %get-tuple-element.226), channel_id=1, source_target_pairs={{0,16},{1,17},{2,18},{3,19},{4,20},{5,21},{6,22},{7,23},{8,24},{9,... | collective-permute-start | bytes 589832 | tf_op jit(solution)/shard_map/ppermute | solution.py:406
  132.7 5.3 %collective-permute-done.37.refs_4_ = bf16[128,768]{1,0:T(8,128)(2,1)S(1)} collective-permute-done((bf16[128,768]{1,0:T(8,128)(2,1)S(1)}, bf16[128,768]{1,0:T(8,128)(2,1)S(1)}, u32[]{:S(2)}, u32[]{:S(2)}) %collective-permute-start.37) | collective-permute-done | bytes 196640 | tf_op jit(solution)/shard_map/ppermute | solution.py:406
  141.5 1.4 collective-permute-start.34
  142.8 3.4 %collective-permute-done.38.refs_2_ = bf16[2,80,768]{2,1,0:T(8,128)(2,1)S(1)} collective-permute-done((bf16[2,80,768]{2,1,0:T(8,128)(2,1)S(1)}, bf16[2,80,768]{2,1,0:T(8,128)(2,1)S(1)}, u32[]{:S(2)}, u32[]{:S(2)}) %collective-permute-start.38) | collective-permute-done | bytes 245792 | tf_op jit(solution)/shard_map/ppermute | solution.py:406
  146.9 8.1 %collective-permute-start.39 = (bf16[80,768]{1,0:T(8,128)(2,1)S(1)}, bf16[80,768]{1,0:T(8,128)(2,1)S(1)}, u32[]{:S(2)}, u32[]{:S(2)}) collective-permute-start(bf16[80,768]{1,0:T(8,128)(2,1)S(1)} %get-tuple-element.236), channel_id=1, source_target_pairs={{0,16},{1,17},{2,18},{3,19},{4,20},{5,21},{6,22},{7,23},{8,24},{9,... | collective-permute-start | bytes 368648 | tf_op jit(solution)/shard_map/ppermute | solution.py:406
  155.5 1.6 back_rows.1
  157.2 4.2 %collective-permute-done.39.refs_2_ = bf16[80,768]{1,0:T(8,128)(2,1)S(1)} collective-permute-done((bf16[80,768]{1,0:T(8,128)(2,1)S(1)}, bf16[80,768]{1,0:T(8,128)(2,1)S(1)}, u32[]{:S(2)}, u32[]{:S(2)}) %collective-permute-start.39) | collective-permute-done | bytes 122912 | tf_op jit(solution)/shard_map/ppermute | solution.py:406
  161.9 1.4 collective-permute-start.41
  163.3 3.5 %collective-permute-done.41.refs_3_ = bf16[80,768]{1,0:T(8,128)(2,1)S(1)} collective-permute-done((bf16[80,768]{1,0:T(8,128)(2,1)S(1)}, bf16[80,768]{1,0:T(8,128)(2,1)S(1)}, u32[]{:S(2)}, u32[]{:S(2)}) %collective-permute-start.41) | collective-permute-done | bytes 122912 | tf_op jit(solution)/shard_map/ppermute | solution.py:406
  166.9 2.3 %dense_outputs.1 = (f32[384,768]{1,0:T(8,128)}, f32[96,3072]{1,0:T(8,128)}, f32[96,768]{1,0:T(8,128)}, f32[1,96]{1,0:T(1,128)}, f32[1,96]{1,0:T(1,128)}, /*index...) custom-call(s32[4]{0:T(128)S(1)} %pad_add_fusion.refs_0_, ...), custom_call_target="tpu_custom_call" | custom-call | flops 1024 | bytes 1024 | tf_op jit(solution)/shard_map/dense_outputs/pallas_call | solution.py:369
  169.8 1.5 joint_outputs.1
  (111 shorter events, 24.0 us)
Async XLA Ops:
  0.6 17.8 %copy-start.5 = (s32[2,16]{1,0:T(2,128)S(1)}, s32[2,16]{1,0:T(2,128)}, u32[]{:S(2)}) copy-start(s32[2,16]{1,0:T(2,128)} %refs_1_.5) | copy-start | bytes 388
  0.7 17.0 %copy-start.7 = (f32[768]{0:T(1024)S(1)}, f32[768]{0:T(1024)}, u32[]{:S(2)}) copy-start(f32[768]{0:T(1024)} %param.19) | copy-start | bytes 9220
  1.8 7.9 %collective-permute-start.3 = (bf16[128,768]{1,0:T(8,128)(2,1)S(1)}, bf16[128,768]{1,0:T(8,128)(2,1)S(1)}, u32[]{:S(2)}, u32[]{:S(2)}) collective-permute-start(bf16[128,768]{1,0:T(8,128)(2,1)S(1)} %get-tuple-element.257), channel_id=1, source_target_pairs={{0,8},{1,24},{2,10},{3,26},{4,12},{5,28},{6,14},{7,30},{8,0},{9,16... | collective-permute-start | bytes 589832 | tf_op jit(solution)/shard_map/ppermute | solution.py:406
  4.9 8.4 %collective-permute-start.1 = (bf16[128,768]{1,0:T(8,128)(2,1)S(1)}, bf16[128,768]{1,0:T(8,128)(2,1)S(1)}, u32[]{:S(2)}, u32[]{:S(2)}) collective-permute-start(bf16[128,768]{1,0:T(8,128)(2,1)S(1)} %get-tuple-element.258), channel_id=1, source_target_pairs={{0,0},{1,16},{2,2},{3,18},{4,4},{5,20},{6,6},{7,22},{8,8},{9,24},{... | collective-permute-start | bytes 589832 | tf_op jit(solution)/shard_map/ppermute | solution.py:406
  5.6 12.1 %collective-permute-start = (s32[2,16]{1,0:T(2,128)}, s32[2,16]{1,0:T(2,128)S(1)}, u32[]{:S(2)}, u32[]{:S(2)}) collective-permute-start(s32[2,16]{1,0:T(2,128)} %refs_1_.5), channel_id=1, source_target_pairs={{0,1},{1,0},{2,3},{3,2},{4,5},{5,4},{6,7},{7,6},{8,9},{9,8},{10,11... | collective-permute-start | bytes 392 | tf_op jit(solution)/shard_map/ppermute | solution.py:406
  9.7 8.1 %collective-permute-start.6 = (bf16[128,768]{1,0:T(8,128)(2,1)S(1)}, bf16[128,768]{1,0:T(8,128)(2,1)S(1)}, u32[]{:S(2)}, u32[]{:S(2)}) collective-permute-start(bf16[128,768]{1,0:T(8,128)(2,1)S(1)} %collective-permute-done.3.refs_4_.refs_7_.refs_2_), channel_id=1, source_target_pairs={{0,1},{1,0},{2,3},{3,2},{4,5},{5,4},{6,7},{7,6},{8,9},{9,8},{10,11... | collective-permute-start | bytes 589832 | tf_op jit(solution)/shard_map/ppermute | solution.py:406
  11.8 14.8 %collective-permute-start.4 = (bf16[128,768]{1,0:T(8,128)(2,1)S(1)}, bf16[128,768]{1,0:T(8,128)(2,1)S(1)}, u32[]{:S(2)}, u32[]{:S(2)}) collective-permute-start(bf16[128,768]{1,0:T(8,128)(2,1)S(1)} %collective-permute-done.3.refs_4_.refs_7_.refs_2_), channel_id=1, source_target_pairs={{0,4},{1,5},{2,6},{3,7},{4,0},{5,1},{6,2},{7,3},{8,12},{9,13},{10,... | collective-permute-start | bytes 589832 | tf_op jit(solution)/shard_map/ppermute | solution.py:406
  13.3 5.1 %collective-permute-start.5 = (bf16[128,768]{1,0:T(8,128)(2,1)S(1)}, bf16[128,768]{1,0:T(8,128)(2,1)S(1)}, u32[]{:S(2)}, u32[]{:S(2)}) collective-permute-start(bf16[128,768]{1,0:T(8,128)(2,1)S(1)} %collective-permute-done.1.refs_3_.refs_6_.refs_1_), channel_id=1, source_target_pairs={{0,1},{1,0},{2,3},{3,2},{4,5},{5,4},{6,7},{7,6},{8,9},{9,8},{10,11... | collective-permute-start | bytes 589832 | tf_op jit(solution)/shard_map/ppermute | solution.py:406
  16.0 10.6 %collective-permute-start.2 = (bf16[128,768]{1,0:T(8,128)(2,1)S(1)}, bf16[128,768]{1,0:T(8,128)(2,1)S(1)}, u32[]{:S(2)}, u32[]{:S(2)}) collective-permute-start(bf16[128,768]{1,0:T(8,128)(2,1)S(1)} %collective-permute-done.1.refs_3_.refs_6_.refs_1_), channel_id=1, source_target_pairs={{0,4},{1,5},{2,6},{3,7},{4,0},{5,1},{6,2},{7,3},{8,12},{9,13},{10,... | collective-permute-start | bytes 589832 | tf_op jit(solution)/shard_map/ppermute | solution.py:406
  17.7 12.9 %collective-permute-start.10 = (bf16[128,768]{1,0:T(8,128)(2,1)S(1)}, bf16[128,768]{1,0:T(8,128)(2,1)S(1)}, u32[]{:S(2)}, u32[]{:S(2)}) collective-permute-start(bf16[128,768]{1,0:T(8,128)(2,1)S(1)} %get-tuple-element.255), channel_id=1, source_target_pairs={{0,8},{1,24},{2,10},{3,26},{4,12},{5,28},{6,14},{7,30},{8,0},{9,16... | collective-permute-start | bytes 589832 | tf_op jit(solution)/shard_map/ppermute | solution.py:406
  17.8 12.9 %collective-permute-start.9 = (bf16[128,768]{1,0:T(8,128)(2,1)S(1)}, bf16[128,768]{1,0:T(8,128)(2,1)S(1)}, u32[]{:S(2)}, u32[]{:S(2)}) collective-permute-start(bf16[128,768]{1,0:T(8,128)(2,1)S(1)} %get-tuple-element.256), channel_id=1, source_target_pairs={{0,0},{1,16},{2,2},{3,18},{4,4},{5,20},{6,6},{7,22},{8,8},{9,24},{... | collective-permute-start | bytes 589832 | tf_op jit(solution)/shard_map/ppermute | solution.py:406
  26.6 5.0 %collective-permute-start.7 = (bf16[128,768]{1,0:T(8,128)(2,1)S(1)}, bf16[128,768]{1,0:T(8,128)(2,1)S(1)}, u32[]{:S(2)}, u32[]{:S(2)}) collective-permute-start(bf16[128,768]{1,0:T(8,128)(2,1)S(1)} %collective-permute-done.2.refs_3_.refs_5_), channel_id=1, source_target_pairs={{0,1},{1,0},{2,3},{3,2},{4,5},{5,4},{6,7},{7,6},{8,9},{9,8},{10,11... | collective-permute-start | bytes 589832 | tf_op jit(solution)/shard_map/ppermute | solution.py:406
  30.6 1.4 collective-permute-start.8
  39.4 1.8 %collective-permute-start.11 = (bf16[512,384]{1,0:T(8,128)(2,1)S(1)}, bf16[512,384]{1,0:T(8,128)(2,1)S(1)}, u32[]{:S(2)}, u32[]{:S(2)}) collective-permute-start(bf16[512,384]{1,0:T(8,128)(2,1)S(1)} %get-tuple-element.142.refs_1_.refs_9_), channel_id=1, source_target_pairs={{0,1},{1,0},{2,3},{3,2},{4,5},{5,4},{6,7},{7,6},{8,9},{9,8},{10,11... | collective-permute-start | bytes 1179656 | tf_op jit(solution)/shard_map/ppermute | solution.py:406
  48.6 3.0 %collective-permute-start.14 = (bf16[16,96,256]{2,1,0:T(8,128)(2,1)S(1)}, bf16[16,96,256]{2,1,0:T(8,128)(2,1)S(1)}, u32[]{:S(2)}, u32[]{:S(2)}) collective-permute-start(bf16[16,96,256]{2,1,0:T(8,128)(2,1)S(1)} %get-tuple-element.157), channel_id=1, source_target_pairs={{0,1},{1,0},{2,3},{3,2},{4,5},{5,4},{6,7},{7,6},{8,9},{9,8},{10,11... | collective-permute-start | bytes 2359304 | tf_op jit(solution)/shard_map/ppermute | solution.py:406
  49.0 2.6 %collective-permute-start.15 = (bf16[272,768]{1,0:T(8,128)(2,1)S(1)}, bf16[272,768]{1,0:T(8,128)(2,1)S(1)}, u32[]{:S(2)}, u32[]{:S(2)}) collective-permute-start(bf16[272,768]{1,0:T(8,128)(2,1)S(1)} %get-tuple-element.151.refs_3_.refs_1_), channel_id=1, source_target_pairs={{0,1},{1,0},{2,3},{3,2},{4,5},{5,4},{6,7},{7,6},{8,9},{9,8},{10,11... | collective-permute-start | bytes 1253384 | tf_op jit(solution)/shard_map/ppermute | solution.py:406
  49.2 7.1 %collective-permute-start.16 = (bf16[256,768]{1,0:T(8,128)(2,1)S(1)}, bf16[256,768]{1,0:T(8,128)(2,1)S(1)}, u32[]{:S(2)}, u32[]{:S(2)}) collective-permute-start(bf16[256,768]{1,0:T(8,128)(2,1)S(1)} %get-tuple-element.160), channel_id=1, source_target_pairs={{0,1},{1,0},{2,3},{3,2},{4,5},{5,4},{6,7},{7,6},{8,9},{9,8},{10,11... | collective-permute-start | bytes 1179656 | tf_op jit(solution)/shard_map/ppermute | solution.py:406
  54.2 15.6 %collective-permute-start.18 = (bf16[4,2,48,768]{3,2,1,0:T(8,128)(2,1)S(1)}, bf16[4,2,48,768]{3,2,1,0:T(8,128)(2,1)S(1)}, u32[]{:S(2)}, u32[]{:S(2)}) collective-permute-start(bf16[4,2,48,768]{3,2,1,0:T(8,128)(2,1)S(1)} %get-tuple-element.164), channel_id=1, source_target_pairs={{0,2},{1,3},{2,0},{3,1},{4,6},{5,7},{6,4},{7,5},{8,10},{9,11},{10,... | collective-permute-start | bytes 1769480 | tf_op jit(solution)/shard_map/ppermute | solution.py:406
  55.8 15.2 %collective-permute-start.19 = (bf16[4,2,48,768]{3,2,1,0:T(8,128)(2,1)S(1)}, bf16[4,2,48,768]{3,2,1,0:T(8,128)(2,1)S(1)}, u32[]{:S(2)}, u32[]{:S(2)}) collective-permute-start(bf16[4,2,48,768]{3,2,1,0:T(8,128)(2,1)S(1)} %get-tuple-element.166), channel_id=1, source_target_pairs={{0,4},{1,5},{2,6},{3,7},{4,0},{5,1},{6,2},{7,3},{8,12},{9,13},{10,... | collective-permute-start | bytes 1769480 | tf_op jit(solution)/shard_map/ppermute | solution.py:406
  63.5 3.0 %collective-permute-start.17 = (bf16[272,768]{1,0:T(8,128)(2,1)S(1)}, bf16[272,768]{1,0:T(8,128)(2,1)S(1)}, u32[]{:S(2)}, u32[]{:S(2)}) collective-permute-start(bf16[272,768]{1,0:T(8,128)(2,1)S(1)} %get-tuple-element.162), channel_id=1, source_target_pairs={{0,1},{1,0},{2,3},{3,2},{4,5},{5,4},{6,7},{7,6},{8,9},{9,8},{10,11... | collective-permute-start | bytes 1253384 | tf_op jit(solution)/shard_map/ppermute | solution.py:406
  63.6 2.3 %collective-permute-start.20 = (bf16[256,768]{1,0:T(8,128)(2,1)S(1)}, bf16[256,768]{1,0:T(8,128)(2,1)S(1)}, u32[]{:S(2)}, u32[]{:S(2)}) collective-permute-start(bf16[256,768]{1,0:T(8,128)(2,1)S(1)} %get-tuple-element.170), channel_id=1, source_target_pairs={{0,1},{1,0},{2,3},{3,2},{4,5},{5,4},{6,7},{7,6},{8,9},{9,8},{10,11... | collective-permute-start | bytes 1179656 | tf_op jit(solution)/shard_map/ppermute | solution.py:406
  64.1 2.4 %collective-permute-start.21 = (bf16[256,768]{1,0:T(8,128)(2,1)S(1)}, bf16[256,768]{1,0:T(8,128)(2,1)S(1)}, u32[]{:S(2)}, u32[]{:S(2)}) collective-permute-start(bf16[256,768]{1,0:T(8,128)(2,1)S(1)} %get-tuple-element.171), channel_id=1, source_target_pairs={{0,1},{1,0},{2,3},{3,2},{4,5},{5,4},{6,7},{7,6},{8,9},{9,8},{10,11... | collective-permute-start | bytes 1179656 | tf_op jit(solution)/shard_map/ppermute | solution.py:406
  72.1 25.0 %collective-permute-start.24 = (bf16[704,768]{1,0:T(8,128)(2,1)S(1)}, bf16[704,768]{1,0:T(8,128)(2,1)S(1)}, u32[]{:S(2)}, u32[]{:S(2)}) collective-permute-start(bf16[704,768]{1,0:T(8,128)(2,1)S(1)} %get-tuple-element.192), channel_id=1, source_target_pairs={{0,2},{1,3},{2,0},{3,1},{4,6},{5,7},{6,4},{7,5},{8,10},{9,11},{10,... | collective-permute-start | bytes 3244040 | tf_op jit(solution)/shard_map/ppermute | solution.py:406
  72.7 24.7 %collective-permute-start.25 = (bf16[704,768]{1,0:T(8,128)(2,1)S(1)}, bf16[704,768]{1,0:T(8,128)(2,1)S(1)}, u32[]{:S(2)}, u32[]{:S(2)}) collective-permute-start(bf16[704,768]{1,0:T(8,128)(2,1)S(1)} %get-tuple-element.193), channel_id=1, source_target_pairs={{0,4},{1,5},{2,6},{3,7},{4,0},{5,1},{6,2},{7,3},{8,12},{9,13},{10,... | collective-permute-start | bytes 3244040 | tf_op jit(solution)/shard_map/ppermute | solution.py:406
  73.2 11.5 %collective-permute-start.12 = (bf16[128,768]{1,0:T(8,128)(2,1)S(1)}, bf16[128,768]{1,0:T(8,128)(2,1)S(1)}, u32[]{:S(2)}, u32[]{:S(2)}) collective-permute-start(bf16[128,768]{1,0:T(8,128)(2,1)S(1)} %get-tuple-element.144), channel_id=1, source_target_pairs={{0,0},{1,16},{2,2},{3,18},{4,4},{5,20},{6,6},{7,22},{8,8},{9,24},{... | collective-permute-start | bytes 589832 | tf_op jit(solution)/shard_map/ppermute | solution.py:406
  74.1 10.6 %collective-permute-start.13 = (bf16[128,768]{1,0:T(8,128)(2,1)S(1)}, bf16[128,768]{1,0:T(8,128)(2,1)S(1)}, u32[]{:S(2)}, u32[]{:S(2)}) collective-permute-start(bf16[128,768]{1,0:T(8,128)(2,1)S(1)} %get-tuple-element.145), channel_id=1, source_target_pairs={{0,8},{1,24},{2,10},{3,26},{4,12},{5,28},{6,14},{7,30},{8,0},{9,16... | collective-permute-start | bytes 589832 | tf_op jit(solution)/shard_map/ppermute | solution.py:406
  87.5 4.4 %collective-permute-start.23 = (bf16[256,768]{1,0:T(8,128)(2,1)S(1)}, bf16[256,768]{1,0:T(8,128)(2,1)S(1)}, u32[]{:S(2)}, u32[]{:S(2)}) collective-permute-start(bf16[256,768]{1,0:T(8,128)(2,1)S(1)} %get-tuple-element.188), channel_id=1, source_target_pairs={{0,1},{1,0},{2,3},{3,2},{4,5},{5,4},{6,7},{7,6},{8,9},{9,8},{10,11... | collective-permute-start | bytes 1179656 | tf_op jit(solution)/shard_map/ppermute | solution.py:406
  98.5 12.1 %collective-permute-start.28 = (bf16[256,768]{1,0:T(8,128)(2,1)S(1)}, bf16[256,768]{1,0:T(8,128)(2,1)S(1)}, u32[]{:S(2)}, u32[]{:S(2)}) collective-permute-start(bf16[256,768]{1,0:T(8,128)(2,1)S(1)} %get-tuple-element.205), channel_id=1, source_target_pairs={{0,2},{1,3},{2,0},{3,1},{4,6},{5,7},{6,4},{7,5},{8,10},{9,11},{10,... | collective-permute-start | bytes 1179656 | tf_op jit(solution)/shard_map/ppermute | solution.py:406
  100.0 12.1 %collective-permute-start.29 = (bf16[256,768]{1,0:T(8,128)(2,1)S(1)}, bf16[256,768]{1,0:T(8,128)(2,1)S(1)}, u32[]{:S(2)}, u32[]{:S(2)}) collective-permute-start(bf16[256,768]{1,0:T(8,128)(2,1)S(1)} %get-tuple-element.206), channel_id=1, source_target_pairs={{0,4},{1,5},{2,6},{3,7},{4,0},{5,1},{6,2},{7,3},{8,12},{9,13},{10,... | collective-permute-start | bytes 1179656 | tf_op jit(solution)/shard_map/ppermute | solution.py:406
  101.3 24.8 %collective-permute-start.26 = (bf16[512,768]{1,0:T(8,128)(2,1)S(1)}, bf16[512,768]{1,0:T(8,128)(2,1)S(1)}, u32[]{:S(2)}, u32[]{:S(2)}) collective-permute-start(bf16[512,768]{1,0:T(8,128)(2,1)S(1)} %get-tuple-element.200), channel_id=1, source_target_pairs={{0,4},{1,5},{2,6},{3,7},{4,0},{5,1},{6,2},{7,3},{8,12},{9,13},{10,... | collective-permute-start | bytes 2359304 | tf_op jit(solution)/shard_map/ppermute | solution.py:406
  102.0 6.7 %collective-permute-start.30 = (bf16[2,96,768]{2,1,0:T(8,128)(2,1)S(1)}, bf16[2,96,768]{2,1,0:T(8,128)(2,1)S(1)}, u32[]{:S(2)}, u32[]{:S(2)}) collective-permute-start(bf16[2,96,768]{2,1,0:T(8,128)(2,1)S(1)} %get-tuple-element.210), channel_id=1, source_target_pairs={{0,8},{1,9},{2,10},{3,11},{4,12},{5,13},{6,14},{7,15},{8,0},{9,1},... | collective-permute-start | bytes 884744 | tf_op jit(solution)/shard_map/ppermute | solution.py:406
  103.2 21.3 %collective-permute-start.27 = (bf16[4,2,48,768]{3,2,1,0:T(8,128)(2,1)S(1)}, bf16[4,2,48,768]{3,2,1,0:T(8,128)(2,1)S(1)}, u32[]{:S(2)}, u32[]{:S(2)}) collective-permute-start(bf16[4,2,48,768]{3,2,1,0:T(8,128)(2,1)S(1)} %get-tuple-element.203), channel_id=1, source_target_pairs={{0,2},{1,3},{2,0},{3,1},{4,6},{5,7},{6,4},{7,5},{8,10},{9,11},{10,... | collective-permute-start | bytes 1769480 | tf_op jit(solution)/shard_map/ppermute | solution.py:406
  112.9 11.0 %collective-permute-start.31 = (bf16[2,128,768]{2,1,0:T(8,128)(2,1)S(1)}, bf16[2,128,768]{2,1,0:T(8,128)(2,1)S(1)}, u32[]{:S(2)}, u32[]{:S(2)}) collective-permute-start(bf16[2,128,768]{2,1,0:T(8,128)(2,1)S(1)} %get-tuple-element.213), channel_id=1, source_target_pairs={{0,8},{1,9},{2,10},{3,11},{4,12},{5,13},{6,14},{7,15},{8,0},{9,1},... | collective-permute-start | bytes 1179656 | tf_op jit(solution)/shard_map/ppermute | solution.py:406
  114.1 17.8 %collective-permute-start.22 = (bf16[256,768]{1,0:T(8,128)(2,1)S(1)}, bf16[256,768]{1,0:T(8,128)(2,1)S(1)}, u32[]{:S(2)}, u32[]{:S(2)}) collective-permute-start(bf16[256,768]{1,0:T(8,128)(2,1)S(1)} %get-tuple-element.186), channel_id=1, source_target_pairs={{0,1},{1,0},{2,3},{3,2},{4,5},{5,4},{6,7},{7,6},{8,9},{9,8},{10,11... | collective-permute-start | bytes 1179656 | tf_op jit(solution)/shard_map/ppermute | solution.py:406
  114.1 8.8 %collective-permute-start.32 = (bf16[96,768]{1,0:T(8,128)(2,1)S(1)}, bf16[96,768]{1,0:T(8,128)(2,1)S(1)}, u32[]{:S(2)}, u32[]{:S(2)}) collective-permute-start(bf16[96,768]{1,0:T(8,128)(2,1)S(1)} %get-tuple-element.215), channel_id=1, source_target_pairs={{0,16},{1,17},{2,18},{3,19},{4,20},{5,21},{6,22},{7,23},{8,24},{9,... | collective-permute-start | bytes 442376 | tf_op jit(solution)/shard_map/ppermute | solution.py:406
  126.8 12.5 %collective-permute-start.36 = (bf16[4,48,768]{2,1,0:T(8,128)(2,1)S(1)}, bf16[4,48,768]{2,1,0:T(8,128)(2,1)S(1)}, u32[]{:S(2)}, u32[]{:S(2)}) collective-permute-start(bf16[4,48,768]{2,1,0:T(8,128)(2,1)S(1)} %get-tuple-element.221), channel_id=1, source_target_pairs={{0,4},{1,5},{2,6},{3,7},{4,0},{5,1},{6,2},{7,3},{8,12},{9,13},{10,... | collective-permute-start | bytes 884744 | tf_op jit(solution)/shard_map/ppermute | solution.py:406
  128.4 9.5 %collective-permute-start.37 = (bf16[128,768]{1,0:T(8,128)(2,1)S(1)}, bf16[128,768]{1,0:T(8,128)(2,1)S(1)}, u32[]{:S(2)}, u32[]{:S(2)}) collective-permute-start(bf16[128,768]{1,0:T(8,128)(2,1)S(1)} %get-tuple-element.226), channel_id=1, source_target_pairs={{0,16},{1,17},{2,18},{3,19},{4,20},{5,21},{6,22},{7,23},{8,24},{9,... | collective-permute-start | bytes 589832 | tf_op jit(solution)/shard_map/ppermute | solution.py:406
  131.3 8.0 %collective-permute-start.35 = (bf16[4,32,768]{2,1,0:T(8,128)(2,1)S(1)}, bf16[4,32,768]{2,1,0:T(8,128)(2,1)S(1)}, u32[]{:S(2)}, u32[]{:S(2)}) collective-permute-start(bf16[4,32,768]{2,1,0:T(8,128)(2,1)S(1)} %get-tuple-element.220), channel_id=1, source_target_pairs={{0,2},{1,3},{2,0},{3,1},{4,6},{5,7},{6,4},{7,5},{8,10},{9,11},{10,... | collective-permute-start | bytes 589832 | tf_op jit(solution)/shard_map/ppermute | solution.py:406
  138.6 16.5 %collective-permute-start.44 = (bf16[224,768]{1,0:T(8,128)(2,1)S(1)}, bf16[224,768]{1,0:T(8,128)(2,1)S(1)}, u32[]{:S(2)}, u32[]{:S(2)}) collective-permute-start(bf16[224,768]{1,0:T(8,128)(2,1)S(1)} %get-tuple-element.239.refs_1_), channel_id=1, source_target_pairs={{0,2},{1,3},{2,0},{3,1},{4,6},{5,7},{6,4},{7,5},{8,10},{9,11},{10,... | collective-permute-start | bytes 1032200 | tf_op jit(solution)/shard_map/ppermute | solution.py:406
  140.0 6.3 %collective-permute-start.38 = (bf16[2,80,768]{2,1,0:T(8,128)(2,1)S(1)}, bf16[2,80,768]{2,1,0:T(8,128)(2,1)S(1)}, u32[]{:S(2)}, u32[]{:S(2)}) collective-permute-start(bf16[2,80,768]{2,1,0:T(8,128)(2,1)S(1)} %get-tuple-element.230), channel_id=1, source_target_pairs={{0,8},{1,9},{2,10},{3,11},{4,12},{5,13},{6,14},{7,15},{8,0},{9,1},... | collective-permute-start | bytes 737288 | tf_op jit(solution)/shard_map/ppermute | solution.py:406
  140.8 14.7 %collective-permute-start.33 = (bf16[128,768]{1,0:T(8,128)(2,1)S(1)}, bf16[128,768]{1,0:T(8,128)(2,1)S(1)}, u32[]{:S(2)}, u32[]{:S(2)}) collective-permute-start(bf16[128,768]{1,0:T(8,128)(2,1)S(1)} %get-tuple-element.218), channel_id=1, source_target_pairs={{0,0},{1,16},{2,2},{3,18},{4,4},{5,20},{6,6},{7,22},{8,8},{9,24},{... | collective-permute-start | bytes 589832 | tf_op jit(solution)/shard_map/ppermute | solution.py:406
  141.5 14.1 %collective-permute-start.34 = (bf16[128,768]{1,0:T(8,128)(2,1)S(1)}, bf16[128,768]{1,0:T(8,128)(2,1)S(1)}, u32[]{:S(2)}, u32[]{:S(2)}) collective-permute-start(bf16[128,768]{1,0:T(8,128)(2,1)S(1)} %get-tuple-element.219), channel_id=1, source_target_pairs={{0,8},{1,24},{2,10},{3,26},{4,12},{5,28},{6,14},{7,30},{8,0},{9,16... | collective-permute-start | bytes 589832 | tf_op jit(solution)/shard_map/ppermute | solution.py:406
  146.9 14.5 %collective-permute-start.39 = (bf16[80,768]{1,0:T(8,128)(2,1)S(1)}, bf16[80,768]{1,0:T(8,128)(2,1)S(1)}, u32[]{:S(2)}, u32[]{:S(2)}) collective-permute-start(bf16[80,768]{1,0:T(8,128)(2,1)S(1)} %get-tuple-element.236), channel_id=1, source_target_pairs={{0,16},{1,17},{2,18},{3,19},{4,20},{5,21},{6,22},{7,23},{8,24},{9,... | collective-permute-start | bytes 368648 | tf_op jit(solution)/shard_map/ppermute | solution.py:406
  155.0 11.9 %collective-permute-start.43 = (bf16[224,768]{1,0:T(8,128)(2,1)S(1)}, bf16[224,768]{1,0:T(8,128)(2,1)S(1)}, u32[]{:S(2)}, u32[]{:S(2)}) collective-permute-start(bf16[224,768]{1,0:T(8,128)(2,1)S(1)} %get-tuple-element.239.refs_1_), channel_id=1, source_target_pairs={{0,1},{1,0},{2,3},{3,2},{4,5},{5,4},{6,7},{7,6},{8,9},{9,8},{10,11... | collective-permute-start | bytes 1032200 | tf_op jit(solution)/shard_map/ppermute | solution.py:406
  155.0 11.8 %collective-permute-start.45 = (bf16[224,768]{1,0:T(8,128)(2,1)S(1)}, bf16[224,768]{1,0:T(8,128)(2,1)S(1)}, u32[]{:S(2)}, u32[]{:S(2)}) collective-permute-start(bf16[224,768]{1,0:T(8,128)(2,1)S(1)} %collective-permute-done.44.refs_3_), channel_id=1, source_target_pairs={{0,1},{1,0},{2,3},{3,2},{4,5},{5,4},{6,7},{7,6},{8,9},{9,8},{10,11... | collective-permute-start | bytes 1032200 | tf_op jit(solution)/shard_map/ppermute | solution.py:406
  161.9 4.9 %collective-permute-start.41 = (bf16[80,768]{1,0:T(8,128)(2,1)S(1)}, bf16[80,768]{1,0:T(8,128)(2,1)S(1)}, u32[]{:S(2)}, u32[]{:S(2)}) collective-permute-start(bf16[80,768]{1,0:T(8,128)(2,1)S(1)} %get-tuple-element.238.refs_1_), channel_id=1, source_target_pairs={{0,2},{1,3},{2,0},{3,1},{4,6},{5,7},{6,4},{7,5},{8,10},{9,11},{10,... | collective-permute-start | bytes 368648 | tf_op jit(solution)/shard_map/ppermute | solution.py:406
  163.3 6.4 %collective-permute-start.40 = (bf16[80,768]{1,0:T(8,128)(2,1)S(1)}, bf16[80,768]{1,0:T(8,128)(2,1)S(1)}, u32[]{:S(2)}, u32[]{:S(2)}) collective-permute-start(bf16[80,768]{1,0:T(8,128)(2,1)S(1)} %get-tuple-element.238.refs_1_), channel_id=1, source_target_pairs={{0,1},{1,0},{2,3},{3,2},{4,5},{5,4},{6,7},{7,6},{8,9},{9,8},{10,11... | collective-permute-start | bytes 368648 | tf_op jit(solution)/shard_map/ppermute | solution.py:406
  166.9 2.9 %collective-permute-start.42 = (bf16[80,768]{1,0:T(8,128)(2,1)S(1)}, bf16[80,768]{1,0:T(8,128)(2,1)S(1)}, u32[]{:S(2)}, u32[]{:S(2)}) collective-permute-start(bf16[80,768]{1,0:T(8,128)(2,1)S(1)} %collective-permute-done.41.refs_3_), channel_id=1, source_target_pairs={{0,1},{1,0},{2,3},{3,2},{4,5},{5,4},{6,7},{7,6},{8,9},{9,8},{10,11... | collective-permute-start | bytes 368648 | tf_op jit(solution)/shard_map/ppermute | solution.py:406
  (14 other events, 122.5 us)

commit v4 on v3

--- a/solution.py
+++ b/solution.py
@@ -461,29 +461,61 @@
     return lax.broadcasted_iota(jnp.int32, (rows, LANES), 1) < HEAD_DIM
 
 
+def columns_kernel(place, columns, query_bias, value_bias, out, query_row, value_row):
+    out[0] = columns[...]
+    query_row[...] = query_bias[...]
+    value_row[...] = value_bias[...]
+
+
+def own_columns(place, joint_weight, query_bias, value_bias):
+    half_row = pl.BlockSpec((1, HALF), lambda i, place: (0, place[3]))
+    results, _ = call(
+        columns_kernel,
+        "own_columns",
+        place,
+        [
+            (joint_weight, pl.BlockSpec((WIDTH, HALF), lambda i, place: (0, 2 * i + place[3]))),
+            (row_of(query_bias), half_row),
+            (row_of(value_bias), half_row),
+        ],
+        [((3, WIDTH, HALF), LOW, pl.BlockSpec((1, WIDTH, HALF), lambda i, place: (i, 0, 0)))]
+        + [made((1, HALF), FLOAT)] * 2,
+        grid=(3,),
+        work=cost(1e6, 4e6),
+    )
+    return results
+
+
 def first_attention_kernel(
-    place, own_lengths, peer_lengths, t0, t1, t2, t3, wq, wk, wv, qb, vb, q_out, k_out, v_out, summed, highest_out, bias
+    place, own_lengths, peer_lengths, t0, t1, t2, t3, columns, qb, vb, q_out, k_out, v_out, summed, stats, bias
 ):
     bases = first_positions(place)
     ends = pair_ends(place, own_lengths, peer_lengths)
     tokens = jnp.concatenate([block[...] for block in (t0, t1, t2, t3)], axis=0)
-    queries = dot(tokens, wq[...]) + qb[...]
+    queries = dot(tokens, columns[0]) + qb[...]
     q_out[...] = (queries.astype(LOW).astype(FLOAT) * HEAD_DIM**-0.5).astype(LOW)
-    k_out[...] = dot(tokens, wk[...]).astype(LOW)
-    v_out[...] = (dot(tokens, wv[...]) + vb[...]).astype(LOW)
+    k_out[...] = dot(tokens, columns[1]).astype(LOW)
+    v_out[...] = (dot(tokens, columns[2]) + vb[...]).astype(LOW)
     fill_bias(bias, bases[:4], bases[:4], ends)
+    stats[...] = jnp.zeros_like(stats)
     for pair in range(PAIRS_OF_HEADS):
         lanes = pl.ds(pair * LANES, LANES)
-        keys = k_out[:, lanes]
-        values_of = with_ones(v_out[:, lanes])
-        for part in range(2):
-            rows = pl.ds(part * OWN, OWN)
-            chosen = halves_of(q_out[rows, lanes])
-            for half in range(2):
-                scores = dot_nt(chosen[half], keys) + bias[rows, :]
-                highest = jnp.max(scores, axis=1, keepdims=True)
-                summed[2 * pair + half, rows, :] = dot(jnp.exp(scores - highest).astype(LOW), values_of[half])
-                highest_out[2 * pair + half, rows, :] = jnp.broadcast_to(highest, (OWN, LANES))
+        scores = masked_scores(k_out[:, lanes], q_out[:, lanes], bias)
+        highest = jnp.max(scores, axis=0, keepdims=True)
+        weights = jnp.exp(scores - highest)
+        summed[pair] = dot(turned(v_out[:, lanes]), weights.astype(LOW))
+        stats[2 * pair : 2 * pair + 1, :] = highest
+        stats[2 * pair + 1 : 2 * pair + 2, :] = column_sum(weights)
+
+
+def turned(array):
+    return jnp.transpose(array.astype(FLOAT)).astype(LOW)
+
+
+def masked_scores(keys, queries, bias):
+    mask = bias[...]
+    chosen = jnp.concatenate(halves_of(queries), axis=0)
+    return dot_nt(keys, chosen) + jnp.concatenate([mask, mask], axis=1)
 
 
 def fill_bias(bias, query_bases, key_bases, ends):
@@ -500,25 +532,13 @@
     return jnp.where(left, array, zeros), jnp.where(left, zeros, array)
 
 
-def with_ones(values):
-    left = head_mask(values.shape[0])
-    ones = jnp.ones_like(values)
-    return jnp.where(left, values, ones), jnp.where(left, ones, values)
-
-
-def first_attention(place, lengths, blocks, joint_weight, query_bias, value_bias, after=()):
-    def columns(kind):
-        return joint_weight, pl.BlockSpec((WIDTH, HALF), lambda i, place, *_: (0, 2 * kind + place[3]))
-
-    half_row = pl.BlockSpec((1, HALF), lambda i, place, *_: (0, place[3]))
-    state = made((HEADS // 2, 512, LANES), FLOAT)
+def first_attention(place, lengths, blocks, columns, query_bias, value_bias, after=()):
     return call(
         first_attention_kernel,
         "first_attention",
         place,
-        [plain(block) for block in blocks]
-        + [columns(0), columns(1), columns(2), (row_of(query_bias), half_row), (row_of(value_bias), half_row)],
-        [made((512, HALF), LOW)] * 3 + [state, state],
+        [plain(array) for array in (*blocks, columns, query_bias, value_bias)],
+        [made((512, HALF), LOW)] * 3 + [made((PAIRS_OF_HEADS, LANES, 1024), FLOAT), made((8, 1024), FLOAT)],
         scratch=[pltpu.VMEM((512, 512), FLOAT)],
         scalars=lengths,
         after=after,
@@ -527,54 +547,40 @@
 
 
 def attention_kernel(
-    place, own_lengths, peer_lengths, t0, t1, t2, t3, wk, wv, vb, q, summed_in, highest_in,
-    att_out, k_out, v_out, log_out, bias, log_columns,
+    place, own_lengths, peer_lengths, t0, t1, t2, t3, columns, vb, q, summed, stats,
+    att_out, k_out, v_out, log_out, bias,
 ):
     bases = first_positions(place)
     ends = pair_ends(place, own_lengths, peer_lengths)
     tokens = jnp.concatenate([block[...] for block in (t0, t1, t2, t3)], axis=0)
-    k_out[...] = dot(tokens, wk[...]).astype(LOW)
-    v_out[...] = (dot(tokens, wv[...]) + vb[...]).astype(LOW)
-    fill_bias(bias, bases[:4], bases[4:], ends)
-    log_columns[...] = jnp.zeros_like(log_columns)
-    column = lax.broadcasted_iota(jnp.int32, (OWN, LANES), 1)
-    left = head_mask(OWN)
+    k_out[...] = dot(tokens, columns[1]).astype(LOW)
+    v_out[...] = (dot(tokens, columns[2]) + vb[...]).astype(LOW)
+    fill_bias(bias, bases[4:], bases[:4], ends)
+    log_out[...] = jnp.zeros_like(log_out)
+    top = lax.broadcasted_iota(jnp.int32, (LANES, 512), 0) < HEAD_DIM
     for pair in range(PAIRS_OF_HEADS):
         lanes = pl.ds(pair * LANES, LANES)
-        keys = k_out[:, lanes]
-        values_of = with_ones(v_out[:, lanes])
-        for part in range(2):
-            rows = pl.ds(part * OWN, OWN)
-            chosen = halves_of(q[rows, lanes])
-            results = []
-            for half in range(2):
-                head = 2 * pair + half
-                scores = dot_nt(chosen[half], keys) + bias[rows, :]
-                before = highest_in[head, rows, :]
-                highest = jnp.maximum(before, jnp.max(scores, axis=1, keepdims=True))
-                weights = jnp.exp(scores - highest[:, 0:1]).astype(LOW)
-                total = dot(weights, values_of[half]) + jnp.exp(before - highest) * summed_in[head, rows, :]
-                turned = pltpu.roll(total, HEAD_DIM, 1)
-                results.append(total / turned)
-                log_total = highest + jnp.log(total if half == 1 else turned)
-                log_columns[rows, :] = jnp.where(column == head, log_total, log_columns[rows, :])
-            att_out[rows, lanes] = jnp.where(left, results[0], results[1]).astype(LOW)
-    log_out[...] = jnp.transpose(log_columns[...])[0:8, :]
-
-
-def attention(place, lengths, blocks, joint_weight, value_bias, q, summed, highest, after=()):
-    def columns(kind):
-        return joint_weight, pl.BlockSpec((WIDTH, HALF), lambda i, place, *_: (0, 2 * kind + place[3]))
-
-    half_row = pl.BlockSpec((1, HALF), lambda i, place, *_: (0, place[3]))
+        scores = masked_scores(k_out[:, lanes], q[:, lanes], bias)
+        before = stats[2 * pair : 2 * pair + 1, :]
+        highest = jnp.maximum(before, jnp.max(scores, axis=0, keepdims=True))
+        weights = jnp.exp(scores - highest)
+        shrink = jnp.exp(before - highest)
+        sums = column_sum(weights) + shrink * stats[2 * pair + 1 : 2 * pair + 2, :]
+        total = (dot(turned(v_out[:, lanes]), weights.astype(LOW)) + shrink * summed[pair]) / sums
+        att_out[:, lanes] = jnp.transpose(jnp.where(top, total[:, 0:512], total[:, 512:])).astype(LOW)
+        logs = highest + jnp.log(sums)
+        log_out[2 * pair : 2 * pair + 1, :] = logs[:, 0:512]
+        log_out[2 * pair + 1 : 2 * pair + 2, :] = logs[:, 512:]
+
+
+def attention(place, lengths, blocks, columns, value_bias, q, summed, stats, after=()):
     return call(
         attention_kernel,
         "attention",
         place,
-        [plain(block) for block in blocks]
-        + [columns(1), columns(2), (row_of(value_bias), half_row), plain(q), plain(summed), plain(highest)],
+        [plain(array) for array in (*blocks, columns, value_bias, q, summed, stats)],
         [made((512, HALF), LOW)] * 3 + [made((8, 512), FLOAT)],
-        scratch=[pltpu.VMEM((512, 512), FLOAT), pltpu.VMEM((512, LANES), FLOAT)],
+        scratch=[pltpu.VMEM((512, 512), FLOAT)],
         scalars=lengths,
         after=after,
         work=cost(4e9, 8e6, 3e6),
@@ -644,7 +650,7 @@
         result = (unit * gain2[...] + shift2[...]).astype(LOW)
         result0[...] = result[0:BLOCK]
         result1[...] = result[BLOCK:]
-        cotangent = jnp.concatenate([cot0[...], cot1[...]], axis=0).astype(FLOAT)
+        cotangent = jnp.concatenate([cot0[0:BLOCK], cot1[0:BLOCK]], axis=0).astype(FLOAT)
         grad = norm_back(cotangent * gain2[...], unit, inverse)
         second_grad[...] = grad
         low_grad = grad.astype(LOW)
@@ -925,24 +931,21 @@
     )
 
 
-def token_kernel(place, dq, dk, dv, wq, wk, wv, own, own_send, far, far_send):
+def token_kernel(place, dq, dk, dv, columns, own, own_send, far, far_send):
     for part, target in enumerate((own, own_send, far, far_send)):
         rows = pl.ds(part * OWN, OWN)
-        total = dot_nt(dk[rows, :], wk[...]) + dot_nt(dv[rows, :], wv[...])
+        total = dot_nt(dk[rows, :], columns[1]) + dot_nt(dv[rows, :], columns[2])
         if part < 2:
-            total = total + dot_nt(dq[rows, :], wq[...])
+            total = total + dot_nt(dq[rows, :], columns[0])
         target[...] = total.astype(LOW)
 
 
-def token_parts(place, dq, dk, dv, joint_weight, after=()):
-    def columns(kind):
-        return joint_weight, pl.BlockSpec((WIDTH, HALF), lambda i, place: (0, 2 * kind + place[3]))
-
+def token_parts(place, dq, dk, dv, columns, after=()):
     return call(
         token_kernel,
         "token_parts",
         place,
-        [plain(dq), plain(dk), plain(dv), columns(0), columns(1), columns(2)],
+        [plain(dq), plain(dk), plain(dv), plain(columns)],
         [made((OWN, WIDTH), LOW)] * 4,
         after=after,
         work=cost(1.5e9, 5e6),
@@ -1191,30 +1194,27 @@
 
 
 def last_sum_kernel(place, *refs):
-    out = refs[-1]
-    at = 0
-    for first, second in zip(refs[0:-1:2], refs[1:-1:2]):
-        out[pl.ds(at, first.shape[0]), :] = added(first[...], second[...])
-        at += first.shape[0]
+    count = len(refs) // 3
+    for index in range(count):
+        refs[2 * count + index][...] = added(refs[2 * index][...], refs[2 * index + 1][...])
 
 
 def last_sum(place, pairs, after=()):
-    arrays = [array for pair in pairs for array in pair]
-    rows = sum(pair[0].shape[0] for pair in pairs)
-    results, mark = call(
+    return call(
         last_sum_kernel,
         "last_sum",
         place,
-        [plain(array) for array in arrays],
-        [made((rows, arrays[0].shape[1]), LOW)],
+        [plain(array) for pair in pairs for array in pair],
+        [made(pair[0].shape, LOW) for pair in pairs],
         after=after,
         work=cost(1e6, 1e6),
     )
-    return results[0], mark
-
-
-def gathered(unit):
+
+
+def gathered(unit, mark=None):
     across = x_swap(unit)
+    if mark is not None:
+        across, mark = lax.optimization_barrier((across, mark))
     return unit, core_swap(unit), across, core_swap(across)
 
 
@@ -1229,13 +1229,14 @@
 
 
 def dense_out_kernel(
-    place, u0, u1, u2, u3, down, up, out, gain2, shift2, down_bias, gain1, shift1, out_bias, up_bias, heads, tails
+    place, d0, d1, d2, d3, u0, u1, u2, u3,
+    down, up, out, gain2, shift2, down_bias, gain1, shift1, out_bias, up_bias, heads, tails,
 ):
-    for unit, (x, c) in zip((u0, u1, u2, u3), quarters(place)):
+    for down_unit, unit, (x, c) in zip((d0, d1, d2, d3), (u0, u1, u2, u3), quarters(place)):
         quarter = 2 * x + c
-        down[pl.ds(pl.multiple_of(quarter * DOWN_ROWS, 32), DOWN_ROWS), :] = unit[0:DOWN_ROWS, :].astype(FLOAT)
-        up[:, pl.ds(pl.multiple_of(quarter * WIDTH, LANES), WIDTH)] = unit[96:192, :].astype(FLOAT)
-        rest = unit[192:224, :].astype(FLOAT)
+        down[pl.ds(pl.multiple_of(quarter * DOWN_ROWS, 32), DOWN_ROWS), :] = down_unit[...].astype(FLOAT)
+        up[:, pl.ds(pl.multiple_of(quarter * WIDTH, LANES), WIDTH)] = unit[0:96, :].astype(FLOAT)
+        rest = unit[96:128, :].astype(FLOAT)
         lanes = pl.ds(pl.multiple_of(c * HALF, LANES), HALF)
         out[pl.ds(pl.multiple_of(x * 48, 8), 24), lanes] = rest[0:24, 0:HALF]
         out[pl.ds(pl.multiple_of(x * 48 + 24, 8), 24), lanes] = rest[0:24, HALF:]
@@ -1348,20 +1349,27 @@
     def local_row(array, index):
         return lax.dynamic_index_in_dim(array, index, 0, keepdims=False)
 
+    columns, query_row, value_row = own_columns(place, joint_weight, query_bias, value_bias)
+    lengths = (pair_lengths, core_swap(pair_lengths))
     own = [row_swap(local_row(tokens, odd), 0), row_swap(local_row(tokens, 1 - odd), 1)]
-    lengths = (pair_lengths, core_swap(pair_lengths))
+    *own, columns, lengths = lax.optimization_barrier((*own, columns, lengths))
     across = [y_swap(block) for block in own]
     here = own + [core_swap(block) for block in own]
-    (q, k_here, v_here, summed, highest), mark = first_attention(
-        place, lengths, here, joint_weight, query_bias, value_bias
-    )
-    across[0], across[1], mark = lax.optimization_barrier((across[0], across[1], mark))
+    (q, k_here, v_here, summed, stats), mark = first_attention(
+        place, lengths, here, columns, query_row, value_row
+    )
+    padding = jnp.zeros((16, WIDTH), LOW)
+    cotangents = [
+        row_swap(jnp.concatenate([local_row(cotangent, index), padding], axis=0), second)
+        for second, index in ((0, odd), (1, 1 - odd))
+    ]
+    across[0], across[1], mark, cotangents[0] = lax.optimization_barrier((across[0], across[1], mark, cotangents[0]))
     there = across + [core_swap(block) for block in across]
     blocks = here + there
-    cotangents = [row_swap(local_row(cotangent, odd), 0), row_swap(local_row(cotangent, 1 - odd), 1)]
     (att, k_there, v_there, log_total), mark = attention(
-        place, lengths, there, joint_weight, value_bias, q, summed, highest, (mark, *cotangents)
-    )
+        place, lengths, there, columns, value_row, q, summed, stats, (mark,)
+    )
+    att, cotangents[1] = lax.optimization_barrier((att, cotangents[1]))
     att_got = core_swap(att)
     results, mark = forward(place, att, att_got, own, cotangents, weights, (mark,))
     (
@@ -1382,7 +1390,7 @@
     (dq, dk, dv), mark = attention_back(
         place, lengths, q, (k_here, k_there), (v_here, v_there), log_total, att, back_own, misc, (mark,)
     )
-    (token_own, own_send, token_far, far_send), mark = token_parts(place, dq, dk, dv, joint_weight, (mark, *done))
+    (token_own, own_send, token_far, far_send), mark = token_parts(place, dq, dk, dv, columns, (mark, *done))
     own_got, far_got = core_swap(own_send), core_swap(far_send)
     (px_send, joint_px, qy_send, joint_qy), mark = joint_units(
         place, blocks, dq, dk, dv, token_far, far_got, (mark,)
@@ -1404,19 +1412,19 @@
     joint_x_got, joint_y_got = x_swap(x_send), y_swap(y_send)
     (token0, token1), mark = token_last(place, (token_own, own_got, across, first_grad), (mark,))
     back = (row_swap(token0, 0), row_swap(token1, 1))
-    dense_unit, mark = last_sum(place, ((down_keep, down_got), (up_keep, up_got)), (mark,))
-    dense_all = gathered(dense_unit)
+    (down_unit, up_unit), mark = last_sum(place, ((down_keep, down_got), (up_keep, up_got)), (mark,))
+    dense_all = (*gathered(down_unit), *gathered(up_unit))
     (joint_send, joint_two), mark = joint_line_stage(place, (joint_x_got, joint_y_got, joint_p, joint_q), (mark,))
     joint_got = z_swap(joint_send, 1)
     (joint_send, joint_keep), mark = end_stage(place, joint_two, joint_got, (mark,))
     joint_got = z_swap(joint_send, 2)
-    (outputs, token_grad), mark = back_rows(place, done, back, (mark,))
-    joint_unit, mark = last_sum(place, ((joint_keep, joint_got),), (mark,))
-    joint_all = gathered(joint_unit)
     (
         down_grad, up_grad, out_grad, second_gain_grad, second_shift_grad, down_bias_grad, first_gain_grad,
         first_shift_grad, out_bias_grad, up_bias_grad,
     ), mark = dense_outputs(place, dense_all, (mark,))
+    (joint_unit,), mark = last_sum(place, ((joint_keep, joint_got),), (mark,))
+    (outputs, token_grad), mark = back_rows(place, done, back, (mark,))
+    joint_all = gathered(joint_unit, mark)
     (joint_grad, query_bias_grad, value_bias_grad), mark = joint_outputs(place, joint_all, (mark,))
     return (
         outputs,

time: 172 us -> 166 us (0.965)
  starting transfers between devices: 56.9 us -> 35.6 us
  waiting for transfers between devices: 46 us -> 63.8 us
  Pallas kernels: 62.7 us -> 60.5 us
    ppermute x46 -> x49, starting transfers between devices: 56.9 us -> 35.6 us  [permute(): return lax.ppermute(value, AXES, pairs)]
    ppermute x46 -> x49, waiting for transfers between devices: 46 us -> 63.8 us  [permute(): return lax.ppermute(value, AXES, pairs)]
    pallas_call x22 -> x23, Pallas kernels: 62.7 us -> 60.5 us  [call(): pl.pallas_call(ordered, grid_spec=pltpu.PrefetchScalarGridSpec(num_scalar...]
  transfers between devices with their start and end apart: 46 -> 49, of which waited for: 20 -> 25; matrix products, arithmetic and copies ran while one was open for 1% -> 2% of each run, Pallas kernels for 26% -> 30%
where the time goes in v4:
time: 166 us
  waiting for transfers between devices  63.8 us (38%)
  Pallas kernels  60.5 us (36%)
  starting transfers between devices  35.6 us (21%)
  local copies, waits for them, and re-layouts  4.23 us (3%)
    ppermute x49, waiting for transfers between devices, permute(): return lax.ppermute(value, AXES, pairs)  63.8 us
    pallas_call x23, Pallas kernels, call(): pl.pallas_call(ordered, grid_spec=pltpu.PrefetchScalarGridSpec(num_scalar...  60.5 us
    ppermute x49, starting transfers between devices, permute(): return lax.ppermute(value, AXES, pairs)  35.6 us
  transfers between devices with their start and end apart: 49, of which 25 were waited for; matrix products, arithmetic and copies ran while one was open for 2% of the time, Pallas kernels for 30%

profile of v4, /device:TPU:0, one launch (start us, length us, event | category | flops | bytes accessed | tf_op | source)
XLA Modules:
  0.0 166.1 jit_solution(10279534888781239395)
XLA Ops:
  1.2 1.0 dynamic-slice_bitcast_fusion.2
  2.2 2.7 %collective-permute-start.1 = (bf16[128,768]{1,0:T(8,128)(2,1)S(1)}, bf16[128,768]{1,0:T(8,128)(2,1)S(1)}, u32[]{:S(2)}, u32[]{:S(2)}) collective-permute-start(bf16[128,768]{1,0:T(8,128)(2,1)S(1)} %get-tuple-element.283), channel_id=1, source_target_pairs={{0,8},{1,24},{2,10},{3,26},{4,12},{5,28},{6,14},{7,30},{8,0},{9,16... | collective-permute-start | bytes 589832 | tf_op jit(solution)/shard_map/ppermute | solution.py:406
  5.6 1.1 dynamic-slice_bitcast_fusion
  7.5 2.0 %copy-done.3 = bf16[768,2304]{1,0:T(8,128)(2,1)S(1)} copy-done((bf16[768,2304]{1,0:T(8,128)(2,1)S(1)}, bf16[768,2304]{1,0:T(8,128)(2,1)}, u32[]{:S(2)}) %copy-start.3) | copy-done | bytes 3538968
  9.5 1.5 own_columns.1
  11.0 8.0 %collective-permute-start.5 = (bf16[128,768]{1,0:T(8,128)(2,1)S(1)}, bf16[128,768]{1,0:T(8,128)(2,1)S(1)}, u32[]{:S(2)}, u32[]{:S(2)}) collective-permute-start(bf16[128,768]{1,0:T(8,128)(2,1)S(1)} %collective-permute-done.refs_3_.refs_6_.refs_1_), channel_id=1, source_target_pairs={{0,1},{1,0},{2,3},{3,2},{4,5},{5,4},{6,7},{7,6},{8,9},{9,8},{10,11... | collective-permute-start | bytes 589832 | tf_op jit(solution)/shard_map/ppermute | solution.py:406
  19.0 1.5 collective-permute-start.3
  21.2 5.0 %first_attention.1 = (bf16[512,384]{1,0:T(8,128)(2,1)S(1)}, bf16[512,384]{1,0:T(8,128)(2,1)S(1)}, bf16[512,384]{1,0:T(8,128)(2,1)S(1)}, f32[3,128,1024]{2,1,0:T(...) custom-call(s32[4]{0:T(128)S(1)} %pad_add_fusion.refs_0_, s32[2,16]{1,0:T(2,128)S(1)} %copy-done.5, ...), custom_call_target="tpu_custom_call" | custom-call | flops 1024 | bytes 1024 | tf_op jit(solution)/shard_map/first_attention/pallas_call | solution.py:369
  26.7 3.8 %collective-permute-done.4.refs_4_.refs_6_ = bf16[128,768]{1,0:T(8,128)(2,1)S(1)} collective-permute-done((bf16[128,768]{1,0:T(8,128)(2,1)S(1)}, bf16[128,768]{1,0:T(8,128)(2,1)S(1)}, u32[]{:S(2)}, u32[]{:S(2)}) %collective-permute-start.4) | collective-permute-done | bytes 196640 | tf_op jit(solution)/shard_map/ppermute | solution.py:406
  31.1 0.9 collective-permute-done.8.refs_5_.refs_7_
  32.4 5.0 %attention.1 = (bf16[512,384]{1,0:T(8,128)(2,1)S(1)}, bf16[512,384]{1,0:T(8,128)(2,1)S(1)}, bf16[512,384]{1,0:T(8,128)(2,1)S(1)}, f32[8,512]{1,0:T(8,128)S(1)}, f32[8,128]{1,0:T(8,128)S(1)}) custom-call(s32[4]{0:T(128)S(1)} %pad_add_fusion.refs_0_, s32[2,16]{1,0:T(2,128)S(1)} %copy-done.5, s32[2,16]{1,0:T(2,128)S(1)} %collective-permute-done.2.refs_2_, ...), custom_call_target="tpu_custom_call" | custom-call | flops 1024 | bytes 1024 | tf_op jit(solution)/shard_map/attention/pallas_call | solution.py:369
  37.8 1.4 collective-permute-done.11.refs_2_
  39.2 7.2 %forward.1 = (bf16[128,768]{1,0:T(8,128)(2,1)S(1)}, bf16[128,768]{1,0:T(8,128)(2,1)S(1)}, bf16[272,768]{1,0:T(8,128)(2,1)S(1)}, f32[256,768]{1,0:T(8,128)S(1)}, ...) custom-call(s32[4]{0:T(128)S(1)} %pad_add_fusion.refs_0_, ...), custom_call_target="tpu_custom_call" | custom-call | flops 1024 | bytes 1024 | tf_op jit(solution)/shard_map/forward/pallas_call | solution.py:369
  47.2 2.1 %collective-permute-done.15.refs_4_.refs_12_ = bf16[272,768]{1,0:T(8,128)(2,1)S(1)} collective-permute-done((bf16[272,768]{1,0:T(8,128)(2,1)S(1)}, bf16[272,768]{1,0:T(8,128)(2,1)S(1)}, u32[]{:S(2)}, u32[]{:S(2)}) %collective-permute-start.15) | collective-permute-done | bytes 417824 | tf_op jit(solution)/shard_map/ppermute | solution.py:406
  49.3 2.8 %down_units.1 = (bf16[4,2,48,768]{3,2,1,0:T(8,128)(2,1)S(1)}, bf16[4,2,48,768]{3,2,1,0:T(8,128)(2,1)S(1)}, bf16[4,2,48,768]{3,2,1,0:T(8,128)(2,1)S(1)}, bf16[4,2,48,768]{3,2,1,0:T(8,128)(2,1)S(1)}, f32[8,128]{1,0:T(8,128)S(1)}) custom-call(s32[4]{0:T(128)S(1)} %pad_add_fusion.refs_0_, bf16[16,96,256]{2,1,0:T(8,128)(2,1)S(1)} %get-tuple-element.180.refs_1_, ...), custom_call_target="tpu_custom_call" | custom-call | flops 1024 | bytes 1024 | tf_op jit(solution)/shard_map/down_units/pallas_call | solution.py:369
  52.2 1.6 collective-permute-start.18
  53.7 1.5 collective-permute-start.19
  55.2 7.2 %backward.1 = (bf16[256,768]{1,0:T(8,128)(2,1)S(1)}, bf16[256,768]{1,0:T(8,128)(2,1)S(1)}, bf16[256,768]{1,0:T(8,128)(2,1)S(1)}, bf16[256,768]{1,0:T(8,128)(2,1)...) custom-call(s32[4]{0:T(128)S(1)} %pad_add_fusion.refs_0_, ...), custom_call_target="tpu_custom_call" | custom-call | flops 1024 | bytes 1024 | tf_op jit(solution)/shard_map/backward/pallas_call | solution.py:369
  63.1 1.7 %collective-permute-done.20.refs_5_ = bf16[256,768]{1,0:T(8,128)(2,1)S(1)} collective-permute-done((bf16[256,768]{1,0:T(8,128)(2,1)S(1)}, bf16[256,768]{1,0:T(8,128)(2,1)S(1)}, u32[]{:S(2)}, u32[]{:S(2)}) %collective-permute-start.20) | collective-permute-done | bytes 393248 | tf_op jit(solution)/shard_map/ppermute | solution.py:406
  65.4 3.3 %up_units.1 = (bf16[704,768]{1,0:T(8,128)(2,1)S(1)}, bf16[704,768]{1,0:T(8,128)(2,1)S(1)}, bf16[4,2,64,768]{3,2,1,0:T(8,128)(2,1)S(1)}, bf16[4,2,64,768]{3,2,1,0:T(8,128)(2,1)S(1)}, f32[8,128]{1,0:T(8,128)S(1)}) custom-call(s32[4]{0:T(128)S(1)} %pad_add_fusion.refs_0_, bf16[768,256]{1,0:T(8,128)(2,1)S(1)} %get-tuple-element.191.refs_1_, ...), custom_call_target="tpu_custom_call" | custom-call | flops 1024 | bytes 1024 | tf_op jit(solution)/shard_map/up_units/pallas_call | solution.py:369
  68.9 1.1 down_pair_stage.1
  70.6 1.5 collective-permute-start.25
  72.9 9.3 %attention_back.1 = (bf16[512,384]{1,0:T(8,128)(2,1)S(1)}, bf16[1024,384]{1,0:T(8,128)(2,1)S(1)}, bf16[1024,384]{1,0:T(8,128)(2,1)S(1)}, f32[8,128]{1,0:T(8,128)S(1)}) custom-call(s32[4]{0:T(128)S(1)} %pad_add_fusion.refs_0_, s32[2,16]{1,0:T(2,128)S(1)} %copy-done.5, s32[2,16]{1,0:T(2,128)S(1)} %collective-permute-done.2.refs_2_, ...), custom_call_target="tpu_custom_call" | custom-call | flops 1024 | bytes 1024 | tf_op jit(solution)/shard_map/attention_back/pallas_call | solution.py:369
  82.7 2.7 %token_parts.1 = (bf16[256,768]{1,0:T(8,128)(2,1)S(1)}, bf16[256,768]{1,0:T(8,128)(2,1)S(1)}, bf16[256,768]{1,0:T(8,128)(2,1)S(1)}, bf16[256,768]{1,0:T(8,128)(2,1)S(1)}, f32[8,128]{1,0:T(8,128)S(1)}) custom-call(s32[4]{0:T(128)S(1)} %pad_add_fusion.refs_0_, bf16[512,384]{1,0:T(8,128)(2,1)S(1)} %get-tuple-element.205.refs_1_.refs_9_, ...), custom_call_target="tpu_custom_call" | custom-call | flops 1024 | bytes 1024 | tf_op jit(solution)/shard_map/token_parts/pallas_call | solution.py:369
  86.1 1.3 collective-permute-done.23.refs_13_
  87.5 3.5 %joint_units.1 = (bf16[4,2,48,768]{3,2,1,0:T(8,128)(2,1)S(1)}, bf16[4,2,48,768]{3,2,1,0:T(8,128)(2,1)S(1)}, bf16[512,768]{1,0:T(8,128)(2,1)S(1)}, bf16[4,2,32,768]{3,2,1,0:T(8,128)(2,1)S(1)}, f32[8,128]{1,0:T(8,128)S(1)}) custom-call(s32[4]{0:T(128)S(1)} %pad_add_fusion.refs_0_, bf16[128,768]{1,0:T(8,128)(2,1)S(1)} %collective-permute-done.refs_3_.refs_6_.refs_1_, ...), custom_call_target="tpu_custom_call" | custom-call | flops 1024 | bytes 1024 | tf_op jit(solution)/shard_map/joint_units/pallas_call | solution.py:369
  91.0 4.9 %collective-permute-done.24.refs_1_ = bf16[704,768]{1,0:T(8,128)(2,1)S(1)} collective-permute-done((bf16[704,768]{1,0:T(8,128)(2,1)S(1)}, bf16[704,768]{1,0:T(8,128)(2,1)S(1)}, u32[]{:S(2)}, u32[]{:S(2)}) %collective-permute-start.24) | collective-permute-done | bytes 1081376 | tf_op jit(solution)/shard_map/ppermute | solution.py:406
  96.1 1.0 second_stage.1
  97.1 1.6 collective-permute-start.28
  99.3 1.4 collective-permute-start.26
  101.2 6.3 %collective-permute-done.30.refs_6_ = bf16[2,96,768]{2,1,0:T(8,128)(2,1)S(1)} collective-permute-done((bf16[2,96,768]{2,1,0:T(8,128)(2,1)S(1)}, bf16[2,96,768]{2,1,0:T(8,128)(2,1)S(1)}, u32[]{:S(2)}, u32[]{:S(2)}) %collective-permute-start.30) | collective-permute-done | bytes 294944 | tf_op jit(solution)/shard_map/ppermute | solution.py:406
  107.6 1.7 collective-permute-done.28.refs_1_
  109.2 1.5 collective-permute-done.29.refs_2_
  110.7 0.8 up_line_stage.1
  111.9 6.8 %collective-permute-done.32.refs_4_.refs_2_ = bf16[96,768]{1,0:T(8,128)(2,1)S(1)} collective-permute-done((bf16[96,768]{1,0:T(8,128)(2,1)S(1)}, bf16[96,768]{1,0:T(8,128)(2,1)S(1)}, u32[]{:S(2)}, u32[]{:S(2)}) %collective-permute-start.32) | collective-permute-done | bytes 147488 | tf_op jit(solution)/shard_map/ppermute | solution.py:406
  118.7 2.3 %collective-permute-done.31.refs_2_ = bf16[2,128,768]{2,1,0:T(8,128)(2,1)S(1)} collective-permute-done((bf16[2,128,768]{2,1,0:T(8,128)(2,1)S(1)}, bf16[2,128,768]{2,1,0:T(8,128)(2,1)S(1)}, u32[]{:S(2)}, u32[]{:S(2)}) %collective-permute-start.31) | collective-permute-done | bytes 393248 | tf_op jit(solution)/shard_map/ppermute | solution.py:406
  121.6 3.4 %collective-permute-done.26.refs_4_.refs_3_ = bf16[512,768]{1,0:T(8,128)(2,1)S(1)} collective-permute-done((bf16[512,768]{1,0:T(8,128)(2,1)S(1)}, bf16[512,768]{1,0:T(8,128)(2,1)S(1)}, u32[]{:S(2)}, u32[]{:S(2)}) %collective-permute-start.26) | collective-permute-done | bytes 786464 | tf_op jit(solution)/shard_map/ppermute | solution.py:406
  127.6 7.0 %collective-permute-done.37.refs_4_ = bf16[128,768]{1,0:T(8,128)(2,1)S(1)} collective-permute-done((bf16[128,768]{1,0:T(8,128)(2,1)S(1)}, bf16[128,768]{1,0:T(8,128)(2,1)S(1)}, u32[]{:S(2)}, u32[]{:S(2)}) %collective-permute-start.37) | collective-permute-done | bytes 196640 | tf_op jit(solution)/shard_map/ppermute | solution.py:406
  136.4 1.6 collective-permute-start.41
  138.6 3.6 %collective-permute-done.44.refs_7_ = bf16[128,768]{1,0:T(8,128)(2,1)S(1)} collective-permute-done((bf16[128,768]{1,0:T(8,128)(2,1)S(1)}, bf16[128,768]{1,0:T(8,128)(2,1)S(1)}, u32[]{:S(2)}, u32[]{:S(2)}) %collective-permute-start.44) | collective-permute-done | bytes 196640 | tf_op jit(solution)/shard_map/ppermute | solution.py:406
  142.2 1.6 collective-permute-done.41.refs_3_
  145.2 2.0 %collective-permute-start.34 = (bf16[128,768]{1,0:T(8,128)(2,1)S(1)}, bf16[128,768]{1,0:T(8,128)(2,1)S(1)}, u32[]{:S(2)}, u32[]{:S(2)}) collective-permute-start(bf16[128,768]{1,0:T(8,128)(2,1)S(1)} %get-tuple-element.243), channel_id=1, source_target_pairs={{0,8},{1,24},{2,10},{3,26},{4,12},{5,28},{6,14},{7,30},{8,0},{9,16... | collective-permute-start | bytes 589832 | tf_op jit(solution)/shard_map/ppermute | solution.py:406
  147.2 2.3 %dense_outputs.1 = (f32[384,768]{1,0:T(8,128)}, f32[96,3072]{1,0:T(8,128)}, f32[96,768]{1,0:T(8,128)}, f32[1,96]{1,0:T(1,128)}, f32[1,96]{1,0:T(1,128)}, /*index...) custom-call(s32[4]{0:T(128)S(1)} %pad_add_fusion.refs_0_, ...), custom_call_target="tpu_custom_call" | custom-call | flops 1024 | bytes 1024 | tf_op jit(solution)/shard_map/dense_outputs/pallas_call | solution.py:369
  149.5 7.8 %collective-permute-done.39.refs_2_ = bf16[80,768]{1,0:T(8,128)(2,1)S(1)} collective-permute-done((bf16[80,768]{1,0:T(8,128)(2,1)S(1)}, bf16[80,768]{1,0:T(8,128)(2,1)S(1)}, u32[]{:S(2)}, u32[]{:S(2)}) %collective-permute-start.39) | collective-permute-done | bytes 122912 | tf_op jit(solution)/shard_map/ppermute | solution.py:406
  157.8 1.2 collective-permute-start.47
  159.1 1.6 back_rows.1
  160.7 2.5 %collective-permute-done.47.refs_3_ = bf16[80,768]{1,0:T(8,128)(2,1)S(1)} collective-permute-done((bf16[80,768]{1,0:T(8,128)(2,1)S(1)}, bf16[80,768]{1,0:T(8,128)(2,1)S(1)}, u32[]{:S(2)}, u32[]{:S(2)}) %collective-permute-start.47) | collective-permute-done | bytes 122912 | tf_op jit(solution)/shard_map/ppermute | solution.py:406
  164.5 1.5 joint_outputs.1
  (115 shorter events, 19.5 us)
Async XLA Ops:
  0.7 10.4 %collective-permute-start.2 = (s32[2,16]{1,0:T(2,128)}, s32[2,16]{1,0:T(2,128)S(1)}, u32[]{:S(2)}, u32[]{:S(2)}) collective-permute-start(s32[2,16]{1,0:T(2,128)} %refs_1_.4), channel_id=1, source_target_pairs={{0,1},{1,0},{2,3},{3,2},{4,5},{5,4},{6,7},{7,6},{8,9},{9,8},{10,11... | collective-permute-start | bytes 392 | tf_op jit(solution)/shard_map/ppermute | solution.py:406
  2.2 8.8 %collective-permute-start.1 = (bf16[128,768]{1,0:T(8,128)(2,1)S(1)}, bf16[128,768]{1,0:T(8,128)(2,1)S(1)}, u32[]{:S(2)}, u32[]{:S(2)}) collective-permute-start(bf16[128,768]{1,0:T(8,128)(2,1)S(1)} %get-tuple-element.283), channel_id=1, source_target_pairs={{0,8},{1,24},{2,10},{3,26},{4,12},{5,28},{6,14},{7,30},{8,0},{9,16... | collective-permute-start | bytes 589832 | tf_op jit(solution)/shard_map/ppermute | solution.py:406
  4.9 6.1 %collective-permute-start = (bf16[128,768]{1,0:T(8,128)(2,1)S(1)}, bf16[128,768]{1,0:T(8,128)(2,1)S(1)}, u32[]{:S(2)}, u32[]{:S(2)}) collective-permute-start(bf16[128,768]{1,0:T(8,128)(2,1)S(1)} %get-tuple-element.284), channel_id=1, source_target_pairs={{0,0},{1,16},{2,2},{3,18},{4,4},{5,20},{6,6},{7,22},{8,8},{9,24},{... | collective-permute-start | bytes 589832 | tf_op jit(solution)/shard_map/ppermute | solution.py:406
  6.7 19.5 %collective-permute-start.7 = (bf16[144,768]{1,0:T(8,128)(2,1)S(1)}, bf16[144,768]{1,0:T(8,128)(2,1)S(1)}, u32[]{:S(2)}, u32[]{:S(2)}) collective-permute-start(bf16[144,768]{1,0:T(8,128)(2,1)S(1)} %concatenate.6), channel_id=1, source_target_pairs={{0,0},{1,16},{2,2},{3,18},{4,4},{5,20},{6,6},{7,22},{8,8},{9,24},{... | collective-permute-start | bytes 663560 | tf_op jit(solution)/shard_map/ppermute | solution.py:406
  11.0 10.1 %collective-permute-start.5 = (bf16[128,768]{1,0:T(8,128)(2,1)S(1)}, bf16[128,768]{1,0:T(8,128)(2,1)S(1)}, u32[]{:S(2)}, u32[]{:S(2)}) collective-permute-start(bf16[128,768]{1,0:T(8,128)(2,1)S(1)} %collective-permute-done.refs_3_.refs_6_.refs_1_), channel_id=1, source_target_pairs={{0,1},{1,0},{2,3},{3,2},{4,5},{5,4},{6,7},{7,6},{8,9},{9,8},{10,11... | collective-permute-start | bytes 589832 | tf_op jit(solution)/shard_map/ppermute | solution.py:406
  19.0 2.1 %collective-permute-start.6 = (bf16[128,768]{1,0:T(8,128)(2,1)S(1)}, bf16[128,768]{1,0:T(8,128)(2,1)S(1)}, u32[]{:S(2)}, u32[]{:S(2)}) collective-permute-start(bf16[128,768]{1,0:T(8,128)(2,1)S(1)} %collective-permute-done.1.refs_4_.refs_7_.refs_2_), channel_id=1, source_target_pairs={{0,1},{1,0},{2,3},{3,2},{4,5},{5,4},{6,7},{7,6},{8,9},{9,8},{10,11... | collective-permute-start | bytes 589832 | tf_op jit(solution)/shard_map/ppermute | solution.py:406
  19.0 7.7 %collective-permute-start.3 = (bf16[128,768]{1,0:T(8,128)(2,1)S(1)}, bf16[128,768]{1,0:T(8,128)(2,1)S(1)}, u32[]{:S(2)}, u32[]{:S(2)}) collective-permute-start(bf16[128,768]{1,0:T(8,128)(2,1)S(1)} %collective-permute-done.refs_3_.refs_6_.refs_1_), channel_id=1, source_target_pairs={{0,4},{1,5},{2,6},{3,7},{4,0},{5,1},{6,2},{7,3},{8,12},{9,13},{10,... | collective-permute-start | bytes 589832 | tf_op jit(solution)/shard_map/ppermute | solution.py:406
  20.6 10.0 %collective-permute-start.4 = (bf16[128,768]{1,0:T(8,128)(2,1)S(1)}, bf16[128,768]{1,0:T(8,128)(2,1)S(1)}, u32[]{:S(2)}, u32[]{:S(2)}) collective-permute-start(bf16[128,768]{1,0:T(8,128)(2,1)S(1)} %collective-permute-done.1.refs_4_.refs_7_.refs_2_), channel_id=1, source_target_pairs={{0,4},{1,5},{2,6},{3,7},{4,0},{5,1},{6,2},{7,3},{8,12},{9,13},{10,... | collective-permute-start | bytes 589832 | tf_op jit(solution)/shard_map/ppermute | solution.py:406
  21.1 16.2 %collective-permute-start.10 = (bf16[144,768]{1,0:T(8,128)(2,1)S(1)}, bf16[144,768]{1,0:T(8,128)(2,1)S(1)}, u32[]{:S(2)}, u32[]{:S(2)}) collective-permute-start(bf16[144,768]{1,0:T(8,128)(2,1)S(1)} %concatenate.7), channel_id=1, source_target_pairs={{0,8},{1,24},{2,10},{3,26},{4,12},{5,28},{6,14},{7,30},{8,0},{9,16... | collective-permute-start | bytes 663560 | tf_op jit(solution)/shard_map/ppermute | solution.py:406
  30.6 1.4 collective-permute-start.8
  30.6 1.7 %collective-permute-start.9 = (bf16[128,768]{1,0:T(8,128)(2,1)S(1)}, bf16[128,768]{1,0:T(8,128)(2,1)S(1)}, u32[]{:S(2)}, u32[]{:S(2)}) collective-permute-start(bf16[128,768]{1,0:T(8,128)(2,1)S(1)} %collective-permute-done.4.refs_4_.refs_6_), channel_id=1, source_target_pairs={{0,1},{1,0},{2,3},{3,2},{4,5},{5,4},{6,7},{7,6},{8,9},{9,8},{10,11... | collective-permute-start | bytes 589832 | tf_op jit(solution)/shard_map/ppermute | solution.py:406
  37.4 1.8 %collective-permute-start.11 = (bf16[512,384]{1,0:T(8,128)(2,1)S(1)}, bf16[512,384]{1,0:T(8,128)(2,1)S(1)}, u32[]{:S(2)}, u32[]{:S(2)}) collective-permute-start(bf16[512,384]{1,0:T(8,128)(2,1)S(1)} %get-tuple-element.164.refs_1_.refs_9_), channel_id=1, source_target_pairs={{0,1},{1,0},{2,3},{3,2},{4,5},{5,4},{6,7},{7,6},{8,9},{9,8},{10,11... | collective-permute-start | bytes 1179656 | tf_op jit(solution)/shard_map/ppermute | solution.py:406
  46.4 3.0 %collective-permute-start.14 = (bf16[16,96,256]{2,1,0:T(8,128)(2,1)S(1)}, bf16[16,96,256]{2,1,0:T(8,128)(2,1)S(1)}, u32[]{:S(2)}, u32[]{:S(2)}) collective-permute-start(bf16[16,96,256]{2,1,0:T(8,128)(2,1)S(1)} %get-tuple-element.181), channel_id=1, source_target_pairs={{0,1},{1,0},{2,3},{3,2},{4,5},{5,4},{6,7},{7,6},{8,9},{9,8},{10,11... | collective-permute-start | bytes 2359304 | tf_op jit(solution)/shard_map/ppermute | solution.py:406
  46.7 2.7 %collective-permute-start.15 = (bf16[272,768]{1,0:T(8,128)(2,1)S(1)}, bf16[272,768]{1,0:T(8,128)(2,1)S(1)}, u32[]{:S(2)}, u32[]{:S(2)}) collective-permute-start(bf16[272,768]{1,0:T(8,128)(2,1)S(1)} %get-tuple-element.175.refs_3_.refs_1_), channel_id=1, source_target_pairs={{0,1},{1,0},{2,3},{3,2},{4,5},{5,4},{6,7},{7,6},{8,9},{9,8},{10,11... | collective-permute-start | bytes 1253384 | tf_op jit(solution)/shard_map/ppermute | solution.py:406
  47.0 8.3 %collective-permute-start.16 = (bf16[256,768]{1,0:T(8,128)(2,1)S(1)}, bf16[256,768]{1,0:T(8,128)(2,1)S(1)}, u32[]{:S(2)}, u32[]{:S(2)}) collective-permute-start(bf16[256,768]{1,0:T(8,128)(2,1)S(1)} %get-tuple-element.184), channel_id=1, source_target_pairs={{0,1},{1,0},{2,3},{3,2},{4,5},{5,4},{6,7},{7,6},{8,9},{9,8},{10,11... | collective-permute-start | bytes 1179656 | tf_op jit(solution)/shard_map/ppermute | solution.py:406
  52.2 16.6 %collective-permute-start.18 = (bf16[4,2,48,768]{3,2,1,0:T(8,128)(2,1)S(1)}, bf16[4,2,48,768]{3,2,1,0:T(8,128)(2,1)S(1)}, u32[]{:S(2)}, u32[]{:S(2)}) collective-permute-start(bf16[4,2,48,768]{3,2,1,0:T(8,128)(2,1)S(1)} %get-tuple-element.188), channel_id=1, source_target_pairs={{0,2},{1,3},{2,0},{3,1},{4,6},{5,7},{6,4},{7,5},{8,10},{9,11},{10,... | collective-permute-start | bytes 1769480 | tf_op jit(solution)/shard_map/ppermute | solution.py:406
  53.7 15.2 %collective-permute-start.19 = (bf16[4,2,48,768]{3,2,1,0:T(8,128)(2,1)S(1)}, bf16[4,2,48,768]{3,2,1,0:T(8,128)(2,1)S(1)}, u32[]{:S(2)}, u32[]{:S(2)}) collective-permute-start(bf16[4,2,48,768]{3,2,1,0:T(8,128)(2,1)S(1)} %get-tuple-element.190), channel_id=1, source_target_pairs={{0,4},{1,5},{2,6},{3,7},{4,0},{5,1},{6,2},{7,3},{8,12},{9,13},{10,... | collective-permute-start | bytes 1769480 | tf_op jit(solution)/shard_map/ppermute | solution.py:406
  62.4 3.0 %collective-permute-start.17 = (bf16[272,768]{1,0:T(8,128)(2,1)S(1)}, bf16[272,768]{1,0:T(8,128)(2,1)S(1)}, u32[]{:S(2)}, u32[]{:S(2)}) collective-permute-start(bf16[272,768]{1,0:T(8,128)(2,1)S(1)} %get-tuple-element.186), channel_id=1, source_target_pairs={{0,1},{1,0},{2,3},{3,2},{4,5},{5,4},{6,7},{7,6},{8,9},{9,8},{10,11... | collective-permute-start | bytes 1253384 | tf_op jit(solution)/shard_map/ppermute | solution.py:406
  62.5 2.3 %collective-permute-start.20 = (bf16[256,768]{1,0:T(8,128)(2,1)S(1)}, bf16[256,768]{1,0:T(8,128)(2,1)S(1)}, u32[]{:S(2)}, u32[]{:S(2)}) collective-permute-start(bf16[256,768]{1,0:T(8,128)(2,1)S(1)} %get-tuple-element.194), channel_id=1, source_target_pairs={{0,1},{1,0},{2,3},{3,2},{4,5},{5,4},{6,7},{7,6},{8,9},{9,8},{10,11... | collective-permute-start | bytes 1179656 | tf_op jit(solution)/shard_map/ppermute | solution.py:406
  63.0 2.4 %collective-permute-start.21 = (bf16[256,768]{1,0:T(8,128)(2,1)S(1)}, bf16[256,768]{1,0:T(8,128)(2,1)S(1)}, u32[]{:S(2)}, u32[]{:S(2)}) collective-permute-start(bf16[256,768]{1,0:T(8,128)(2,1)S(1)} %get-tuple-element.195), channel_id=1, source_target_pairs={{0,1},{1,0},{2,3},{3,2},{4,5},{5,4},{6,7},{7,6},{8,9},{9,8},{10,11... | collective-permute-start | bytes 1179656 | tf_op jit(solution)/shard_map/ppermute | solution.py:406
  70.0 25.8 %collective-permute-start.24 = (bf16[704,768]{1,0:T(8,128)(2,1)S(1)}, bf16[704,768]{1,0:T(8,128)(2,1)S(1)}, u32[]{:S(2)}, u32[]{:S(2)}) collective-permute-start(bf16[704,768]{1,0:T(8,128)(2,1)S(1)} %get-tuple-element.216), channel_id=1, source_target_pairs={{0,2},{1,3},{2,0},{3,1},{4,6},{5,7},{6,4},{7,5},{8,10},{9,11},{10,... | collective-permute-start | bytes 3244040 | tf_op jit(solution)/shard_map/ppermute | solution.py:406
  70.6 25.5 %collective-permute-start.25 = (bf16[704,768]{1,0:T(8,128)(2,1)S(1)}, bf16[704,768]{1,0:T(8,128)(2,1)S(1)}, u32[]{:S(2)}, u32[]{:S(2)}) collective-permute-start(bf16[704,768]{1,0:T(8,128)(2,1)S(1)} %get-tuple-element.217), channel_id=1, source_target_pairs={{0,4},{1,5},{2,6},{3,7},{4,0},{5,1},{6,2},{7,3},{8,12},{9,13},{10,... | collective-permute-start | bytes 3244040 | tf_op jit(solution)/shard_map/ppermute | solution.py:406
  72.1 10.1 %collective-permute-start.12 = (bf16[128,768]{1,0:T(8,128)(2,1)S(1)}, bf16[128,768]{1,0:T(8,128)(2,1)S(1)}, u32[]{:S(2)}, u32[]{:S(2)}) collective-permute-start(bf16[128,768]{1,0:T(8,128)(2,1)S(1)} %get-tuple-element.168), channel_id=1, source_target_pairs={{0,0},{1,16},{2,2},{3,18},{4,4},{5,20},{6,6},{7,22},{8,8},{9,24},{... | collective-permute-start | bytes 589832 | tf_op jit(solution)/shard_map/ppermute | solution.py:406
  72.8 9.9 %collective-permute-start.13 = (bf16[128,768]{1,0:T(8,128)(2,1)S(1)}, bf16[128,768]{1,0:T(8,128)(2,1)S(1)}, u32[]{:S(2)}, u32[]{:S(2)}) collective-permute-start(bf16[128,768]{1,0:T(8,128)(2,1)S(1)} %get-tuple-element.169), channel_id=1, source_target_pairs={{0,8},{1,24},{2,10},{3,26},{4,12},{5,28},{6,14},{7,30},{8,0},{9,16... | collective-permute-start | bytes 589832 | tf_op jit(solution)/shard_map/ppermute | solution.py:406
  85.5 2.0 %collective-permute-start.23 = (bf16[256,768]{1,0:T(8,128)(2,1)S(1)}, bf16[256,768]{1,0:T(8,128)(2,1)S(1)}, u32[]{:S(2)}, u32[]{:S(2)}) collective-permute-start(bf16[256,768]{1,0:T(8,128)(2,1)S(1)} %get-tuple-element.212), channel_id=1, source_target_pairs={{0,1},{1,0},{2,3},{3,2},{4,5},{5,4},{6,7},{7,6},{8,9},{9,8},{10,11... | collective-permute-start | bytes 1179656 | tf_op jit(solution)/shard_map/ppermute | solution.py:406
  97.1 12.1 %collective-permute-start.28 = (bf16[256,768]{1,0:T(8,128)(2,1)S(1)}, bf16[256,768]{1,0:T(8,128)(2,1)S(1)}, u32[]{:S(2)}, u32[]{:S(2)}) collective-permute-start(bf16[256,768]{1,0:T(8,128)(2,1)S(1)} %get-tuple-element.229), channel_id=1, source_target_pairs={{0,2},{1,3},{2,0},{3,1},{4,6},{5,7},{6,4},{7,5},{8,10},{9,11},{10,... | collective-permute-start | bytes 1179656 | tf_op jit(solution)/shard_map/ppermute | solution.py:406
  98.7 12.1 %collective-permute-start.29 = (bf16[256,768]{1,0:T(8,128)(2,1)S(1)}, bf16[256,768]{1,0:T(8,128)(2,1)S(1)}, u32[]{:S(2)}, u32[]{:S(2)}) collective-permute-start(bf16[256,768]{1,0:T(8,128)(2,1)S(1)} %get-tuple-element.230), channel_id=1, source_target_pairs={{0,4},{1,5},{2,6},{3,7},{4,0},{5,1},{6,2},{7,3},{8,12},{9,13},{10,... | collective-permute-start | bytes 1179656 | tf_op jit(solution)/shard_map/ppermute | solution.py:406
  99.3 25.8 %collective-permute-start.26 = (bf16[512,768]{1,0:T(8,128)(2,1)S(1)}, bf16[512,768]{1,0:T(8,128)(2,1)S(1)}, u32[]{:S(2)}, u32[]{:S(2)}) collective-permute-start(bf16[512,768]{1,0:T(8,128)(2,1)S(1)} %get-tuple-element.224), channel_id=1, source_target_pairs={{0,4},{1,5},{2,6},{3,7},{4,0},{5,1},{6,2},{7,3},{8,12},{9,13},{10,... | collective-permute-start | bytes 2359304 | tf_op jit(solution)/shard_map/ppermute | solution.py:406
  100.7 6.9 %collective-permute-start.30 = (bf16[2,96,768]{2,1,0:T(8,128)(2,1)S(1)}, bf16[2,96,768]{2,1,0:T(8,128)(2,1)S(1)}, u32[]{:S(2)}, u32[]{:S(2)}) collective-permute-start(bf16[2,96,768]{2,1,0:T(8,128)(2,1)S(1)} %get-tuple-element.234), channel_id=1, source_target_pairs={{0,8},{1,9},{2,10},{3,11},{4,12},{5,13},{6,14},{7,15},{8,0},{9,1},... | collective-permute-start | bytes 884744 | tf_op jit(solution)/shard_map/ppermute | solution.py:406
  100.7 20.9 %collective-permute-start.27 = (bf16[4,2,48,768]{3,2,1,0:T(8,128)(2,1)S(1)}, bf16[4,2,48,768]{3,2,1,0:T(8,128)(2,1)S(1)}, u32[]{:S(2)}, u32[]{:S(2)}) collective-permute-start(bf16[4,2,48,768]{3,2,1,0:T(8,128)(2,1)S(1)} %get-tuple-element.227), channel_id=1, source_target_pairs={{0,2},{1,3},{2,0},{3,1},{4,6},{5,7},{6,4},{7,5},{8,10},{9,11},{10,... | collective-permute-start | bytes 1769480 | tf_op jit(solution)/shard_map/ppermute | solution.py:406
  111.6 9.4 %collective-permute-start.31 = (bf16[2,128,768]{2,1,0:T(8,128)(2,1)S(1)}, bf16[2,128,768]{2,1,0:T(8,128)(2,1)S(1)}, u32[]{:S(2)}, u32[]{:S(2)}) collective-permute-start(bf16[2,128,768]{2,1,0:T(8,128)(2,1)S(1)} %get-tuple-element.237), channel_id=1, source_target_pairs={{0,8},{1,9},{2,10},{3,11},{4,12},{5,13},{6,14},{7,15},{8,0},{9,1},... | collective-permute-start | bytes 1179656 | tf_op jit(solution)/shard_map/ppermute | solution.py:406
  111.6 7.1 %collective-permute-start.32 = (bf16[96,768]{1,0:T(8,128)(2,1)S(1)}, bf16[96,768]{1,0:T(8,128)(2,1)S(1)}, u32[]{:S(2)}, u32[]{:S(2)}) collective-permute-start(bf16[96,768]{1,0:T(8,128)(2,1)S(1)} %get-tuple-element.239), channel_id=1, source_target_pairs={{0,16},{1,17},{2,18},{3,19},{4,20},{5,21},{6,22},{7,23},{8,24},{9,... | collective-permute-start | bytes 442376 | tf_op jit(solution)/shard_map/ppermute | solution.py:406
  111.9 15.0 %collective-permute-start.22 = (bf16[256,768]{1,0:T(8,128)(2,1)S(1)}, bf16[256,768]{1,0:T(8,128)(2,1)S(1)}, u32[]{:S(2)}, u32[]{:S(2)}) collective-permute-start(bf16[256,768]{1,0:T(8,128)(2,1)S(1)} %get-tuple-element.210), channel_id=1, source_target_pairs={{0,1},{1,0},{2,3},{3,2},{4,5},{5,4},{6,7},{7,6},{8,9},{9,8},{10,11... | collective-permute-start | bytes 1179656 | tf_op jit(solution)/shard_map/ppermute | solution.py:406
  125.9 9.8 %collective-permute-start.36 = (bf16[4,48,768]{2,1,0:T(8,128)(2,1)S(1)}, bf16[4,48,768]{2,1,0:T(8,128)(2,1)S(1)}, u32[]{:S(2)}, u32[]{:S(2)}) collective-permute-start(bf16[4,48,768]{2,1,0:T(8,128)(2,1)S(1)} %get-tuple-element.245), channel_id=1, source_target_pairs={{0,4},{1,5},{2,6},{3,7},{4,0},{5,1},{6,2},{7,3},{8,12},{9,13},{10,... | collective-permute-start | bytes 884744 | tf_op jit(solution)/shard_map/ppermute | solution.py:406
  126.2 8.3 %collective-permute-start.37 = (bf16[128,768]{1,0:T(8,128)(2,1)S(1)}, bf16[128,768]{1,0:T(8,128)(2,1)S(1)}, u32[]{:S(2)}, u32[]{:S(2)}) collective-permute-start(bf16[128,768]{1,0:T(8,128)(2,1)S(1)} %get-tuple-element.250), channel_id=1, source_target_pairs={{0,16},{1,17},{2,18},{3,19},{4,20},{5,21},{6,22},{7,23},{8,24},{9,... | collective-permute-start | bytes 589832 | tf_op jit(solution)/shard_map/ppermute | solution.py:406
  126.2 9.5 %collective-permute-start.35 = (bf16[4,32,768]{2,1,0:T(8,128)(2,1)S(1)}, bf16[4,32,768]{2,1,0:T(8,128)(2,1)S(1)}, u32[]{:S(2)}, u32[]{:S(2)}) collective-permute-start(bf16[4,32,768]{2,1,0:T(8,128)(2,1)S(1)} %get-tuple-element.244), channel_id=1, source_target_pairs={{0,2},{1,3},{2,0},{3,1},{4,6},{5,7},{6,4},{7,5},{8,10},{9,11},{10,... | collective-permute-start | bytes 589832 | tf_op jit(solution)/shard_map/ppermute | solution.py:406
  135.1 7.1 %collective-permute-start.44 = (bf16[128,768]{1,0:T(8,128)(2,1)S(1)}, bf16[128,768]{1,0:T(8,128)(2,1)S(1)}, u32[]{:S(2)}, u32[]{:S(2)}) collective-permute-start(bf16[128,768]{1,0:T(8,128)(2,1)S(1)} %get-tuple-element.259.refs_5_), channel_id=1, source_target_pairs={{0,2},{1,3},{2,0},{3,1},{4,6},{5,7},{6,4},{7,5},{8,10},{9,11},{10,... | collective-permute-start | bytes 589832 | tf_op jit(solution)/shard_map/ppermute | solution.py:406
  136.4 7.4 %collective-permute-start.38 = (bf16[2,80,768]{2,1,0:T(8,128)(2,1)S(1)}, bf16[2,80,768]{2,1,0:T(8,128)(2,1)S(1)}, u32[]{:S(2)}, u32[]{:S(2)}) collective-permute-start(bf16[2,80,768]{2,1,0:T(8,128)(2,1)S(1)} %get-tuple-element.254), channel_id=1, source_target_pairs={{0,8},{1,9},{2,10},{3,11},{4,12},{5,13},{6,14},{7,15},{8,0},{9,1},... | collective-permute-start | bytes 737288 | tf_op jit(solution)/shard_map/ppermute | solution.py:406
  136.4 7.4 %collective-permute-start.41 = (bf16[96,768]{1,0:T(8,128)(2,1)S(1)}, bf16[96,768]{1,0:T(8,128)(2,1)S(1)}, u32[]{:S(2)}, u32[]{:S(2)}) collective-permute-start(bf16[96,768]{1,0:T(8,128)(2,1)S(1)} %get-tuple-element.258.refs_1_), channel_id=1, source_target_pairs={{0,2},{1,3},{2,0},{3,1},{4,6},{5,7},{6,4},{7,5},{8,10},{9,11},{10,... | collective-permute-start | bytes 442376 | tf_op jit(solution)/shard_map/ppermute | solution.py:406
  138.1 7.1 %collective-permute-start.43 = (bf16[128,768]{1,0:T(8,128)(2,1)S(1)}, bf16[128,768]{1,0:T(8,128)(2,1)S(1)}, u32[]{:S(2)}, u32[]{:S(2)}) collective-permute-start(bf16[128,768]{1,0:T(8,128)(2,1)S(1)} %get-tuple-element.259.refs_5_), channel_id=1, source_target_pairs={{0,1},{1,0},{2,3},{3,2},{4,5},{5,4},{6,7},{7,6},{8,9},{9,8},{10,11... | collective-permute-start | bytes 589832 | tf_op jit(solution)/shard_map/ppermute | solution.py:406
  138.1 6.4 %collective-permute-start.40 = (bf16[96,768]{1,0:T(8,128)(2,1)S(1)}, bf16[96,768]{1,0:T(8,128)(2,1)S(1)}, u32[]{:S(2)}, u32[]{:S(2)}) collective-permute-start(bf16[96,768]{1,0:T(8,128)(2,1)S(1)} %get-tuple-element.258.refs_1_), channel_id=1, source_target_pairs={{0,1},{1,0},{2,3},{3,2},{4,5},{5,4},{6,7},{7,6},{8,9},{9,8},{10,11... | collective-permute-start | bytes 442376 | tf_op jit(solution)/shard_map/ppermute | solution.py:406
  142.2 5.0 %collective-permute-start.45 = (bf16[128,768]{1,0:T(8,128)(2,1)S(1)}, bf16[128,768]{1,0:T(8,128)(2,1)S(1)}, u32[]{:S(2)}, u32[]{:S(2)}) collective-permute-start(bf16[128,768]{1,0:T(8,128)(2,1)S(1)} %collective-permute-done.44.refs_7_), channel_id=1, source_target_pairs={{0,1},{1,0},{2,3},{3,2},{4,5},{5,4},{6,7},{7,6},{8,9},{9,8},{10,11... | collective-permute-start | bytes 589832 | tf_op jit(solution)/shard_map/ppermute | solution.py:406
  143.8 3.4 %collective-permute-start.42 = (bf16[96,768]{1,0:T(8,128)(2,1)S(1)}, bf16[96,768]{1,0:T(8,128)(2,1)S(1)}, u32[]{:S(2)}, u32[]{:S(2)}) collective-permute-start(bf16[96,768]{1,0:T(8,128)(2,1)S(1)} %collective-permute-done.41.refs_3_), channel_id=1, source_target_pairs={{0,1},{1,0},{2,3},{3,2},{4,5},{5,4},{6,7},{7,6},{8,9},{9,8},{10,11... | collective-permute-start | bytes 442376 | tf_op jit(solution)/shard_map/ppermute | solution.py:406
  144.4 12.8 %collective-permute-start.39 = (bf16[80,768]{1,0:T(8,128)(2,1)S(1)}, bf16[80,768]{1,0:T(8,128)(2,1)S(1)}, u32[]{:S(2)}, u32[]{:S(2)}) collective-permute-start(bf16[80,768]{1,0:T(8,128)(2,1)S(1)} %get-tuple-element.257), channel_id=1, source_target_pairs={{0,16},{1,17},{2,18},{3,19},{4,20},{5,21},{6,22},{7,23},{8,24},{9,... | collective-permute-start | bytes 368648 | tf_op jit(solution)/shard_map/ppermute | solution.py:406
  144.5 14.6 %collective-permute-start.33 = (bf16[128,768]{1,0:T(8,128)(2,1)S(1)}, bf16[128,768]{1,0:T(8,128)(2,1)S(1)}, u32[]{:S(2)}, u32[]{:S(2)}) collective-permute-start(bf16[128,768]{1,0:T(8,128)(2,1)S(1)} %get-tuple-element.242), channel_id=1, source_target_pairs={{0,0},{1,16},{2,2},{3,18},{4,4},{5,20},{6,6},{7,22},{8,8},{9,24},{... | collective-permute-start | bytes 589832 | tf_op jit(solution)/shard_map/ppermute | solution.py:406
  145.2 13.9 %collective-permute-start.34 = (bf16[128,768]{1,0:T(8,128)(2,1)S(1)}, bf16[128,768]{1,0:T(8,128)(2,1)S(1)}, u32[]{:S(2)}, u32[]{:S(2)}) collective-permute-start(bf16[128,768]{1,0:T(8,128)(2,1)S(1)} %get-tuple-element.243), channel_id=1, source_target_pairs={{0,8},{1,24},{2,10},{3,26},{4,12},{5,28},{6,14},{7,30},{8,0},{9,16... | collective-permute-start | bytes 589832 | tf_op jit(solution)/shard_map/ppermute | solution.py:406
  157.8 5.4 %collective-permute-start.47 = (bf16[80,768]{1,0:T(8,128)(2,1)S(1)}, bf16[80,768]{1,0:T(8,128)(2,1)S(1)}, u32[]{:S(2)}, u32[]{:S(2)}) collective-permute-start(bf16[80,768]{1,0:T(8,128)(2,1)S(1)} %get-tuple-element.265.refs_1_), channel_id=1, source_target_pairs={{0,2},{1,3},{2,0},{3,1},{4,6},{5,7},{6,4},{7,5},{8,10},{9,11},{10,... | collective-permute-start | bytes 368648 | tf_op jit(solution)/shard_map/ppermute | solution.py:406
  159.1 4.7 %collective-permute-start.46 = (bf16[80,768]{1,0:T(8,128)(2,1)S(1)}, bf16[80,768]{1,0:T(8,128)(2,1)S(1)}, u32[]{:S(2)}, u32[]{:S(2)}) collective-permute-start(bf16[80,768]{1,0:T(8,128)(2,1)S(1)} %get-tuple-element.265.refs_1_), channel_id=1, source_target_pairs={{0,1},{1,0},{2,3},{3,2},{4,5},{5,4},{6,7},{7,6},{8,9},{9,8},{10,11... | collective-permute-start | bytes 368648 | tf_op jit(solution)/shard_map/ppermute | solution.py:406
  (15 other events, 124.4 us)
